TPU v7x, 256 devices: a whole 4x4x8 slice. The times are simulated.
256 devices in a mesh: region: 32 (over z, y), frac: 8 (over x, core).
Axes of the slice: x: 4, y: 4, z: 8, core: 2. Of those that a mesh axis runs over, the one named last changes fastest.
Arguments:
- pres_old: float32 [32, 32, 1024], P('region', None, 'frac'), may hold values from -6 to 6
- satur_old: float32 [32, 32, 1024], P('region', None, 'frac'), may hold values from 0.1 to 0.9
- permeability: float32 [32, 32, 1024], P('region', None, 'frac'), may hold values from 0.1 to 10
- storage: float32 [2, 32, 32, 1024], P(None, 'region', None, 'frac'), may hold values from 0.5 to 2
- source: float32 [2, 32, 32, 1024], P(None, 'region', None, 'frac'), may hold values from -4 to 4
- face_upwind: int32 [3, 32, 32, 1024], P(None, 'region', None, 'frac'), may hold values 0 or 1
- frac_pres_old: float32 [262144], P(('region', 'frac')), may hold values from -6 to 6
- frac_satur_old: float32 [262144], P(('region', 'frac')), may hold values from 0.1 to 0.9
- frac_storage: float32 [2, 262144], P(None, ('region', 'frac')), may hold values from 0.5 to 2
- frac_trans: float32 [262144], P(('region', 'frac')), may hold values from 1 to 10
- frac_upwind: int32 [262144], P(('region', 'frac')), may hold values 0 or 1
- coupling: float32 [4096, 64, 128], P(('region', 'frac')), may hold values from 0.002 to 0.05
- target_part: int32 [4096], P(('region', 'frac')), may hold values from 0 to 7
- target_row: int32 [4096], P(('region', 'frac')), may hold values from 0 to 31
- live_count: int32 [256], P(('region', 'frac')), may hold values from 4 to 16, as said below
Outputs:
- cell_state: float32 [2, 32, 32, 1024], P(None, 'region', None, 'frac')
- seg_state: float32 [2, 262144], P(None, ('region', 'frac'))
Inputs may be any that keep to these rules, and one draw needn't show every extreme that they name: `live_count`: some device has all 16 slots live and some device has 4 live.
All inputs are finite; a program needn't handle non-finite values. No bound on the sum of `face_upwind` or of `frac_upwind` on one device may be relied on, other than what follows from the above.
Results may differ from a plain program's by a relative error of at most 0.0003.
Values sent between devices are 32-bit elements; how exact they have to be, the bound alone decides.
No kernel may reach another device: no remote copies, remote signals or barrier semaphores. Data moves between devices by JAX's collectives and lax.ppermute only.
A program may use at most 128 MiB of HBM per device.

v0:
```python
import jax
import jax.numpy as jnp
from jax import lax
from jax.sharding import PartitionSpec as P

NEWTON = 2
SWEEPS = 5


HIGHEST = lax.Precision.HIGHEST
VISCOSITY_RATIO = 0.5
TINY = 1e-06


def extended(block, sides, width):
    for axis, dim in sides:
        count = lax.axis_size(axis)
        forward = [(i, i + 1) for i in range(count - 1)]
        backward = [(target, source) for source, target in forward]
        low = lax.ppermute(
            lax.slice_in_dim(block, block.shape[dim] - width, None, axis=dim), axis, forward
        )
        high = lax.ppermute(lax.slice_in_dim(block, 0, width, axis=dim), axis, backward)
        block = jnp.concatenate([low, block, high], axis=dim)
    return block


def passed_along(block, axis, distance):
    devices = range(lax.axis_size(axis))
    route = [(i - distance, i) for i in devices if i - distance in devices]
    return lax.ppermute(block, axis, route)


def mobility(satur):
    water_mob = satur * satur
    total_mob = water_mob + VISCOSITY_RATIO * (1.0 - satur) * (1.0 - satur)
    return (water_mob, total_mob)


def harmonic(left_val, right_val):
    return 2.0 * left_val * right_val / (left_val + right_val)


def face_trans(perm_pad):
    trans_z = harmonic(perm_pad[:-1, 1:-1, 1:-1], perm_pad[1:, 1:-1, 1:-1])
    trans_y = harmonic(perm_pad[1:-1, :-1, 1:-1], perm_pad[1:-1, 1:, 1:-1])
    trans_x = harmonic(perm_pad[1:-1, 1:-1, :-1], perm_pad[1:-1, 1:-1, 1:])
    return (trans_z, trans_y, trans_x)


def directed(pres_left, pres_right, satur_left, satur_right, upwind, trans_face):
    satur_up = jnp.where(upwind == 1, satur_left, satur_right)
    water_mob, total_mob = mobility(satur_up)
    cond_total = trans_face * total_mob
    cond_water = trans_face * water_mob
    pres_drop = pres_left - pres_right
    return (cond_total * pres_drop, cond_water * pres_drop, cond_total, cond_water)


def net_faces(parts, member, sign):
    flux_z = parts[0][member]
    flux_y = parts[1][member]
    flux_x = parts[2][member]
    return (
        flux_z[1:]
        + sign * flux_z[:-1]
        + (flux_y[:, 1:] + sign * flux_y[:, :-1])
        + (flux_x[:, :, 1:] + sign * flux_x[:, :, :-1])
    )


def cell_flux(pres_pad, satur_pad, flag_pad, trans_faces):
    trans_z, trans_y, trans_x = trans_faces
    along_z = directed(
        pres_pad[:-1, 1:-1, 1:-1],
        pres_pad[1:, 1:-1, 1:-1],
        satur_pad[:-1, 1:-1, 1:-1],
        satur_pad[1:, 1:-1, 1:-1],
        flag_pad[0, :-1, 1:-1, 1:-1],
        trans_z,
    )
    along_y = directed(
        pres_pad[1:-1, :-1, 1:-1],
        pres_pad[1:-1, 1:, 1:-1],
        satur_pad[1:-1, :-1, 1:-1],
        satur_pad[1:-1, 1:, 1:-1],
        flag_pad[1, 1:-1, :-1, 1:-1],
        trans_y,
    )
    along_x = directed(
        pres_pad[1:-1, 1:-1, :-1],
        pres_pad[1:-1, 1:-1, 1:],
        satur_pad[1:-1, 1:-1, :-1],
        satur_pad[1:-1, 1:-1, 1:],
        flag_pad[2, 1:-1, 1:-1, :-1],
        trans_x,
    )
    parts = (along_z, along_y, along_x)
    return (
        net_faces(parts, 0, -1.0),
        net_faces(parts, 1, -1.0),
        net_faces(parts, 2, 1.0),
        net_faces(parts, 3, 1.0),
    )


def chain_net(values, sign):
    return jnp.pad(values, ((0, 0), (0, 1))) + sign * jnp.pad(values, ((0, 0), (1, 0)))


def seg_flux(seg_pres, seg_satur, seg_trans, seg_flags):
    chain = directed(
        seg_pres[:, :-1],
        seg_pres[:, 1:],
        seg_satur[:, :-1],
        seg_satur[:, 1:],
        seg_flags[:, :-1],
        seg_trans[:, :-1],
    )
    return (
        chain_net(chain[0], -1.0),
        chain_net(chain[1], -1.0),
        chain_net(chain[2], 1.0),
        chain_net(chain[3], 1.0),
    )


def couple(weight, row_pres, row_satur, seg_pres):
    water_mob, total_mob = mobility(row_satur)
    mobile = jnp.stack([total_mob, water_mob])
    vectors = jnp.concatenate([mobile * row_pres[None], mobile])
    reached = jnp.einsum("bac,gbc->gba", weight, vectors, precision=HIGHEST)
    inflow = reached[:2] - seg_pres[None] * reached[2:]
    colsum = jnp.sum(weight, axis=1)
    returned = jnp.einsum("ba,bac->bc", seg_pres, weight, precision=HIGHEST)
    outflow = mobile * (row_pres * colsum - returned)[None]
    return (inflow, outflow)


def precondition(remain, store, diag_t, diag_w):
    first = remain[0] / (store[0] + diag_t)
    second = (remain[1] - diag_w * first) / store[1]
    return jnp.stack([first, second])


def tangent_triple(func, first_point, second_point, third_point):
    values, pullback = jax.vjp(func, first_point, second_point, third_point)
    zero_cot = jax.tree.map(jnp.zeros_like, values)
    _, pushforward = jax.vjp(pullback, zero_cot)

    def forward_map(first_dir, second_dir, third_dir):
        return pushforward((first_dir, second_dir, third_dir))[0]

    return (values, forward_map)


def padded(field):
    widened = extended(field, (("region", 1), ("frac", 3)), 1)
    return jnp.pad(widened, ((0, 0), (0, 0), (1, 1), (0, 0)))


def on_device(
    pres_old,
    satur_old,
    permeability,
    storage,
    source,
    face_upwind,
    frac_pres_old,
    frac_satur_old,
    frac_storage,
    frac_trans,
    frac_upwind,
    coupling,
    target_part,
    target_row,
    live_count,
):
    depth_cells, line_count, row_width = pres_old.shape
    blocks = coupling.shape[0]
    seg_len = coupling.shape[1]
    row_count = depth_cells * line_count
    group_size = lax.axis_size("frac")
    perm_wide = extended(permeability, (("region", 0), ("frac", 2)), 1)
    trans_faces = face_trans(jnp.pad(perm_wide, ((0, 0), (1, 1), (0, 0))))
    below_layer = passed_along(face_upwind[0, -1:, :, :], "region", 1)
    before_column = passed_along(face_upwind[2, :, :, -1:], "frac", 1)
    flag_pad = jnp.pad(face_upwind, ((0, 0), (1, 1), (1, 1), (1, 1)))
    flag_pad = flag_pad.at[0, 0:1, 1:-1, 1:-1].set(below_layer)
    flag_pad = flag_pad.at[2, 1:-1, 1:-1, 0:1].set(before_column)
    slot_ids = jnp.arange(blocks, dtype=jnp.int32)
    live_int = (slot_ids < live_count[0]).astype(jnp.int32)
    live_mask = live_int.astype(jnp.float32)
    seg_trans = frac_trans.reshape(blocks, seg_len)
    seg_flags = frac_upwind.reshape(blocks, seg_len)
    seg_store = frac_storage.reshape(2, blocks, seg_len)
    live_segment = live_mask[None, :, None]
    old_cells = jnp.stack([pres_old, satur_old])
    old_segs = jnp.stack([frac_pres_old, frac_satur_old]).reshape(2, blocks, seg_len)
    weights = coupling * live_mask[:, None, None]
    picked = target_part * row_count + target_row
    spread = (
        jnp.arange(group_size * row_count, dtype=jnp.int32)[:, None] == picked[None, :]
    ).astype(jnp.float32)

    def fetch_remote(cell_now):
        gathered = lax.all_gather(
            cell_now.reshape(2, row_count, row_width), "frac", axis=1, tiled=True
        )
        return jnp.take(gathered, picked, axis=1)

    def local_all(cell_pad, remote, seg_now):
        div_t, div_w, _, _ = cell_flux(cell_pad[0], cell_pad[1], flag_pad, trans_faces)
        inflow, outflow = couple(weights, remote[0], remote[1], seg_now[0])
        partial_value = jnp.einsum("gb,fbc->fgc", spread, outflow, precision=HIGHEST)
        chain_t, chain_w, _, _ = seg_flux(seg_now[0], seg_now[1], seg_trans, seg_flags)
        return (jnp.stack([div_t, div_w]), jnp.stack([chain_t, chain_w]) - inflow, partial_value)

    def send_terms(partial_value):
        return lax.psum_scatter(partial_value, "frac", scatter_dimension=1, tiled=True)

    def settle(cell_div, seg_div, summed):
        return (cell_div + summed.reshape(2, depth_cells, line_count, row_width), seg_div)

    cell_now = old_cells
    seg_now = old_segs
    for newton in range(NEWTON):
        cell_pad = padded(cell_now)
        remote = fetch_remote(cell_now)
        (cell_div, seg_div, partial_value), linear = tangent_triple(
            local_all, cell_pad, remote, seg_now
        )
        cell_div, seg_div = settle(cell_div, seg_div, send_terms(partial_value))
        res_cells = storage * (cell_now - old_cells) + cell_div - source
        res_segs = live_segment * (seg_store * (seg_now - old_segs) + seg_div)
        _, _, diag_t, diag_w = cell_flux(cell_pad[0], cell_pad[1], flag_pad, trans_faces)
        _, _, chain_dt, chain_dw = seg_flux(seg_now[0], seg_now[1], seg_trans, seg_flags)
        remain_cell = -res_cells
        remain_seg = -res_segs
        step_cell = jnp.zeros_like(cell_now)
        step_seg = jnp.zeros_like(seg_now)
        for sweep_index in range(SWEEPS):
            dir_cell = precondition(remain_cell, storage, diag_t, diag_w)
            dir_seg = precondition(remain_seg, seg_store, chain_dt, chain_dw)
            tan_cell, tan_seg, tan_partial = linear(
                padded(dir_cell), fetch_remote(dir_cell), dir_seg
            )
            tan_cell, tan_seg = settle(tan_cell, tan_seg, send_terms(tan_partial))
            image_cell = storage * dir_cell + tan_cell
            image_seg = live_segment * (seg_store * dir_seg + tan_seg)
            cross_local = jnp.sum(remain_cell * image_cell) + jnp.sum(remain_seg * image_seg)
            square_local = jnp.sum(image_cell * image_cell) + jnp.sum(image_seg * image_seg)
            cross_sum, square = lax.psum((cross_local, square_local), ("region", "frac"))
            step_size = cross_sum / (square + TINY)
            step_cell = step_cell + step_size * dir_cell
            step_seg = step_seg + step_size * dir_seg
            remain_cell = remain_cell - step_size * image_cell
            remain_seg = remain_seg - step_size * image_seg
        cell_now = cell_now + step_cell
        seg_now = seg_now + step_seg
    return (cell_now, seg_now.reshape(2, blocks * seg_len))


def solution(mesh):
    placed = (
        P("region", None, "frac"),
        P("region", None, "frac"),
        P("region", None, "frac"),
        P(None, "region", None, "frac"),
        P(None, "region", None, "frac"),
        P(None, "region", None, "frac"),
        P(("region", "frac")),
        P(("region", "frac")),
        P(None, ("region", "frac")),
        P(("region", "frac")),
        P(("region", "frac")),
        P(("region", "frac"), None, None),
        P(("region", "frac")),
        P(("region", "frac")),
        P(("region", "frac")),
    )
    return jax.shard_map(
        on_device,
        mesh=mesh,
        in_specs=placed,
        out_specs=(P(None, "region", None, "frac"), P(None, ("region", "frac"))),
        check_vma=False,
    )
```

profile of v0, /device:TPU:1, one launch (start us, length us, event | category | flops | bytes accessed | tf_op | source)
XLA Modules:
  0.0 1961.1 jit_solution(12104216525536535509)
XLA Ops:
  7.2 4.2 collective-permute-start
  14.7 4.6 collective-permute-start.4
  19.5 4.5 collective-permute-start.3
  28.0 11.9 all-gather
  69.7 39.4 %all-reduce.105.cloned.1.call-done = f32[2,256,128]{2,0,1:T(2,128)} async-done(((f32[2,256,128]{2,0,1:T(2,128)}), f32[2,256,128]{2,0,1:T(2,128)}) %all-reduce.105.cloned.1.call-update) | async-done | bytes 262160
  111.3 4.0 collective-permute-start.10
  115.3 16.0 all-gather.1
  144.0 62.8 %all-reduce.107.cloned.1.call-done = f32[2,256,128]{2,0,1:T(2,128)} async-done(((f32[2,256,128]{2,0,1:T(2,128)}), f32[2,256,128]{2,0,1:T(2,128)}) %all-reduce.107.cloned.1.call-update) | async-done | bytes 262160
  210.8 78.4 %all-reduce.91 = (f32[]{:T(128)}, f32[]{:T(128)}) all-reduce(f32[]{:T(128)S(6)} %add.927, f32[]{:T(128)S(6)} %add.928), channel_id=1, replica_groups=mesh['region'=32,'frac'=8] {'region','frac'}, use_global_device_ids=true, to_apply=%region_5.7 | all-reduce | flops 2 | bytes 16 | tf_op jit(solution)/shard_map/psum | solution.py:253
  291.9 4.0 collective-permute-start.14
  296.7 14.2 all-gather.2
  321.7 59.1 %all-reduce.109.cloned.1.call-done = f32[2,256,128]{2,0,1:T(2,128)} async-done(((f32[2,256,128]{2,0,1:T(2,128)}), f32[2,256,128]{2,0,1:T(2,128)}) %all-reduce.109.cloned.1.call-update) | async-done | bytes 262160
  384.8 78.4 %all-reduce.90 = (f32[]{:T(128)}, f32[]{:T(128)}) all-reduce(f32[]{:T(128)S(6)} %add.934, f32[]{:T(128)S(6)} %add.935), channel_id=1, replica_groups=mesh['region'=32,'frac'=8] {'region','frac'}, use_global_device_ids=true, to_apply=%region_12.14 | all-reduce | flops 2 | bytes 16 | tf_op jit(solution)/shard_map/psum | solution.py:253
  465.9 4.0 collective-permute-start.18
  470.8 14.2 all-gather.3
  495.7 59.1 %all-reduce.111.cloned.1.call-done = f32[2,256,128]{2,0,1:T(2,128)} async-done(((f32[2,256,128]{2,0,1:T(2,128)}), f32[2,256,128]{2,0,1:T(2,128)}) %all-reduce.111.cloned.1.call-update) | async-done | bytes 262160
  558.8 78.4 %all-reduce.89 = (f32[]{:T(128)}, f32[]{:T(128)}) all-reduce(f32[]{:T(128)S(6)} %add.942, f32[]{:T(128)S(6)} %add.943), channel_id=1, replica_groups=mesh['region'=32,'frac'=8] {'region','frac'}, use_global_device_ids=true, to_apply=%region_19.21 | all-reduce | flops 2 | bytes 16 | tf_op jit(solution)/shard_map/psum | solution.py:253
  639.9 4.0 collective-permute-start.22
  644.7 14.2 all-gather.4
  669.7 59.1 %all-reduce.113.cloned.1.call-done = f32[2,256,128]{2,0,1:T(2,128)} async-done(((f32[2,256,128]{2,0,1:T(2,128)}), f32[2,256,128]{2,0,1:T(2,128)}) %all-reduce.113.cloned.1.call-update) | async-done | bytes 262160
  732.8 78.4 %all-reduce.88 = (f32[]{:T(128)}, f32[]{:T(128)}) all-reduce(f32[]{:T(128)S(6)} %add.950, f32[]{:T(128)S(6)} %add.951), channel_id=1, replica_groups=mesh['region'=32,'frac'=8] {'region','frac'}, use_global_device_ids=true, to_apply=%region_26.28 | all-reduce | flops 2 | bytes 16 | tf_op jit(solution)/shard_map/psum | solution.py:253
  813.9 4.0 collective-permute-start.26
  818.7 14.2 all-gather.5
  843.7 59.1 %all-reduce.115.cloned.1.call-done = f32[2,256,128]{2,0,1:T(2,128)} async-done(((f32[2,256,128]{2,0,1:T(2,128)}), f32[2,256,128]{2,0,1:T(2,128)}) %all-reduce.115.cloned.1.call-update) | async-done | bytes 262160
  906.8 78.4 %all-reduce.87 = (f32[]{:T(128)}, f32[]{:T(128)}) all-reduce(f32[]{:T(128)S(6)} %add.958, f32[]{:T(128)S(6)} %add.959), channel_id=1, replica_groups=mesh['region'=32,'frac'=8] {'region','frac'}, use_global_device_ids=true, to_apply=%region_33.35 | all-reduce | flops 2 | bytes 16 | tf_op jit(solution)/shard_map/psum | solution.py:253
  987.9 4.0 collective-permute-start.30
  992.7 14.2 all_gather.42
  1016.9 58.1 %all-reduce.117.cloned.1.call-done = f32[2,256,128]{2,0,1:T(2,128)} async-done(((f32[2,256,128]{2,0,1:T(2,128)}), f32[2,256,128]{2,0,1:T(2,128)}) %all-reduce.117.cloned.1.call-update) | async-done | bytes 262160
  1077.3 4.0 collective-permute-start.34
  1081.3 16.0 all-gather.6
  1110.0 62.8 %all-reduce.119.cloned.1.call-done = f32[2,256,128]{2,0,1:T(2,128)} async-done(((f32[2,256,128]{2,0,1:T(2,128)}), f32[2,256,128]{2,0,1:T(2,128)}) %all-reduce.119.cloned.1.call-update) | async-done | bytes 262160
  1176.9 78.4 %all-reduce.86 = (f32[]{:T(128)}, f32[]{:T(128)}) all-reduce(f32[]{:T(128)S(6)} %add.1012, f32[]{:T(128)S(6)} %add.1013), channel_id=1, replica_groups=mesh['region'=32,'frac'=8] {'region','frac'}, use_global_device_ids=true, to_apply=%region_41.43 | all-reduce | flops 2 | bytes 16 | tf_op jit(solution)/shard_map/psum | solution.py:253
  1257.9 4.0 collective-permute-start.38
  1262.8 14.2 all-gather.7
  1287.8 59.1 %all-reduce.121.cloned.1.call-done = f32[2,256,128]{2,0,1:T(2,128)} async-done(((f32[2,256,128]{2,0,1:T(2,128)}), f32[2,256,128]{2,0,1:T(2,128)}) %all-reduce.121.cloned.1.call-update) | async-done | bytes 262160
  1350.9 78.5 %all-reduce.85 = (f32[]{:T(128)}, f32[]{:T(128)}) all-reduce(f32[]{:T(128)S(6)} %add.1019, f32[]{:T(128)S(6)} %add.1020), channel_id=1, replica_groups=mesh['region'=32,'frac'=8] {'region','frac'}, use_global_device_ids=true, to_apply=%region_48.50 | all-reduce | flops 2 | bytes 16 | tf_op jit(solution)/shard_map/psum | solution.py:253
  1432.1 4.0 collective-permute-start.42
  1437.0 14.2 all-gather.8
  1462.0 59.1 %all-reduce.123.cloned.1.call-done = f32[2,256,128]{2,0,1:T(2,128)} async-done(((f32[2,256,128]{2,0,1:T(2,128)}), f32[2,256,128]{2,0,1:T(2,128)}) %all-reduce.123.cloned.1.call-update) | async-done | bytes 262160
  1525.0 78.4 %all-reduce.84 = (f32[]{:T(128)}, f32[]{:T(128)}) all-reduce(f32[]{:T(128)S(6)} %add.1027, f32[]{:T(128)S(6)} %add.1028), channel_id=1, replica_groups=mesh['region'=32,'frac'=8] {'region','frac'}, use_global_device_ids=true, to_apply=%region_55.57 | all-reduce | flops 2 | bytes 16 | tf_op jit(solution)/shard_map/psum | solution.py:253
  1606.1 4.0 collective-permute-start.46
  1611.0 14.2 all-gather.9
  1635.9 59.1 %all-reduce.125.cloned.1.call-done = f32[2,256,128]{2,0,1:T(2,128)} async-done(((f32[2,256,128]{2,0,1:T(2,128)}), f32[2,256,128]{2,0,1:T(2,128)}) %all-reduce.125.cloned.1.call-update) | async-done | bytes 262160
  1699.0 78.4 %all-reduce.83 = (f32[]{:T(128)}, f32[]{:T(128)}) all-reduce(f32[]{:T(128)S(6)} %add.1035, f32[]{:T(128)S(6)} %add.1036), channel_id=1, replica_groups=mesh['region'=32,'frac'=8] {'region','frac'}, use_global_device_ids=true, to_apply=%region_62.64 | all-reduce | flops 2 | bytes 16 | tf_op jit(solution)/shard_map/psum | solution.py:253
  1780.1 4.0 collective-permute-start.50
  1784.9 14.2 all-gather.10
  1809.9 59.1 %all-reduce.127.cloned.1.call-done = f32[2,256,128]{2,0,1:T(2,128)} async-done(((f32[2,256,128]{2,0,1:T(2,128)}), f32[2,256,128]{2,0,1:T(2,128)}) %all-reduce.127.cloned.1.call-update) | async-done | bytes 262160
  1873.1 78.4 %all-reduce.82 = (f32[]{:T(128)}, f32[]{:T(128)}) all-reduce(f32[]{:T(128)S(6)} %add.1043, f32[]{:T(128)S(6)} %add.1044), channel_id=1, replica_groups=mesh['region'=32,'frac'=8] {'region','frac'}, use_global_device_ids=true, to_apply=%region_69.71 | all-reduce | flops 2 | bytes 16 | tf_op jit(solution)/shard_map/psum | solution.py:253
  (584 shorter events, 196.2 us)
Async XLA Ops:
  7.2 101.9 %all-reduce.105.cloned.1.call-start = ((), (), s32[]{:S(2)}) async-start(), calls=%async_computation | async-start | bytes 524288
  7.2 44.0 %collective-permute-start = (f32[1,32,128]{2,1,0:T(8,128)}, f32[1,32,128]{2,1,0:T(8,128)S(1)}, u32[]{:S(2)}, u32[]{:S(2)}) collective-permute-start(f32[1,32,128]{2,1,0:T(8,128)} %param.23), channel_id=1, source_target_pairs={{0,8},{8,16},{16,24},{24,32},{32,40},{40,48},{48,56},{56,64},{64,7... | collective-permute-start | bytes 49160 | tf_op jit(solution)/shard_map/ppermute | solution.py:20
  11.4 40.5 %collective-permute-start.1 = (f32[1,32,128]{2,1,0:T(8,128)}, f32[1,32,128]{2,1,0:T(8,128)S(1)}, u32[]{:S(2)}, u32[]{:S(2)}) collective-permute-start(f32[1,32,128]{2,1,0:T(8,128)} %param.23), channel_id=1, source_target_pairs={{8,0},{16,8},{24,16},{32,24},{40,32},{48,40},{56,48},{64,56},{72,6... | collective-permute-start | bytes 49160 | tf_op jit(solution)/shard_map/ppermute | solution.py:23
  13.4 45.2 %collective-permute-start.5 = (f32[2,1,32,128]{3,2,1,0:T(8,128)S(1)}, f32[2,1,32,128]{3,2,1,0:T(8,128)S(1)}, u32[]{:S(2)}, u32[]{:S(2)}) collective-permute-start(f32[2,1,32,128]{3,2,1,0:T(8,128)S(1)} %pad_maximum_fusion.14), channel_id=1, source_target_pairs={{8,0},{16,8},{24,16},{32,24},{40,32},{48,40},{56,48},{64,56},{72,6... | collective-permute-start | bytes 98312 | tf_op jit(solution)/shard_map/ppermute | solution.py:23
  14.7 43.9 %collective-permute-start.4 = (f32[2,1,32,128]{3,2,1,0:T(8,128)S(1)}, f32[2,1,32,128]{3,2,1,0:T(8,128)S(1)}, u32[]{:S(2)}, u32[]{:S(2)}) collective-permute-start(f32[2,1,32,128]{3,2,1,0:T(8,128)S(1)} %pad_maximum_fusion.14), channel_id=1, source_target_pairs={{0,8},{8,16},{16,24},{24,32},{32,40},{40,48},{48,56},{56,64},{64,7... | collective-permute-start | bytes 98312 | tf_op jit(solution)/shard_map/ppermute | solution.py:20
  19.5 27.9 %collective-permute-start.3 = (s32[1,32,1]{1,2,0:T(1,128)S(1)}, s32[1,32,1]{1,2,0:T(1,128)S(1)}, u32[]{:S(2)}, u32[]{:S(2)}) collective-permute-start(s32[1,32,1]{1,2,0:T(1,128)S(1)} %bitcast.958), channel_id=1, source_target_pairs={{0,1},{1,2},{2,3},{3,4},{4,5},{5,6},{6,7},{8,9},{9,10},{10,11},{11... | collective-permute-start | bytes 392 | tf_op jit(solution)/shard_map/ppermute | solution.py:31
  41.9 164.9 %all-reduce.107.cloned.1.call-start = ((), (), s32[]{:S(2)}) async-start(), calls=%async_computation.1 | async-start | bytes 524288
  47.5 9.6 collective-permute-start.2
  52.0 12.6 collective-permute-start.8
  55.2 9.5 collective-permute-start.9
  110.0 25.4 %collective-permute-start.11 = (f32[2,1,32,128]{3,2,1,0:T(8,128)S(1)}, f32[2,1,32,128]{3,2,1,0:T(8,128)S(1)}, u32[]{:S(2)}, u32[]{:S(2)}) collective-permute-start(f32[2,1,32,128]{3,2,1,0:T(8,128)S(1)} %pad_maximum_fusion.15), channel_id=1, source_target_pairs={{8,0},{16,8},{24,16},{32,24},{40,32},{48,40},{56,48},{64,56},{72,6... | collective-permute-start | bytes 98312 | tf_op jit(solution)/shard_map/ppermute | solution.py:23
  111.3 24.1 %collective-permute-start.10 = (f32[2,1,32,128]{3,2,1,0:T(8,128)S(1)}, f32[2,1,32,128]{3,2,1,0:T(8,128)S(1)}, u32[]{:S(2)}, u32[]{:S(2)}) collective-permute-start(f32[2,1,32,128]{3,2,1,0:T(8,128)S(1)} %pad_maximum_fusion.15), channel_id=1, source_target_pairs={{0,8},{8,16},{16,24},{24,32},{32,40},{40,48},{48,56},{56,64},{64,7... | collective-permute-start | bytes 98312 | tf_op jit(solution)/shard_map/ppermute | solution.py:20
  135.5 6.1 collective-permute-start.12
  141.6 239.3 %all-reduce.109.cloned.1.call-start = ((), (), s32[]{:S(2)}) async-start(), calls=%async_computation.2 | async-start | bytes 524288
  290.6 22.5 %collective-permute-start.15 = (f32[2,1,32,128]{3,2,1,0:T(8,128)S(1)}, f32[2,1,32,128]{3,2,1,0:T(8,128)S(1)}, u32[]{:S(2)}, u32[]{:S(2)}) collective-permute-start(f32[2,1,32,128]{3,2,1,0:T(8,128)S(1)} %pad_maximum_fusion.17), channel_id=1, source_target_pairs={{8,0},{16,8},{24,16},{32,24},{40,32},{48,40},{56,48},{64,56},{72,6... | collective-permute-start | bytes 98312 | tf_op jit(solution)/shard_map/ppermute | solution.py:23
  291.9 21.2 %collective-permute-start.14 = (f32[2,1,32,128]{3,2,1,0:T(8,128)S(1)}, f32[2,1,32,128]{3,2,1,0:T(8,128)S(1)}, u32[]{:S(2)}, u32[]{:S(2)}) collective-permute-start(f32[2,1,32,128]{3,2,1,0:T(8,128)S(1)} %pad_maximum_fusion.17), channel_id=1, source_target_pairs={{0,8},{8,16},{16,24},{24,32},{32,40},{40,48},{48,56},{56,64},{64,7... | collective-permute-start | bytes 98312 | tf_op jit(solution)/shard_map/ppermute | solution.py:20
  313.2 6.3 collective-permute-start.16
  319.2 235.6 %all-reduce.111.cloned.1.call-start = ((), (), s32[]{:S(2)}) async-start(), calls=%async_computation.3 | async-start | bytes 524288
  464.6 22.5 %collective-permute-start.19 = (f32[2,1,32,128]{3,2,1,0:T(8,128)S(1)}, f32[2,1,32,128]{3,2,1,0:T(8,128)S(1)}, u32[]{:S(2)}, u32[]{:S(2)}) collective-permute-start(f32[2,1,32,128]{3,2,1,0:T(8,128)S(1)} %pad_maximum_fusion.18), channel_id=1, source_target_pairs={{8,0},{16,8},{24,16},{32,24},{40,32},{48,40},{56,48},{64,56},{72,6... | collective-permute-start | bytes 98312 | tf_op jit(solution)/shard_map/ppermute | solution.py:23
  465.9 21.2 %collective-permute-start.18 = (f32[2,1,32,128]{3,2,1,0:T(8,128)S(1)}, f32[2,1,32,128]{3,2,1,0:T(8,128)S(1)}, u32[]{:S(2)}, u32[]{:S(2)}) collective-permute-start(f32[2,1,32,128]{3,2,1,0:T(8,128)S(1)} %pad_maximum_fusion.18), channel_id=1, source_target_pairs={{0,8},{8,16},{16,24},{24,32},{32,40},{40,48},{48,56},{56,64},{64,7... | collective-permute-start | bytes 98312 | tf_op jit(solution)/shard_map/ppermute | solution.py:20
  487.2 6.1 collective-permute-start.20
  493.3 235.6 %all-reduce.113.cloned.1.call-start = ((), (), s32[]{:S(2)}) async-start(), calls=%async_computation.4 | async-start | bytes 524288
  638.6 22.5 %collective-permute-start.23 = (f32[2,1,32,128]{3,2,1,0:T(8,128)S(1)}, f32[2,1,32,128]{3,2,1,0:T(8,128)S(1)}, u32[]{:S(2)}, u32[]{:S(2)}) collective-permute-start(f32[2,1,32,128]{3,2,1,0:T(8,128)S(1)} %pad_maximum_fusion.19), channel_id=1, source_target_pairs={{8,0},{16,8},{24,16},{32,24},{40,32},{48,40},{56,48},{64,56},{72,6... | collective-permute-start | bytes 98312 | tf_op jit(solution)/shard_map/ppermute | solution.py:23
  639.9 21.2 %collective-permute-start.22 = (f32[2,1,32,128]{3,2,1,0:T(8,128)S(1)}, f32[2,1,32,128]{3,2,1,0:T(8,128)S(1)}, u32[]{:S(2)}, u32[]{:S(2)}) collective-permute-start(f32[2,1,32,128]{3,2,1,0:T(8,128)S(1)} %pad_maximum_fusion.19), channel_id=1, source_target_pairs={{0,8},{8,16},{16,24},{24,32},{32,40},{40,48},{48,56},{56,64},{64,7... | collective-permute-start | bytes 98312 | tf_op jit(solution)/shard_map/ppermute | solution.py:20
  667.3 235.6 %all-reduce.115.cloned.1.call-start = ((), (), s32[]{:S(2)}) async-start(), calls=%async_computation.5 | async-start | bytes 524288
  812.6 22.5 %collective-permute-start.27 = (f32[2,1,32,128]{3,2,1,0:T(8,128)S(1)}, f32[2,1,32,128]{3,2,1,0:T(8,128)S(1)}, u32[]{:S(2)}, u32[]{:S(2)}) collective-permute-start(f32[2,1,32,128]{3,2,1,0:T(8,128)S(1)} %pad_maximum_fusion.20), channel_id=1, source_target_pairs={{8,0},{16,8},{24,16},{32,24},{40,32},{48,40},{56,48},{64,56},{72,6... | collective-permute-start | bytes 98312 | tf_op jit(solution)/shard_map/ppermute | solution.py:23
  813.9 21.2 %collective-permute-start.26 = (f32[2,1,32,128]{3,2,1,0:T(8,128)S(1)}, f32[2,1,32,128]{3,2,1,0:T(8,128)S(1)}, u32[]{:S(2)}, u32[]{:S(2)}) collective-permute-start(f32[2,1,32,128]{3,2,1,0:T(8,128)S(1)} %pad_maximum_fusion.20), channel_id=1, source_target_pairs={{0,8},{8,16},{16,24},{24,32},{32,40},{40,48},{48,56},{56,64},{64,7... | collective-permute-start | bytes 98312 | tf_op jit(solution)/shard_map/ppermute | solution.py:20
  835.2 6.5 collective-permute-start.28
  841.3 233.8 %all-reduce.117.cloned.1.call-start = ((), (), s32[]{:S(2)}) async-start(), calls=%async_computation.6 | async-start | bytes 524288
  986.6 21.4 %collective-permute-start.31 = (f32[2,1,32,128]{3,2,1,0:T(8,128)S(1)}, f32[2,1,32,128]{3,2,1,0:T(8,128)S(1)}, u32[]{:S(2)}, u32[]{:S(2)}) collective-permute-start(f32[2,1,32,128]{3,2,1,0:T(8,128)S(1)} %add_add_fusion.1), channel_id=1, source_target_pairs={{8,0},{16,8},{24,16},{32,24},{40,32},{48,40},{56,48},{64,56},{72,6... | collective-permute-start | bytes 98312 | tf_op jit(solution)/shard_map/ppermute | solution.py:23
  987.9 20.1 %collective-permute-start.30 = (f32[2,1,32,128]{3,2,1,0:T(8,128)S(1)}, f32[2,1,32,128]{3,2,1,0:T(8,128)S(1)}, u32[]{:S(2)}, u32[]{:S(2)}) collective-permute-start(f32[2,1,32,128]{3,2,1,0:T(8,128)S(1)} %add_add_fusion.1), channel_id=1, source_target_pairs={{0,8},{8,16},{16,24},{24,32},{32,40},{40,48},{48,56},{56,64},{64,7... | collective-permute-start | bytes 98312 | tf_op jit(solution)/shard_map/ppermute | solution.py:20
  1013.4 159.5 %all-reduce.119.cloned.1.call-start = ((), (), s32[]{:S(2)}) async-start(), calls=%async_computation.7 | async-start | bytes 524288
  1076.0 25.4 %collective-permute-start.35 = (f32[2,1,32,128]{3,2,1,0:T(8,128)S(1)}, f32[2,1,32,128]{3,2,1,0:T(8,128)S(1)}, u32[]{:S(2)}, u32[]{:S(2)}) collective-permute-start(f32[2,1,32,128]{3,2,1,0:T(8,128)S(1)} %pad_maximum_fusion.21), channel_id=1, source_target_pairs={{8,0},{16,8},{24,16},{32,24},{40,32},{48,40},{56,48},{64,56},{72,6... | collective-permute-start | bytes 98312 | tf_op jit(solution)/shard_map/ppermute | solution.py:23
  1077.3 24.1 %collective-permute-start.34 = (f32[2,1,32,128]{3,2,1,0:T(8,128)S(1)}, f32[2,1,32,128]{3,2,1,0:T(8,128)S(1)}, u32[]{:S(2)}, u32[]{:S(2)}) collective-permute-start(f32[2,1,32,128]{3,2,1,0:T(8,128)S(1)} %pad_maximum_fusion.21), channel_id=1, source_target_pairs={{0,8},{8,16},{16,24},{24,32},{32,40},{40,48},{48,56},{56,64},{64,7... | collective-permute-start | bytes 98312 | tf_op jit(solution)/shard_map/ppermute | solution.py:20
  1101.5 6.1 collective-permute-start.36
  1107.6 239.3 %all-reduce.121.cloned.1.call-start = ((), (), s32[]{:S(2)}) async-start(), calls=%async_computation.8 | async-start | bytes 524288
  1256.6 22.5 %collective-permute-start.39 = (f32[2,1,32,128]{3,2,1,0:T(8,128)S(1)}, f32[2,1,32,128]{3,2,1,0:T(8,128)S(1)}, u32[]{:S(2)}, u32[]{:S(2)}) collective-permute-start(f32[2,1,32,128]{3,2,1,0:T(8,128)S(1)} %pad_maximum_fusion.23), channel_id=1, source_target_pairs={{8,0},{16,8},{24,16},{32,24},{40,32},{48,40},{56,48},{64,56},{72,6... | collective-permute-start | bytes 98312 | tf_op jit(solution)/shard_map/ppermute | solution.py:23
  1257.9 21.2 %collective-permute-start.38 = (f32[2,1,32,128]{3,2,1,0:T(8,128)S(1)}, f32[2,1,32,128]{3,2,1,0:T(8,128)S(1)}, u32[]{:S(2)}, u32[]{:S(2)}) collective-permute-start(f32[2,1,32,128]{3,2,1,0:T(8,128)S(1)} %pad_maximum_fusion.23), channel_id=1, source_target_pairs={{0,8},{8,16},{16,24},{24,32},{32,40},{40,48},{48,56},{56,64},{64,7... | collective-permute-start | bytes 98312 | tf_op jit(solution)/shard_map/ppermute | solution.py:20
  1285.3 235.7 %all-reduce.123.cloned.1.call-start = ((), (), s32[]{:S(2)}) async-start(), calls=%async_computation.9 | async-start | bytes 524288
  1430.8 22.5 %collective-permute-start.43 = (f32[2,1,32,128]{3,2,1,0:T(8,128)S(1)}, f32[2,1,32,128]{3,2,1,0:T(8,128)S(1)}, u32[]{:S(2)}, u32[]{:S(2)}) collective-permute-start(f32[2,1,32,128]{3,2,1,0:T(8,128)S(1)} %pad_maximum_fusion.24), channel_id=1, source_target_pairs={{8,0},{16,8},{24,16},{32,24},{40,32},{48,40},{56,48},{64,56},{72,6... | collective-permute-start | bytes 98312 | tf_op jit(solution)/shard_map/ppermute | solution.py:23
  1432.1 21.2 %collective-permute-start.42 = (f32[2,1,32,128]{3,2,1,0:T(8,128)S(1)}, f32[2,1,32,128]{3,2,1,0:T(8,128)S(1)}, u32[]{:S(2)}, u32[]{:S(2)}) collective-permute-start(f32[2,1,32,128]{3,2,1,0:T(8,128)S(1)} %pad_maximum_fusion.24), channel_id=1, source_target_pairs={{0,8},{8,16},{16,24},{24,32},{32,40},{40,48},{48,56},{56,64},{64,7... | collective-permute-start | bytes 98312 | tf_op jit(solution)/shard_map/ppermute | solution.py:20
  1459.5 235.5 %all-reduce.125.cloned.1.call-start = ((), (), s32[]{:S(2)}) async-start(), calls=%async_computation.10 | async-start | bytes 524288
  1604.8 22.5 %collective-permute-start.47 = (f32[2,1,32,128]{3,2,1,0:T(8,128)S(1)}, f32[2,1,32,128]{3,2,1,0:T(8,128)S(1)}, u32[]{:S(2)}, u32[]{:S(2)}) collective-permute-start(f32[2,1,32,128]{3,2,1,0:T(8,128)S(1)} %pad_maximum_fusion.25), channel_id=1, source_target_pairs={{8,0},{16,8},{24,16},{32,24},{40,32},{48,40},{56,48},{64,56},{72,6... | collective-permute-start | bytes 98312 | tf_op jit(solution)/shard_map/ppermute | solution.py:23
  1606.1 21.2 %collective-permute-start.46 = (f32[2,1,32,128]{3,2,1,0:T(8,128)S(1)}, f32[2,1,32,128]{3,2,1,0:T(8,128)S(1)}, u32[]{:S(2)}, u32[]{:S(2)}) collective-permute-start(f32[2,1,32,128]{3,2,1,0:T(8,128)S(1)} %pad_maximum_fusion.25), channel_id=1, source_target_pairs={{0,8},{8,16},{16,24},{24,32},{32,40},{40,48},{48,56},{56,64},{64,7... | collective-permute-start | bytes 98312 | tf_op jit(solution)/shard_map/ppermute | solution.py:20
  1627.4 6.1 collective-permute-start.48
  1633.5 235.6 %all-reduce.127.cloned.1.call-start = ((), (), s32[]{:S(2)}) async-start(), calls=%async_computation.11 | async-start | bytes 524288
  1778.8 22.5 %collective-permute-start.51 = (f32[2,1,32,128]{3,2,1,0:T(8,128)S(1)}, f32[2,1,32,128]{3,2,1,0:T(8,128)S(1)}, u32[]{:S(2)}, u32[]{:S(2)}) collective-permute-start(f32[2,1,32,128]{3,2,1,0:T(8,128)S(1)} %pad_maximum_fusion.26), channel_id=1, source_target_pairs={{8,0},{16,8},{24,16},{32,24},{40,32},{48,40},{56,48},{64,56},{72,6... | collective-permute-start | bytes 98312 | tf_op jit(solution)/shard_map/ppermute | solution.py:23
  1780.1 21.2 %collective-permute-start.50 = (f32[2,1,32,128]{3,2,1,0:T(8,128)S(1)}, f32[2,1,32,128]{3,2,1,0:T(8,128)S(1)}, u32[]{:S(2)}, u32[]{:S(2)}) collective-permute-start(f32[2,1,32,128]{3,2,1,0:T(8,128)S(1)} %pad_maximum_fusion.26), channel_id=1, source_target_pairs={{0,8},{8,16},{16,24},{24,32},{32,40},{40,48},{48,56},{56,64},{64,7... | collective-permute-start | bytes 98312 | tf_op jit(solution)/shard_map/ppermute | solution.py:20
  (31 other events, 226.0 us)
Sparse Core Ops, SparseCore 0:
  42.0 67.0 all-reduce.104
  141.7 65.0 all-reduce.106
  319.4 61.4 all-reduce.108
  493.4 61.3 all-reduce.110
  667.4 61.4 all-reduce.112
  841.4 61.4 all-reduce.114
  1013.5 61.4 all-reduce.116
  1107.7 65.1 all-reduce.118
  1285.4 61.4 all-reduce.120
  1459.6 61.3 all-reduce.122
  1633.6 61.3 all-reduce.124
  1807.6 61.4 all-reduce.126
where the time goes:
time: 1970 us; the launch traced here: 1960 us
  blocking collectives  955 us (48%)
  waiting for transfers between devices  720 us (37%)
  starting transfers between devices  137 us (7%)
  between operations  56.3 us (3%)
  local copies, waits for them, and re-layouts  37.8 us (2%)
  other arithmetic  31.8 us (2%)
  matrix products  23.2 us (1%)
    psum x10, blocking collectives, on_device(): lax.psum((cross_local, square_local), ('region', 'frac'))  784 us
    unnamed x24, waiting for transfers between devices  696 us
    all_gather x12, blocking collectives, fetch_remote(): lax.all_gather(cell_now.reshape(2, row_count, row_width), 'frac', axis=1,...  172 us
    ppermute x26, starting transfers between devices, extended(): lax.ppermute(lax.slice_in_dim(block, block.shape[dim] - width, None, axis...  80.6 us
    ppermute x26, starting transfers between devices, extended(): lax.ppermute(lax.slice_in_dim(block, 0, width, axis=dim), axis, backward)  47.1 us
  transfers between devices with their start and end apart: 66, of which 24 were waited for; matrix products, arithmetic and copies ran while one was open for 4% of the time, Pallas kernels for 0%

commit v1 on v0

v1 whole, which is shorter than its diff:
```python
import jax
import jax.numpy as jnp
from jax import lax
from jax.experimental import pallas as pl
from jax.experimental.pallas import tpu as pltpu
from jax.sharding import PartitionSpec as P

NEWTON = 2
SWEEPS = 5
VISCOSITY_RATIO = 0.5
TINY = 1e-06
SCALE = 1.0 / 16.0
UNROLL = 4
PAIRS = [(i, j) for i in range(SWEEPS + 1) for j in range(i, SWEEPS + 1)]
DOTS = 24
F32 = jnp.float32
VMEM_LIMIT = 24 * 2**20


def vmem(*shape):
    return pltpu.VMEM(shape, F32)


def smem_i32(*shape):
    return jax.ShapeDtypeStruct(shape, jnp.int32)


def call(body, outs, args, spaces, scratch=(), out_spaces=None, flops=20000, name=None):
    ins = []
    for arg, space in zip(args, spaces):
        if space == "v":
            arg = pltpu.with_memory_space_constraint(arg, pltpu.VMEM)
        ins.append(arg)
    kinds = {"v": pltpu.VMEM, "s": pltpu.SMEM, "a": pl.ANY}
    out_spaces = out_spaces or "v" * len(outs)
    return pl.pallas_call(
        body,
        out_shape=list(outs),
        in_specs=[pl.BlockSpec(memory_space=kinds[s]) for s in spaces],
        out_specs=[pl.BlockSpec(memory_space=kinds[s]) for s in out_spaces],
        scratch_shapes=list(scratch),
        compiler_params=pltpu.CompilerParams(vmem_limit_bytes=VMEM_LIMIT),
        cost_estimate=pl.CostEstimate(flops=flops, bytes_accessed=flops, transcendentals=0),
        name=name,
    )(*ins)


def mobility(satur):
    water_mob = satur * satur
    total_mob = water_mob + VISCOSITY_RATIO * (1.0 - satur) * (1.0 - satur)
    return water_mob, total_mob


def slopes(satur):
    return 2.0 * satur, 2.0 * satur - 2.0 * VISCOSITY_RATIO * (1.0 - satur)


def neighbours(own, below, above, left, right):
    lane = lax.broadcasted_iota(jnp.int32, own.shape, 1)
    x_next = jnp.where(lane == 127, pltpu.roll(right, 127, 1), pltpu.roll(own, 127, 1))
    x_prev = jnp.where(lane == 0, pltpu.roll(left, 1, 1), pltpu.roll(own, 1, 1))
    return (above, below, pltpu.roll(own, 31, 0), pltpu.roll(own, 1, 0), x_next, x_prev)


def chain_neighbours(own):
    return (pltpu.roll(own, 63, 0), pltpu.roll(own, 1, 0))


def harmonic(left_val, right_val):
    return 2.0 * left_val * right_val / (left_val + right_val)


def geometry(ids, own, below, above, left, right, flag_y, faces_ref, own_up_ref):
    region, frac, regions, fracs = ids[0], ids[1], ids[2], ids[3]
    block = [r[...] for r in (own, below, above, left, right)]
    perm = neighbours(*[b[64:96] for b in block])
    row = lax.broadcasted_iota(jnp.int32, (32, 128), 0)
    lane = lax.broadcasted_iota(jnp.int32, (32, 128), 1)
    everywhere = row >= 0
    inside = (
        everywhere & (region < regions - 1),
        everywhere & (region > 0),
        row < 31,
        row > 0,
        (lane < 127) | (frac < fracs - 1),
        (lane > 0) | (frac > 0),
    )
    here = block[0][64:96]
    for f in range(6):
        faces_ref[32 * f : 32 * f + 32] = jnp.where(inside[f], harmonic(here, perm[f]), 0.0)
    flag_z = block[0][96:128]
    flag_x = block[0][128:160]
    y_here = flag_y[...].astype(F32)
    z_prev = block[1][96:128]
    y_prev = pltpu.roll(y_here, 1, 0)
    x_prev = neighbours(flag_x, flag_x, flag_x, block[3][128:160], flag_x)[5]
    for f, (flag, forward) in enumerate(
        ((flag_z, 1), (z_prev, 0), (y_here, 1), (y_prev, 0), (flag_x, 1), (x_prev, 0))
    ):
        upstream = jnp.where(flag == 1.0, 1.0, 0.0)
        own_up_ref[32 * f : 32 * f + 32] = upstream if forward else 1.0 - upstream


def collect(
    ids, codes, *refs
):
    pieces = refs[:8]
    record = refs[8]
    weights, slots, rows, count, seg_old, seg_face, seg_up, seg_store, seg_live, sems = refs[9:]
    me = ids[1]
    blocks = 128

    def source(owner, slot, act):
        other = lax.rem(owner + me, 2)
        base = jnp.where(other == 1, me + 1 - 2 * lax.rem(me, 2), me)
        turn = lax.rem(base - owner + 8, 8) // 2
        which = other * 4 + turn
        for k in range(8):

            @pl.when(which == k)
            def _():
                act(pieces[k].at[slot])

    def visit(b, n):
        mine = (codes[b] >= 0) & (codes[b] // 32 == me)

        @pl.when(mine)
        def _():
            slots[n] = b
            rows[n] = lax.rem(codes[b], 32)
            source(
                b // 16,
                lax.rem(b, 16),
                lambda src: pltpu.make_async_copy(src, weights.at[n], sems.at[n]).start(),
            )

        return n + mine.astype(jnp.int32)

    n = lax.fori_loop(0, blocks, visit, jnp.int32(0))
    rounds = (n + UNROLL - 1) // UNROLL
    count[0] = rounds

    def fill(i, carry):
        slots[i] = -1
        rows[i] = 0
        pltpu.make_async_copy(pieces[0].at[0], weights.at[i], sems.at[i]).start()
        return carry

    lax.fori_loop(n, rounds * UNROLL, fill, 0)

    turned = [record[:, 128 * k : 128 * k + 128].T for k in range(4)]
    seg_old[...] = turned[0]
    trans, flags = turned[1][:64], turned[1][64:]
    at = lax.broadcasted_iota(jnp.int32, (64, 128), 0)
    seg_face[:64] = jnp.where(at < 63, trans, 0.0)
    seg_face[64:] = jnp.where(at > 0, pltpu.roll(trans, 1, 0), 0.0)
    upstream = jnp.where(flags == 1.0, 1.0, 0.0)
    seg_up[:64] = upstream
    seg_up[64:] = 1.0 - pltpu.roll(upstream, 1, 0)
    seg_store[...] = turned[2]
    code = turned[3][:8]
    first = (me * 32).astype(F32)
    seg_live[...] = jnp.where((code >= first) & (code < first + 32.0), 1.0, 0.0)

    def settle(i, carry):
        pltpu.make_async_copy(pieces[0].at[0], weights.at[i], sems.at[i]).wait()
        return carry

    lax.fori_loop(0, rounds * UNROLL, settle, 0)


def over_blocks(slots, rows, count, weights, lines, q, sums, returned, columns):
    lane = lax.broadcasted_iota(jnp.int32, (64, 128), 1)
    sums[...] = jnp.zeros_like(sums)
    returned[...] = jnp.zeros_like(returned)
    if columns is not None:
        columns[...] = jnp.zeros_like(columns)

    def body(step, carry):
        added = [jnp.zeros((64, 128), F32) for _ in range(4)]
        q_all = q[:64]
        backs = []
        for k in range(UNROLL):
            i = step * UNROLL + k
            slot, row = slots[i], rows[i]
            weight = weights[i]
            here = lane == slot
            for v in range(4):
                line = lines[pl.ds(32 * v + row, 1), :]
                total = jnp.sum(weight * line, axis=1, keepdims=True)
                added[v] = added[v] + jnp.where(here, total, 0.0)
            q_col = jnp.sum(jnp.where(here, q_all, 0.0), axis=1, keepdims=True)
            back = jnp.sum(weight * q_col, axis=0, keepdims=True)
            col = None
            if columns is not None:
                valid = jnp.where(slot >= 0, 1.0, 0.0)
                col = jnp.sum(weight, axis=0, keepdims=True) * valid
            backs.append((row, back, col))
        for v in range(4):
            sums[64 * v : 64 * v + 64] += added[v]
        for row, back, col in backs:
            returned[pl.ds(row, 1), :] += back
            if columns is not None:
                columns[pl.ds(row, 1), :] += col
        return carry

    lax.fori_loop(0, count[0], body, 0)


def combine(dots):
    total = jnp.sum(dots, axis=1, keepdims=True)
    total = jnp.broadcast_to(total, (DOTS, 128))
    gram = {}
    for n, (i, j) in enumerate(PAIRS):
        gram[i, j] = gram[j, i] = jnp.broadcast_to(total[n : n + 1, :], (8, 128))
    one = jnp.ones((8, 128), F32)
    remain = [one]
    factors = [jnp.zeros((8, 128), F32) for _ in range(SWEEPS)]
    for sweep in range(SWEEPS):
        image = [(j + 1, value / SCALE) for j, value in enumerate(remain)]
        cross = sum(value * factor * gram[j, i] for j, value in enumerate(remain) for i, factor in image)
        square = sum(a * b * gram[i, j] for i, a in image for j, b in image)
        alpha = cross / (square + TINY)
        for j, value in enumerate(remain):
            factors[j] = factors[j] + alpha * value
        longer = remain + [jnp.zeros((8, 128), F32)]
        for i, factor in image:
            longer[i] = longer[i] - alpha * factor
        remain = longer
    return factors


def spread(factor, rows):
    return jnp.broadcast_to(factor[:1], (rows, 128))


def summed(parts_ref):
    total = parts_ref[0]
    for k in range(1, parts_ref.shape[0]):
        total = total + parts_ref[k]
    return total


def face_terms(pres, satur, pres_across, satur_across, faces, own_up, coef_ref, stride):
    div_t = div_w = diag_t = diag_w = None
    count = len(pres_across)
    rows = pres.shape[0]
    for f in range(count):
        trans = faces[rows * f : rows * f + rows]
        up = own_up[rows * f : rows * f + rows]
        s_up = jnp.where(up == 1.0, satur, satur_across[f])
        drop = pres - pres_across[f]
        water, total = mobility(s_up)
        water_slope, total_slope = slopes(s_up)
        cond_t, cond_w = trans * total, trans * water
        lean = trans * drop
        at = rows * f
        coef_ref[at : at + rows] = cond_t
        coef_ref[stride + at : stride + at + rows] = cond_w
        coef_ref[2 * stride + at : 2 * stride + at + rows] = total_slope * lean
        coef_ref[3 * stride + at : 3 * stride + at + rows] = water_slope * lean
        flux_t, flux_w = cond_t * drop, cond_w * drop
        if f == 0:
            div_t, div_w, diag_t, diag_w = flux_t, flux_w, cond_t, cond_w
        else:
            div_t, div_w = div_t + flux_t, div_w + flux_w
            diag_t, diag_w = diag_t + cond_t, diag_w + cond_w
    return div_t, div_w, diag_t, diag_w


def face_tangents(dp, ds, dp_across, ds_across, own_up, coef, stride):
    rows = dp.shape[0]
    out_t = out_w = None
    for f in range(len(dp_across)):
        at = rows * f
        up = own_up[at : at + rows]
        drop = dp - dp_across[f]
        ds_up = jnp.where(up == 1.0, ds, ds_across[f])
        part_t = coef[at : at + rows] * drop + coef[2 * stride + at : 2 * stride + at + rows] * ds_up
        part_w = (
            coef[stride + at : stride + at + rows] * drop
            + coef[3 * stride + at : 3 * stride + at + rows] * ds_up
        )
        out_t = part_t if f == 0 else out_t + part_t
        out_w = part_w if f == 0 else out_w + part_w
    return out_t, out_w


def linearise(newton, *refs):
    refs = list(refs)

    def take(n):
        out = refs[:n]
        del refs[:n]
        return out

    slots, rows, count = take(3)
    cell_old, store, source, faces, own_up = take(5)
    seg_old, seg_store, seg_face, seg_up, seg_live, weights = take(6)
    [cell_in] = take(1)
    around = take(4)
    [seg_in] = take(1)
    if newton:
        [parts] = take(1)
        dir_cells = take(SWEEPS)
        dir_segs = take(SWEEPS)
        dir_around = [take(4) for _ in range(SWEEPS)]
    base_cell, base_seg, dir_cell, dir_seg = take(4)
    coef, seg_coef, lead, seg_lead, lines, reach, couple_rows = take(7)
    if newton:
        cell_out, seg_out = take(2)
    inner_lines, sums, returned, columns = refs

    cell = cell_in[...]
    near = [r[...] for r in around]
    if newton:
        factors = combine(summed(parts))
        for j in range(SWEEPS):
            g = spread(factors[j], 64)
            cell = cell + g * dir_cells[j][...]
            near = [n + g * d[...] for n, d in zip(near, dir_around[j])]
        cell_out[...] = cell
        seg = seg_in[...]
        for j in range(SWEEPS):
            seg = seg + spread(factors[j], 128) * dir_segs[j][...]
        seg_out[...] = seg
        seg_ref = seg_out
    else:
        seg = seg_in[...]
        seg_ref = seg_in
    pres, satur = cell[:32], cell[32:]
    q, r = seg[:64], seg[64:]

    water, total = mobility(satur)
    water_slope, total_slope = slopes(satur)
    lines[0:32] = total
    lines[32:64] = water
    lines[64:96] = total_slope
    lines[96:128] = water_slope
    lines[128:160] = pres
    inner_lines[0:32] = total
    inner_lines[32:64] = water
    inner_lines[64:96] = total * pres
    inner_lines[96:128] = water * pres
    over_blocks(slots, rows, count, weights, inner_lines, seg_ref, sums, returned, columns)
    reach[...] = sums[0:128]
    column = columns[...]
    pull = pres * column - returned[...]
    couple_rows[0:32] = column
    couple_rows[32:64] = pull

    pres_across = neighbours(pres, *[n[:32] for n in near])
    satur_across = neighbours(satur, *[n[32:] for n in near])
    div_t, div_w, diag_t, diag_w = face_terms(
        pres, satur, pres_across, satur_across, faces, own_up, coef, 192
    )
    st, sw = store[:32], store[32:]
    moved = cell - cell_old[...]
    base_t = source[:32] - st * moved[:32] - div_t - total * pull
    base_w = source[32:] - sw * moved[32:] - div_w - water * pull
    lead_t = 1.0 / (st + diag_t)
    lead_w = 1.0 / sw
    lead[0:32] = lead_t
    lead[32:64] = diag_w
    lead[64:96] = lead_w
    base_cell[0:32] = base_t
    base_cell[32:64] = base_w
    first = base_t * lead_t
    dir_cell[0:32] = first
    dir_cell[32:64] = (base_w - diag_w * first) * lead_w

    chain_t, chain_w, chain_dt, chain_dw = face_terms(
        q, r, chain_neighbours(q), chain_neighbours(r), seg_face, seg_up, seg_coef, 128
    )
    live = jnp.broadcast_to(seg_live[:1], (64, 128))
    sst, ssw = seg_store[:64], seg_store[64:]
    shifted = seg - seg_old[...]
    inflow_t = sums[128:192] - q * sums[0:64]
    inflow_w = sums[192:256] - q * sums[64:128]
    seg_t = -live * (sst * shifted[:64] + chain_t - inflow_t)
    seg_w = -live * (ssw * shifted[64:] + chain_w - inflow_w)
    lead_t = 1.0 / (sst + chain_dt)
    lead_w = 1.0 / ssw
    seg_lead[0:64] = lead_t
    seg_lead[64:128] = chain_dw
    seg_lead[128:192] = lead_w
    base_seg[0:64] = seg_t
    base_seg[64:128] = seg_w
    first = seg_t * lead_t
    dir_seg[0:64] = first
    dir_seg[64:128] = (seg_w - chain_dw * first) * lead_w


def couple_dirs(
    slots, rows, count, dir_cell, dir_seg, seg, lines, reach, weights, inflow, returned, inner_lines, sums
):
    dp, ds = dir_cell[:32], dir_cell[32:]
    pres = lines[128:160]
    lean_t = lines[64:96] * ds
    lean_w = lines[96:128] * ds
    inner_lines[0:32] = lines[0:32] * dp + lean_t * pres
    inner_lines[32:64] = lines[32:64] * dp + lean_w * pres
    inner_lines[64:96] = lean_t
    inner_lines[96:128] = lean_w
    over_blocks(slots, rows, count, weights, inner_lines, dir_seg, sums, returned, None)
    q, dq = seg[:64], dir_seg[:64]
    inflow[0:64] = sums[0:64] - q * sums[128:192] - dq * reach[0:64]
    inflow[64:128] = sums[64:128] - q * sums[192:256] - dq * reach[64:128]


def advance(last, *refs):
    (
        dir_cell,
        below,
        above,
        left,
        right,
        dir_seg,
        inflow,
        returned,
        store,
        own_up,
        seg_store,
        seg_up,
        seg_live,
        coef,
        seg_coef,
        lead,
        seg_lead,
        lines,
        couple_rows,
    ) = refs[:19]
    next_cell, next_seg = refs[19:21]
    dp, ds = dir_cell[:32], dir_cell[32:]
    near = [n[...] for n in (below, above, left, right)]
    out_t, out_w = face_tangents(
        dp,
        ds,
        neighbours(dp, *[n[:32] for n in near]),
        neighbours(ds, *[n[32:] for n in near]),
        own_up,
        coef,
        192,
    )
    flow = dp * couple_rows[0:32] - returned[...]
    pull = ds * couple_rows[32:64]
    image_t = store[:32] * dp + out_t + lines[0:32] * flow + lines[64:96] * pull
    image_w = store[32:] * ds + out_w + lines[32:64] * flow + lines[96:128] * pull
    cell_t, cell_w = SCALE * image_t, SCALE * image_w
    next_cell[0:32] = cell_t
    next_cell[32:64] = cell_w

    dq, dr = dir_seg[:64], dir_seg[64:]
    chain_t, chain_w = face_tangents(
        dq, dr, chain_neighbours(dq), chain_neighbours(dr), seg_up, seg_coef, 128
    )
    live = jnp.broadcast_to(SCALE * seg_live[:1], (64, 128))
    seg_t = live * (seg_store[:64] * dq + chain_t - inflow[:64])
    seg_w = live * (seg_store[64:] * dr + chain_w - inflow[64:])
    next_seg[0:64] = seg_t
    next_seg[64:128] = seg_w
    if not last:
        next_dir, next_dir_seg = refs[21:23]
        first = cell_t * lead[0:32]
        next_dir[0:32] = first
        next_dir[32:64] = (cell_w - lead[32:64] * first) * lead[64:96]
        first = seg_t * seg_lead[0:64]
        next_dir_seg[0:64] = first
        next_dir_seg[64:128] = (seg_w - seg_lead[64:128] * first) * seg_lead[128:192]


def inner_products(*refs):
    cells, segs, out = refs[: SWEEPS + 1], refs[SWEEPS + 1 : 2 * SWEEPS + 2], refs[-1]
    lines = []
    for i, j in PAIRS:
        part = jnp.sum(cells[i][...] * cells[j][...], axis=0, keepdims=True)
        lines.append(part + jnp.sum(segs[i][...] * segs[j][...], axis=0, keepdims=True))
    lines.append(jnp.zeros((DOTS - len(PAIRS), 128), F32))
    total = jnp.concatenate(lines, axis=0)
    for k in range(out.shape[0]):
        out[k] = total


def add_parts(parts, out):
    total = summed(parts)
    for k in range(out.shape[0]):
        out[k] = total


def finish(*refs):
    parts, cell, seg, seg_old = refs[:4]
    dir_cells = refs[4 : 4 + SWEEPS]
    dir_segs = refs[4 + SWEEPS : 4 + 2 * SWEEPS]
    cell_out, moved = refs[4 + 2 * SWEEPS :]
    factors = combine(summed(parts))
    total = cell[...]
    shift = seg[...] - seg_old[...]
    for j in range(SWEEPS):
        total = total + spread(factors[j], 64) * dir_cells[j][...]
        shift = shift + spread(factors[j], 128) * dir_segs[j][...]
    cell_out[...] = total
    moved[...] = shift.T


def ring(block, axis, distance):
    count = lax.axis_size(axis)
    return lax.ppermute(block, axis, [(i, (i + distance) % count) for i in range(count)])


def swapped(block, axis):
    return lax.ppermute(block, axis, [(i, i ^ 1) for i in range(lax.axis_size(axis))])


def exchanged(block):
    return [
        ring(block, "region", 1),
        ring(block, "region", -1),
        ring(block, "frac", 1),
        ring(block, "frac", -1),
    ]


def reduced(parts):
    y_groups = [[4 * z + y for y in range(4)] for z in range(8)]
    z_groups = [[4 * z + y for z in range(8)] for y in range(4)]
    parts = lax.all_to_all(parts, "frac", 0, 0)
    [parts] = call(add_parts, [vmem(4, DOTS, 128)], [parts], "v")
    parts = lax.all_to_all(parts, "region", 0, 0, axis_index_groups=y_groups)
    [parts] = call(add_parts, [vmem(8, DOTS, 128)], [parts], "v")
    return lax.all_to_all(parts, "region", 0, 0, axis_index_groups=z_groups)


def on_device(
    pres_old,
    satur_old,
    permeability,
    storage,
    source,
    face_upwind,
    frac_pres_old,
    frac_satur_old,
    frac_storage,
    frac_trans,
    frac_upwind,
    coupling,
    target_part,
    target_row,
    live_count,
):
    blocks = coupling.shape[0]
    ids = jnp.stack(
        [
            lax.axis_index("region"),
            lax.axis_index("frac"),
            jnp.int32(lax.axis_size("region")),
            jnp.int32(lax.axis_size("frac")),
        ]
    ).astype(jnp.int32)
    cell_old = jnp.concatenate([pres_old[0], satur_old[0]], axis=0)
    message = jnp.concatenate(
        [
            cell_old,
            permeability[0],
            face_upwind[0, 0].astype(F32),
            face_upwind[2, 0].astype(F32),
        ],
        axis=0,
    )
    live = jnp.arange(blocks, dtype=jnp.int32) < live_count[0]
    code = jnp.where(live, target_part * 32 + target_row, -1)
    record = jnp.concatenate(
        [
            x.reshape(blocks, 64)
            for x in (
                frac_pres_old,
                frac_satur_old,
                frac_trans,
                frac_upwind.astype(F32),
                frac_storage[0],
                frac_storage[1],
            )
        ]
        + [jnp.broadcast_to(code.astype(F32)[:, None], (blocks, 128))],
        axis=1,
    )
    around = exchanged(message)
    same = [coupling] + [ring(coupling, "frac", 2 * k) for k in (1, 2, 3)]
    pieces = same + [swapped(x, "frac") for x in same]
    record_all = lax.all_gather(record, "frac", axis=0, tiled=True)
    codes = record_all[:, 384].astype(jnp.int32)

    faces, own_up = call(
        geometry,
        [vmem(192, 128), vmem(192, 128)],
        [ids, message, *around, face_upwind[1, 0]],
        "svvvvvv",
    )
    room = 8 * blocks + UNROLL
    weights, slots, rows, count, seg_old, seg_face, seg_up, seg_store, seg_live = call(
        collect,
        [
            vmem(room, 64, 128),
            smem_i32(room),
            smem_i32(room),
            smem_i32(1),
            vmem(128, 128),
            vmem(128, 128),
            vmem(128, 128),
            vmem(128, 128),
            vmem(8, 128),
        ],
        [ids, codes, *pieces, record_all],
        "ss" + "a" * 8 + "v",
        scratch=[pltpu.SemaphoreType.DMA((room,))],
        out_spaces="vsss" + "v" * 5,
    )
    lists = [slots, rows, count]
    store = storage.reshape(64, 128)
    wells = source.reshape(64, 128)
    inner = [vmem(128, 128), vmem(256, 128)]

    cell, seg = cell_old, seg_old
    near = [x[:64] for x in around]
    parts = None
    for newton in range(NEWTON):
        args = [
            *lists,
            cell_old,
            store,
            wells,
            faces,
            own_up,
            seg_old,
            seg_store,
            seg_face,
            seg_up,
            seg_live,
            weights,
            cell,
            *near,
            seg,
        ]
        outs = [
            vmem(64, 128),
            vmem(128, 128),
            vmem(64, 128),
            vmem(128, 128),
            vmem(768, 128),
            vmem(512, 128),
            vmem(96, 128),
            vmem(192, 128),
            vmem(160, 128),
            vmem(128, 128),
            vmem(64, 128),
        ]
        if newton:
            args += [parts, *dir_cells, *dir_segs, *[x for group in dir_around for x in group]]
            outs += [vmem(64, 128), vmem(128, 128)]
        made = call(
            lambda *refs, newton=newton: linearise(newton, *refs),
            outs,
            args,
            "sss" + "v" * (len(args) - 3),
            scratch=[*inner, vmem(32, 128), vmem(32, 128)],
            name="linearise",
        )
        base_cell, base_seg, dir_cell, dir_seg = made[:4]
        coef, seg_coef, lead, seg_lead, lines, reach, couple_rows = made[4:11]
        if newton:
            cell, seg = made[11:]
        base_cells, base_segs = [base_cell], [base_seg]
        dir_cells, dir_segs, dir_around = [], [], []
        for sweep in range(SWEEPS):
            last = sweep == SWEEPS - 1
            nearby = exchanged(dir_cell)
            inflow, returned = call(
                couple_dirs,
                [vmem(128, 128), vmem(32, 128)],
                [*lists, dir_cell, dir_seg, seg, lines, reach, weights],
                "sss" + "v" * 6,
                scratch=inner,
                name="couple",
            )
            dir_cells.append(dir_cell)
            dir_segs.append(dir_seg)
            dir_around.append(nearby)
            args = [
                dir_cell,
                *nearby,
                dir_seg,
                inflow,
                returned,
                store,
                own_up,
                seg_store,
                seg_up,
                seg_live,
                coef,
                seg_coef,
                lead,
                seg_lead,
                lines,
                couple_rows,
            ]
            made = call(
                lambda *refs, last=last: advance(last, *refs),
                [vmem(64, 128), vmem(128, 128)] * (1 if last else 2),
                args,
                "v" * len(args),
                name="advance",
            )
            base_cells.append(made[0])
            base_segs.append(made[1])
            if not last:
                dir_cell, dir_seg = made[2:]
        [parts] = call(
            inner_products,
            [vmem(8, DOTS, 128)],
            [*base_cells, *base_segs],
            "v" * (2 * SWEEPS + 2),
            name="inner_products",
        )
        parts = reduced(parts)

    args = [parts, cell, seg, seg_old, *dir_cells, *dir_segs]
    cell_state, moved = call(
        finish,
        [jax.ShapeDtypeStruct((64, 128), F32), vmem(128, 128)],
        args,
        "v" * len(args),
        name="finish",
    )
    moved = lax.all_to_all(moved.reshape(8, blocks, 128), "frac", 0, 0)
    moved = jnp.sum(moved, axis=0)
    seg_state = jnp.stack(
        [
            frac_pres_old + moved[:, :64].reshape(-1),
            frac_satur_old + moved[:, 64:].reshape(-1),
        ]
    )
    return (cell_state.reshape(2, 1, 32, 128), seg_state)


def solution(mesh):
    placed = (
        P("region", None, "frac"),
        P("region", None, "frac"),
        P("region", None, "frac"),
        P(None, "region", None, "frac"),
        P(None, "region", None, "frac"),
        P(None, "region", None, "frac"),
        P(("region", "frac")),
        P(("region", "frac")),
        P(None, ("region", "frac")),
        P(("region", "frac")),
        P(("region", "frac")),
        P(("region", "frac"), None, None),
        P(("region", "frac")),
        P(("region", "frac")),
        P(("region", "frac")),
    )
    return jax.shard_map(
        on_device,
        mesh=mesh,
        in_specs=placed,
        out_specs=(P(None, "region", None, "frac"), P(None, ("region", "frac"))),
        check_vma=False,
    )
```

time: 1970 us -> 248 us (0.13)
  blocking collectives: 955 us -> 82.5 us
  waiting for transfers between devices: 720 us -> 15.7 us
  between operations: 56.3 us -> 2 us
  starting transfers between devices: 137 us -> 98.3 us
  Pallas kernels: 0 us -> 37.5 us
  local copies, waits for them, and re-layouts: 37.8 us -> 7.58 us
  other arithmetic: 31.8 us -> 4.36 us
  matrix products: 23.2 us -> 0 us
    psum x10 -> x0, blocking collectives: 784 us -> none  [on_device(): lax.psum((cross_local, square_local), ('region', 'frac'))]
    unnamed x24 -> x0, waiting for transfers between devices: 696 us -> none
    all_gather x12 -> x1, blocking collectives: 172 us -> 13.2 us  [on_device(): record_all = lax.all_gather(record, 'frac', axis=0, tiled=True)]
    all_to_all x0 -> x7, blocking collectives: none -> 69.4 us  [the longest x2 22.9 us: reduced(): return lax.all_to_all(parts, 'region', 0, 0, axis_index_groups=z_groups)]
    pallas_call x0 -> x31, Pallas kernels: none -> 37.5 us  [call(): pl.pallas_call(body, out_shape=list(outs), in_specs=[pl.BlockSpec(memory_...]
    ppermute x54 -> x51, starting transfers between devices: 136 us -> 98.3 us  [the longest x47 95 us: ring(): lax.ppermute(block, axis, [(i, (i + distance) % count) for i in range(cou...]
    dot_general x36 -> x0, matrix products: 23.2 us -> none  [the longest x12 12.1 us: couple(): reached = jnp.einsum('bac,gbc->gba', weight, vectors, precision=HIGHEST)]
  transfers between devices with their start and end apart: 66 -> 51, of which waited for: 24 -> 7; matrix products, arithmetic and copies ran while one was open for 4% -> 4% of each run, Pallas kernels for 0% -> 9%
where the time goes in v1:
time: 248 us
  starting transfers between devices  98.3 us (40%)
  blocking collectives  82.5 us (33%)
  Pallas kernels  37.5 us (15%)
  waiting for transfers between devices  15.7 us (6%)
  local copies, waits for them, and re-layouts  7.58 us (3%)
  other arithmetic  4.36 us (2%)
    ppermute x47, starting transfers between devices, ring(): lax.ppermute(block, axis, [(i, (i + distance) % count) for i in range(cou...  95 us
    pallas_call x31, Pallas kernels, call(): pl.pallas_call(body, out_shape=list(outs), in_specs=[pl.BlockSpec(memory_...  37.5 us
    all_to_all x2, blocking collectives, reduced(): return lax.all_to_all(parts, 'region', 0, 0, axis_index_groups=z_groups)  22.9 us
    all_to_all x2, blocking collectives, reduced(): parts = lax.all_to_all(parts, 'frac', 0, 0)  22.5 us
    ppermute x47, waiting for transfers between devices, ring(): lax.ppermute(block, axis, [(i, (i + distance) % count) for i in range(cou...  15.7 us
    all_to_all x2, blocking collectives, reduced(): parts = lax.all_to_all(parts, 'region', 0, 0, axis_index_groups=y_groups)  13.5 us
    all_gather x1, blocking collectives, on_device(): record_all = lax.all_gather(record, 'frac', axis=0, tiled=True)  13.2 us
    all_to_all x1, blocking collectives, on_device(): moved = lax.all_to_all(moved.reshape(8, blocks, 128), 'frac', 0, 0)  10.5 us
  transfers between devices with their start and end apart: 51, of which 7 were waited for; matrix products, arithmetic and copies ran while one was open for 4% of the time, Pallas kernels for 9%

profile of v1, /device:TPU:1, one launch (start us, length us, event | category | flops | bytes accessed | tf_op | source)
XLA Modules:
  0.0 248.0 jit_solution(4524067503514547853)
XLA Ops:
  0.6 2.1 collective-permute-start
  2.8 2.5 collective-permute-start.1
  6.4 1.5 collective-permute-start.3
  18.1 9.8 %collective-permute-done.1.refs_2_ = f32[16,64,128]{2,1,0:T(8,128)S(1)} collective-permute-done((f32[16,64,128]{2,1,0:T(8,128)}, f32[16,64,128]{2,1,0:T(8,128)S(1)}, u32[]{:S(2)}, u32[]{:S(2)}) %collective-permute-start.1) | collective-permute-done | bytes 524320 | tf_op jit(solution)/shard_map/ppermute | solution.py:507
  28.0 1.5 collective-permute-start.5
  30.6 13.2 %all_gather.3.refs_8_ = f32[128,512]{1,0:T(8,128)S(1)} all-gather(f32[16,512]{1,0:T(8,128)S(1)} %concatenate.10), channel_id=1, replica_groups=mesh['region'=32,'frac'=8] {'frac'}, dimensions={0}, use_global_device_ids=true | all-gather | bytes 294912 | tf_op jit(solution)/shard_map/all_gather | solution.py:589
  43.8 8.0 %collective-permute-start.8 = (f32[160,128]{1,0:T(8,128)S(1)}, f32[160,128]{1,0:T(8,128)S(1)}, u32[]{:S(2)}, u32[]{:S(2)}) collective-permute-start(f32[160,128]{1,0:T(8,128)S(1)} %bitcast_dynamic-update-slice_fusion.own), channel_id=1, source_target_pairs={{0,248},{8,0},{16,8},{24,16},{32,24},{40,32},{48,40},{56,48},{64,5... | collective-permute-start | bytes 245768 | tf_op jit(solution)/shard_map/ppermute | solution.py:507
  51.9 1.6 collective-permute-done.8.above
  56.1 3.4 %collective-permute-start.10 = (f32[160,128]{1,0:T(8,128)S(1)}, f32[160,128]{1,0:T(8,128)S(1)}, u32[]{:S(2)}, u32[]{:S(2)}) collective-permute-start(f32[160,128]{1,0:T(8,128)S(1)} %bitcast_dynamic-update-slice_fusion.own), channel_id=1, source_target_pairs={{0,7},{1,0},{2,1},{3,2},{4,3},{5,4},{6,5},{7,6},{8,15},{9,8},{10,9... | collective-permute-start | bytes 245768 | tf_op jit(solution)/shard_map/ppermute | solution.py:507
  62.4 6.7 %shard_map.158 = (f32[132,64,128]{2,1,0:T(8,128)S(1)}, s32[132]{0:T(256)S(1)}, s32[132]{0:T(256)S(1)}, s32[1]{0:T(128)}, f32[128,128]{1,0:T(8,128)S(1)}, /*index...) custom-call(s32[4]{0:T(128)S(1)} %pad_add_fusion.ids, ...), custom_call_target="tpu_custom_call" | custom-call | flops 20000 | bytes 20000 | tf_op jit(solution)/shard_map/pallas_call | solution.py:36
  69.1 2.5 linearise.2
  71.7 4.8 %collective-permute-start.12 = (f32[64,128]{1,0:T(8,128)S(1)}, f32[64,128]{1,0:T(8,128)S(1)}, u32[]{:S(2)}, u32[]{:S(2)}) collective-permute-start(f32[64,128]{1,0:T(8,128)S(1)} %get-tuple-element.107.dir_cell.refs_0_.refs_21_), channel_id=1, source_target_pairs={{0,248},{8,0},{16,8},{24,16},{32,24},{40,32},{48,40},{56,48},{64,5... | collective-permute-start | bytes 98312 | tf_op jit(solution)/shard_map/ppermute | solution.py:507
  77.4 2.2 couple.10
  80.4 4.8 %collective-permute-start.16 = (f32[64,128]{1,0:T(8,128)S(1)}, f32[64,128]{1,0:T(8,128)S(1)}, u32[]{:S(2)}, u32[]{:S(2)}) collective-permute-start(f32[64,128]{1,0:T(8,128)S(1)} %get-tuple-element.119.dir_cell.refs_0_.refs_22_), channel_id=1, source_target_pairs={{0,248},{8,0},{16,8},{24,16},{32,24},{40,32},{48,40},{56,48},{64,5... | collective-permute-start | bytes 98312 | tf_op jit(solution)/shard_map/ppermute | solution.py:507
  86.2 1.8 collective-permute-start.18
  88.0 2.2 couple.11
  90.7 4.8 %collective-permute-start.20 = (f32[64,128]{1,0:T(8,128)S(1)}, f32[64,128]{1,0:T(8,128)S(1)}, u32[]{:S(2)}, u32[]{:S(2)}) collective-permute-start(f32[64,128]{1,0:T(8,128)S(1)} %get-tuple-element.124.dir_cell.refs_0_.refs_23_), channel_id=1, source_target_pairs={{0,248},{8,0},{16,8},{24,16},{32,24},{40,32},{48,40},{56,48},{64,5... | collective-permute-start | bytes 98312 | tf_op jit(solution)/shard_map/ppermute | solution.py:507
  95.7 2.7 %collective-permute-start.22 = (f32[64,128]{1,0:T(8,128)S(1)}, f32[64,128]{1,0:T(8,128)S(1)}, u32[]{:S(2)}, u32[]{:S(2)}) collective-permute-start(f32[64,128]{1,0:T(8,128)S(1)} %get-tuple-element.124.dir_cell.refs_0_.refs_23_), channel_id=1, source_target_pairs={{0,7},{1,0},{2,1},{3,2},{4,3},{5,4},{6,5},{7,6},{8,15},{9,8},{10,9... | collective-permute-start | bytes 98312 | tf_op jit(solution)/shard_map/ppermute | solution.py:507
  98.5 2.2 couple.12
  101.0 4.8 %collective-permute-start.24 = (f32[64,128]{1,0:T(8,128)S(1)}, f32[64,128]{1,0:T(8,128)S(1)}, u32[]{:S(2)}, u32[]{:S(2)}) collective-permute-start(f32[64,128]{1,0:T(8,128)S(1)} %get-tuple-element.129.dir_cell.refs_0_.refs_24_), channel_id=1, source_target_pairs={{0,248},{8,0},{16,8},{24,16},{32,24},{40,32},{48,40},{56,48},{64,5... | collective-permute-start | bytes 98312 | tf_op jit(solution)/shard_map/ppermute | solution.py:507
  105.8 3.0 %collective-permute-start.26 = (f32[64,128]{1,0:T(8,128)S(1)}, f32[64,128]{1,0:T(8,128)S(1)}, u32[]{:S(2)}, u32[]{:S(2)}) collective-permute-start(f32[64,128]{1,0:T(8,128)S(1)} %get-tuple-element.129.dir_cell.refs_0_.refs_24_), channel_id=1, source_target_pairs={{0,7},{1,0},{2,1},{3,2},{4,3},{5,4},{6,5},{7,6},{8,15},{9,8},{10,9... | collective-permute-start | bytes 98312 | tf_op jit(solution)/shard_map/ppermute | solution.py:507
  108.8 2.2 couple.13
  111.3 4.8 %collective-permute-start.28 = (f32[64,128]{1,0:T(8,128)S(1)}, f32[64,128]{1,0:T(8,128)S(1)}, u32[]{:S(2)}, u32[]{:S(2)}) collective-permute-start(f32[64,128]{1,0:T(8,128)S(1)} %get-tuple-element.134.dir_cell.refs_0_.refs_25_), channel_id=1, source_target_pairs={{0,248},{8,0},{16,8},{24,16},{32,24},{40,32},{48,40},{56,48},{64,5... | collective-permute-start | bytes 98312 | tf_op jit(solution)/shard_map/ppermute | solution.py:507
  116.1 3.0 %collective-permute-start.30 = (f32[64,128]{1,0:T(8,128)S(1)}, f32[64,128]{1,0:T(8,128)S(1)}, u32[]{:S(2)}, u32[]{:S(2)}) collective-permute-start(f32[64,128]{1,0:T(8,128)S(1)} %get-tuple-element.134.dir_cell.refs_0_.refs_25_), channel_id=1, source_target_pairs={{0,7},{1,0},{2,1},{3,2},{4,3},{5,4},{6,5},{7,6},{8,15},{9,8},{10,9... | collective-permute-start | bytes 98312 | tf_op jit(solution)/shard_map/ppermute | solution.py:507
  119.1 2.2 couple.14
  121.7 11.3 %all_to_all.35.parts = f32[8,24,128]{2,1,0:T(8,128)S(1)} all-to-all(f32[8,24,128]{2,1,0:T(8,128)S(1)} %inner_products.2), channel_id=1, replica_groups=mesh['region'=32,'frac'=8] {'frac'}, dimensions={0} | all-to-all | bytes 196608 | tf_op jit(solution)/shard_map/all_to_all | solution.py:526
  133.0 6.7 %all_to_all.36.parts = f32[4,24,128]{2,1,0:T(8,128)S(1)} all-to-all(f32[4,24,128]{2,1,0:T(8,128)S(1)} %shard_map.160), channel_id=1, replica_groups={{0,8,16,24},{32,40,48,56},{64,72,80,88},{96,104,112,120},{128,136,144,1..., dimensions={0} | all-to-all | bytes 98304 | tf_op jit(solution)/shard_map/all_to_all | solution.py:528
  139.8 12.6 %all_to_all.37.refs_20_ = f32[8,24,128]{2,1,0:T(8,128)S(1)} all-to-all(f32[8,24,128]{2,1,0:T(8,128)S(1)} %shard_map.161), channel_id=1, replica_groups={{0,32,64,96,128,160,192,224},{8,40,72,104,136,168,200,232},{16,48,80,11..., dimensions={0} | all-to-all | bytes 196608 | tf_op jit(solution)/shard_map/all_to_all | solution.py:530
  152.3 2.8 %linearise.3 = (f32[64,128]{1,0:T(8,128)S(1)}, f32[128,128]{1,0:T(8,128)S(1)}, f32[64,128]{1,0:T(8,128)S(1)}, f32[128,128]{1,0:T(8,128)S(1)}, f32[768,128]{1,0:T...) custom-call(s32[132]{0:T(256)S(1)} %get-tuple-element.95.refs_0_.slo, ...), custom_call_target="tpu_custom_call" | custom-call | flops 20000 | bytes 20000 | tf_op jit(solution)/shard_map/linearise/pallas_call | solution.py:36
  155.2 4.7 %collective-permute-start.32 = (f32[64,128]{1,0:T(8,128)S(1)}, f32[64,128]{1,0:T(8,128)S(1)}, u32[]{:S(2)}, u32[]{:S(2)}) collective-permute-start(f32[64,128]{1,0:T(8,128)S(1)} %get-tuple-element.146.dir_cell.refs_0_.refs_4_), channel_id=1, source_target_pairs={{0,248},{8,0},{16,8},{24,16},{32,24},{40,32},{48,40},{56,48},{64,5... | collective-permute-start | bytes 98312 | tf_op jit(solution)/shard_map/ppermute | solution.py:507
  160.0 3.8 %collective-permute-start.33 = (f32[64,128]{1,0:T(8,128)S(1)}, f32[64,128]{1,0:T(8,128)S(1)}, u32[]{:S(2)}, u32[]{:S(2)}) collective-permute-start(f32[64,128]{1,0:T(8,128)S(1)} %get-tuple-element.146.dir_cell.refs_0_.refs_4_), channel_id=1, source_target_pairs={{0,1},{1,2},{2,3},{3,4},{4,5},{5,6},{6,7},{7,0},{8,9},{9,10},{10,1... | collective-permute-start | bytes 98312 | tf_op jit(solution)/shard_map/ppermute | solution.py:507
  163.8 2.2 couple.15
  166.0 1.3 collective-permute-done.34.refs_4_
  167.6 4.8 %collective-permute-start.36 = (f32[64,128]{1,0:T(8,128)S(1)}, f32[64,128]{1,0:T(8,128)S(1)}, u32[]{:S(2)}, u32[]{:S(2)}) collective-permute-start(f32[64,128]{1,0:T(8,128)S(1)} %get-tuple-element.159.dir_cell.refs_0_.refs_5_), channel_id=1, source_target_pairs={{0,248},{8,0},{16,8},{24,16},{32,24},{40,32},{48,40},{56,48},{64,5... | collective-permute-start | bytes 98312 | tf_op jit(solution)/shard_map/ppermute | solution.py:507
  173.6 2.2 couple.16
  176.7 4.8 %collective-permute-start.40 = (f32[64,128]{1,0:T(8,128)S(1)}, f32[64,128]{1,0:T(8,128)S(1)}, u32[]{:S(2)}, u32[]{:S(2)}) collective-permute-start(f32[64,128]{1,0:T(8,128)S(1)} %get-tuple-element.164.dir_cell.refs_0_.refs_6_), channel_id=1, source_target_pairs={{0,248},{8,0},{16,8},{24,16},{32,24},{40,32},{48,40},{56,48},{64,5... | collective-permute-start | bytes 98312 | tf_op jit(solution)/shard_map/ppermute | solution.py:507
  182.4 1.5 collective-permute-start.42
  184.0 2.2 couple.17
  186.7 4.8 %collective-permute-start.44 = (f32[64,128]{1,0:T(8,128)S(1)}, f32[64,128]{1,0:T(8,128)S(1)}, u32[]{:S(2)}, u32[]{:S(2)}) collective-permute-start(f32[64,128]{1,0:T(8,128)S(1)} %get-tuple-element.169.dir_cell.refs_0_.refs_7_), channel_id=1, source_target_pairs={{0,248},{8,0},{16,8},{24,16},{32,24},{40,32},{48,40},{56,48},{64,5... | collective-permute-start | bytes 98312 | tf_op jit(solution)/shard_map/ppermute | solution.py:507
  192.0 2.5 collective-permute-start.46
  194.5 2.2 couple.18
  197.0 4.8 %collective-permute-start.48 = (f32[64,128]{1,0:T(8,128)S(1)}, f32[64,128]{1,0:T(8,128)S(1)}, u32[]{:S(2)}, u32[]{:S(2)}) collective-permute-start(f32[64,128]{1,0:T(8,128)S(1)} %get-tuple-element.174.dir_cell.refs_0_.refs_8_), channel_id=1, source_target_pairs={{0,248},{8,0},{16,8},{24,16},{32,24},{40,32},{48,40},{56,48},{64,5... | collective-permute-start | bytes 98312 | tf_op jit(solution)/shard_map/ppermute | solution.py:507
  201.8 3.0 %collective-permute-start.50 = (f32[64,128]{1,0:T(8,128)S(1)}, f32[64,128]{1,0:T(8,128)S(1)}, u32[]{:S(2)}, u32[]{:S(2)}) collective-permute-start(f32[64,128]{1,0:T(8,128)S(1)} %get-tuple-element.174.dir_cell.refs_0_.refs_8_), channel_id=1, source_target_pairs={{0,7},{1,0},{2,1},{3,2},{4,3},{5,4},{6,5},{7,6},{8,15},{9,8},{10,9... | collective-permute-start | bytes 98312 | tf_op jit(solution)/shard_map/ppermute | solution.py:507
  204.8 2.3 couple.19
  207.5 11.2 %all_to_all.38.parts = f32[8,24,128]{2,1,0:T(8,128)S(1)} all-to-all(f32[8,24,128]{2,1,0:T(8,128)S(1)} %inner_products.3), channel_id=1, replica_groups=mesh['region'=32,'frac'=8] {'frac'}, dimensions={0} | all-to-all | bytes 196608 | tf_op jit(solution)/shard_map/all_to_all | solution.py:526
  218.7 6.7 %all_to_all.39.parts = f32[4,24,128]{2,1,0:T(8,128)S(1)} all-to-all(f32[4,24,128]{2,1,0:T(8,128)S(1)} %shard_map.162), channel_id=1, replica_groups={{0,8,16,24},{32,40,48,56},{64,72,80,88},{96,104,112,120},{128,136,144,1..., dimensions={0} | all-to-all | bytes 98304 | tf_op jit(solution)/shard_map/all_to_all | solution.py:528
  225.5 10.3 %all_to_all.40.refs_0_ = f32[8,24,128]{2,1,0:T(8,128)S(1)} all-to-all(f32[8,24,128]{2,1,0:T(8,128)S(1)} %shard_map.163), channel_id=1, replica_groups={{0,32,64,96,128,160,192,224},{8,40,72,104,136,168,200,232},{16,48,80,11..., dimensions={0} | all-to-all | bytes 196608 | tf_op jit(solution)/shard_map/all_to_all | solution.py:530
  236.6 10.5 %all_to_all.41 = f32[8,16,128]{2,1,0:T(8,128)S(1)} all-to-all(f32[8,16,128]{2,1,0:T(8,128)S(1)} %bitcast.38), channel_id=1, replica_groups=mesh['region'=32,'frac'=8] {'frac'}, dimensions={0} | all-to-all | bytes 131072 | tf_op jit(solution)/shard_map/all_to_all | solution.py:733
  (134 shorter events, 28.2 us)
Async XLA Ops:
  0.6 17.2 %collective-permute-start = (f32[16,64,128]{2,1,0:T(8,128)}, f32[16,64,128]{2,1,0:T(8,128)S(1)}, u32[]{:S(2)}, u32[]{:S(2)}) collective-permute-start(f32[16,64,128]{2,1,0:T(8,128)} %refs_0_.1), channel_id=1, source_target_pairs={{0,2},{1,3},{2,4},{3,5},{4,6},{5,7},{6,0},{7,1},{8,10},{9,11},{10,... | collective-permute-start | bytes 1572872 | tf_op jit(solution)/shard_map/ppermute | solution.py:507
  2.8 25.2 %collective-permute-start.1 = (f32[16,64,128]{2,1,0:T(8,128)}, f32[16,64,128]{2,1,0:T(8,128)S(1)}, u32[]{:S(2)}, u32[]{:S(2)}) collective-permute-start(f32[16,64,128]{2,1,0:T(8,128)} %refs_0_.1), channel_id=1, source_target_pairs={{0,4},{1,5},{2,6},{3,7},{4,0},{5,1},{6,2},{7,3},{8,12},{9,13},{10,... | collective-permute-start | bytes 1572872 | tf_op jit(solution)/shard_map/ppermute | solution.py:507
  5.2 24.3 %collective-permute-start.2 = (f32[16,64,128]{2,1,0:T(8,128)}, f32[16,64,128]{2,1,0:T(8,128)S(1)}, u32[]{:S(2)}, u32[]{:S(2)}) collective-permute-start(f32[16,64,128]{2,1,0:T(8,128)} %refs_0_.1), channel_id=1, source_target_pairs={{0,6},{1,7},{2,0},{3,1},{4,2},{5,3},{6,4},{7,5},{8,14},{9,15},{10,... | collective-permute-start | bytes 1572872 | tf_op jit(solution)/shard_map/ppermute | solution.py:507
  6.4 55.0 %collective-permute-start.3 = (f32[16,64,128]{2,1,0:T(8,128)}, f32[16,64,128]{2,1,0:T(8,128)S(1)}, u32[]{:S(2)}, u32[]{:S(2)}) collective-permute-start(f32[16,64,128]{2,1,0:T(8,128)} %refs_0_.1), channel_id=1, source_target_pairs={{0,1},{1,0},{2,3},{3,2},{4,5},{5,4},{6,7},{7,6},{8,9},{9,8},{10,11... | collective-permute-start | bytes 1572872 | tf_op jit(solution)/shard_map/ppermute | solution.py:511
  11.5 32.3 %collective-permute-start.7 = (f32[160,128]{1,0:T(8,128)S(1)}, f32[160,128]{1,0:T(8,128)S(1)}, u32[]{:S(2)}, u32[]{:S(2)}) collective-permute-start(f32[160,128]{1,0:T(8,128)S(1)} %bitcast_dynamic-update-slice_fusion.own), channel_id=1, source_target_pairs={{0,8},{8,16},{16,24},{24,32},{32,40},{40,48},{48,56},{56,64},{64,7... | collective-permute-start | bytes 245768 | tf_op jit(solution)/shard_map/ppermute | solution.py:507
  17.9 43.5 %collective-permute-start.4 = (f32[16,64,128]{2,1,0:T(8,128)S(1)}, f32[16,64,128]{2,1,0:T(8,128)S(1)}, u32[]{:S(2)}, u32[]{:S(2)}) collective-permute-start(f32[16,64,128]{2,1,0:T(8,128)S(1)} %collective-permute-done.refs_1_), channel_id=1, source_target_pairs={{0,1},{1,0},{2,3},{3,2},{4,5},{5,4},{6,7},{7,6},{8,9},{9,8},{10,11... | collective-permute-start | bytes 1572872 | tf_op jit(solution)/shard_map/ppermute | solution.py:511
  28.0 33.4 %collective-permute-start.5 = (f32[16,64,128]{2,1,0:T(8,128)S(1)}, f32[16,64,128]{2,1,0:T(8,128)S(1)}, u32[]{:S(2)}, u32[]{:S(2)}) collective-permute-start(f32[16,64,128]{2,1,0:T(8,128)S(1)} %collective-permute-done.1.refs_2_), channel_id=1, source_target_pairs={{0,1},{1,0},{2,3},{3,2},{4,5},{5,4},{6,7},{7,6},{8,9},{9,8},{10,11... | collective-permute-start | bytes 1572872 | tf_op jit(solution)/shard_map/ppermute | solution.py:511
  29.5 31.8 %collective-permute-start.6 = (f32[16,64,128]{2,1,0:T(8,128)S(1)}, f32[16,64,128]{2,1,0:T(8,128)}, u32[]{:S(2)}, u32[]{:S(2)}) collective-permute-start(f32[16,64,128]{2,1,0:T(8,128)S(1)} %collective-permute-done.2.refs_3_), channel_id=1, source_target_pairs={{0,1},{1,0},{2,3},{3,2},{4,5},{5,4},{6,7},{7,6},{8,9},{9,8},{10,11... | collective-permute-start | bytes 1572872 | tf_op jit(solution)/shard_map/ppermute | solution.py:511
  43.8 9.7 %collective-permute-start.8 = (f32[160,128]{1,0:T(8,128)S(1)}, f32[160,128]{1,0:T(8,128)S(1)}, u32[]{:S(2)}, u32[]{:S(2)}) collective-permute-start(f32[160,128]{1,0:T(8,128)S(1)} %bitcast_dynamic-update-slice_fusion.own), channel_id=1, source_target_pairs={{0,248},{8,0},{16,8},{24,16},{32,24},{40,32},{48,40},{56,48},{64,5... | collective-permute-start | bytes 245768 | tf_op jit(solution)/shard_map/ppermute | solution.py:507
  56.1 4.5 %collective-permute-start.10 = (f32[160,128]{1,0:T(8,128)S(1)}, f32[160,128]{1,0:T(8,128)S(1)}, u32[]{:S(2)}, u32[]{:S(2)}) collective-permute-start(f32[160,128]{1,0:T(8,128)S(1)} %bitcast_dynamic-update-slice_fusion.own), channel_id=1, source_target_pairs={{0,7},{1,0},{2,1},{3,2},{4,3},{5,4},{6,5},{7,6},{8,15},{9,8},{10,9... | collective-permute-start | bytes 245768 | tf_op jit(solution)/shard_map/ppermute | solution.py:507
  71.6 8.1 %collective-permute-start.11 = (f32[64,128]{1,0:T(8,128)S(1)}, f32[64,128]{1,0:T(8,128)S(1)}, u32[]{:S(2)}, u32[]{:S(2)}) collective-permute-start(f32[64,128]{1,0:T(8,128)S(1)} %get-tuple-element.107.dir_cell.refs_0_.refs_21_), channel_id=1, source_target_pairs={{0,8},{8,16},{16,24},{24,32},{32,40},{40,48},{48,56},{56,64},{64,7... | collective-permute-start | bytes 98312 | tf_op jit(solution)/shard_map/ppermute | solution.py:507
  71.7 8.0 %collective-permute-start.12 = (f32[64,128]{1,0:T(8,128)S(1)}, f32[64,128]{1,0:T(8,128)S(1)}, u32[]{:S(2)}, u32[]{:S(2)}) collective-permute-start(f32[64,128]{1,0:T(8,128)S(1)} %get-tuple-element.107.dir_cell.refs_0_.refs_21_), channel_id=1, source_target_pairs={{0,248},{8,0},{16,8},{24,16},{32,24},{40,32},{48,40},{56,48},{64,5... | collective-permute-start | bytes 98312 | tf_op jit(solution)/shard_map/ppermute | solution.py:507
  76.9 3.3 %collective-permute-start.14 = (f32[64,128]{1,0:T(8,128)S(1)}, f32[64,128]{1,0:T(8,128)S(1)}, u32[]{:S(2)}, u32[]{:S(2)}) collective-permute-start(f32[64,128]{1,0:T(8,128)S(1)} %get-tuple-element.107.dir_cell.refs_0_.refs_21_), channel_id=1, source_target_pairs={{0,7},{1,0},{2,1},{3,2},{4,3},{5,4},{6,5},{7,6},{8,15},{9,8},{10,9... | collective-permute-start | bytes 98312 | tf_op jit(solution)/shard_map/ppermute | solution.py:507
  80.3 9.9 %collective-permute-start.15 = (f32[64,128]{1,0:T(8,128)S(1)}, f32[64,128]{1,0:T(8,128)S(1)}, u32[]{:S(2)}, u32[]{:S(2)}) collective-permute-start(f32[64,128]{1,0:T(8,128)S(1)} %get-tuple-element.119.dir_cell.refs_0_.refs_22_), channel_id=1, source_target_pairs={{0,8},{8,16},{16,24},{24,32},{32,40},{40,48},{48,56},{56,64},{64,7... | collective-permute-start | bytes 98312 | tf_op jit(solution)/shard_map/ppermute | solution.py:507
  80.4 9.8 %collective-permute-start.16 = (f32[64,128]{1,0:T(8,128)S(1)}, f32[64,128]{1,0:T(8,128)S(1)}, u32[]{:S(2)}, u32[]{:S(2)}) collective-permute-start(f32[64,128]{1,0:T(8,128)S(1)} %get-tuple-element.119.dir_cell.refs_0_.refs_22_), channel_id=1, source_target_pairs={{0,248},{8,0},{16,8},{24,16},{32,24},{40,32},{48,40},{56,48},{64,5... | collective-permute-start | bytes 98312 | tf_op jit(solution)/shard_map/ppermute | solution.py:507
  85.2 5.1 %collective-permute-start.17 = (f32[64,128]{1,0:T(8,128)S(1)}, f32[64,128]{1,0:T(8,128)S(1)}, u32[]{:S(2)}, u32[]{:S(2)}) collective-permute-start(f32[64,128]{1,0:T(8,128)S(1)} %get-tuple-element.119.dir_cell.refs_0_.refs_22_), channel_id=1, source_target_pairs={{0,1},{1,2},{2,3},{3,4},{4,5},{5,6},{6,7},{7,0},{8,9},{9,10},{10,1... | collective-permute-start | bytes 98312 | tf_op jit(solution)/shard_map/ppermute | solution.py:507
  86.2 4.1 %collective-permute-start.18 = (f32[64,128]{1,0:T(8,128)S(1)}, f32[64,128]{1,0:T(8,128)S(1)}, u32[]{:S(2)}, u32[]{:S(2)}) collective-permute-start(f32[64,128]{1,0:T(8,128)S(1)} %get-tuple-element.119.dir_cell.refs_0_.refs_22_), channel_id=1, source_target_pairs={{0,7},{1,0},{2,1},{3,2},{4,3},{5,4},{6,5},{7,6},{8,15},{9,8},{10,9... | collective-permute-start | bytes 98312 | tf_op jit(solution)/shard_map/ppermute | solution.py:507
  90.4 10.3 %collective-permute-start.19 = (f32[64,128]{1,0:T(8,128)S(1)}, f32[64,128]{1,0:T(8,128)S(1)}, u32[]{:S(2)}, u32[]{:S(2)}) collective-permute-start(f32[64,128]{1,0:T(8,128)S(1)} %get-tuple-element.124.dir_cell.refs_0_.refs_23_), channel_id=1, source_target_pairs={{0,8},{8,16},{16,24},{24,32},{32,40},{40,48},{48,56},{56,64},{64,7... | collective-permute-start | bytes 98312 | tf_op jit(solution)/shard_map/ppermute | solution.py:507
  90.7 10.1 %collective-permute-start.20 = (f32[64,128]{1,0:T(8,128)S(1)}, f32[64,128]{1,0:T(8,128)S(1)}, u32[]{:S(2)}, u32[]{:S(2)}) collective-permute-start(f32[64,128]{1,0:T(8,128)S(1)} %get-tuple-element.124.dir_cell.refs_0_.refs_23_), channel_id=1, source_target_pairs={{0,248},{8,0},{16,8},{24,16},{32,24},{40,32},{48,40},{56,48},{64,5... | collective-permute-start | bytes 98312 | tf_op jit(solution)/shard_map/ppermute | solution.py:507
  95.5 5.3 %collective-permute-start.21 = (f32[64,128]{1,0:T(8,128)S(1)}, f32[64,128]{1,0:T(8,128)S(1)}, u32[]{:S(2)}, u32[]{:S(2)}) collective-permute-start(f32[64,128]{1,0:T(8,128)S(1)} %get-tuple-element.124.dir_cell.refs_0_.refs_23_), channel_id=1, source_target_pairs={{0,1},{1,2},{2,3},{3,4},{4,5},{5,6},{6,7},{7,0},{8,9},{9,10},{10,1... | collective-permute-start | bytes 98312 | tf_op jit(solution)/shard_map/ppermute | solution.py:507
  95.7 5.0 %collective-permute-start.22 = (f32[64,128]{1,0:T(8,128)S(1)}, f32[64,128]{1,0:T(8,128)S(1)}, u32[]{:S(2)}, u32[]{:S(2)}) collective-permute-start(f32[64,128]{1,0:T(8,128)S(1)} %get-tuple-element.124.dir_cell.refs_0_.refs_23_), channel_id=1, source_target_pairs={{0,7},{1,0},{2,1},{3,2},{4,3},{5,4},{6,5},{7,6},{8,15},{9,8},{10,9... | collective-permute-start | bytes 98312 | tf_op jit(solution)/shard_map/ppermute | solution.py:507
  100.9 10.1 %collective-permute-start.23 = (f32[64,128]{1,0:T(8,128)S(1)}, f32[64,128]{1,0:T(8,128)S(1)}, u32[]{:S(2)}, u32[]{:S(2)}) collective-permute-start(f32[64,128]{1,0:T(8,128)S(1)} %get-tuple-element.129.dir_cell.refs_0_.refs_24_), channel_id=1, source_target_pairs={{0,8},{8,16},{16,24},{24,32},{32,40},{40,48},{48,56},{56,64},{64,7... | collective-permute-start | bytes 98312 | tf_op jit(solution)/shard_map/ppermute | solution.py:507
  101.0 10.1 %collective-permute-start.24 = (f32[64,128]{1,0:T(8,128)S(1)}, f32[64,128]{1,0:T(8,128)S(1)}, u32[]{:S(2)}, u32[]{:S(2)}) collective-permute-start(f32[64,128]{1,0:T(8,128)S(1)} %get-tuple-element.129.dir_cell.refs_0_.refs_24_), channel_id=1, source_target_pairs={{0,248},{8,0},{16,8},{24,16},{32,24},{40,32},{48,40},{56,48},{64,5... | collective-permute-start | bytes 98312 | tf_op jit(solution)/shard_map/ppermute | solution.py:507
  105.8 5.3 %collective-permute-start.25 = (f32[64,128]{1,0:T(8,128)S(1)}, f32[64,128]{1,0:T(8,128)S(1)}, u32[]{:S(2)}, u32[]{:S(2)}) collective-permute-start(f32[64,128]{1,0:T(8,128)S(1)} %get-tuple-element.129.dir_cell.refs_0_.refs_24_), channel_id=1, source_target_pairs={{0,1},{1,2},{2,3},{3,4},{4,5},{5,6},{6,7},{7,0},{8,9},{9,10},{10,1... | collective-permute-start | bytes 98312 | tf_op jit(solution)/shard_map/ppermute | solution.py:507
  105.8 5.3 %collective-permute-start.26 = (f32[64,128]{1,0:T(8,128)S(1)}, f32[64,128]{1,0:T(8,128)S(1)}, u32[]{:S(2)}, u32[]{:S(2)}) collective-permute-start(f32[64,128]{1,0:T(8,128)S(1)} %get-tuple-element.129.dir_cell.refs_0_.refs_24_), channel_id=1, source_target_pairs={{0,7},{1,0},{2,1},{3,2},{4,3},{5,4},{6,5},{7,6},{8,15},{9,8},{10,9... | collective-permute-start | bytes 98312 | tf_op jit(solution)/shard_map/ppermute | solution.py:507
  111.2 10.1 %collective-permute-start.27 = (f32[64,128]{1,0:T(8,128)S(1)}, f32[64,128]{1,0:T(8,128)S(1)}, u32[]{:S(2)}, u32[]{:S(2)}) collective-permute-start(f32[64,128]{1,0:T(8,128)S(1)} %get-tuple-element.134.dir_cell.refs_0_.refs_25_), channel_id=1, source_target_pairs={{0,8},{8,16},{16,24},{24,32},{32,40},{40,48},{48,56},{56,64},{64,7... | collective-permute-start | bytes 98312 | tf_op jit(solution)/shard_map/ppermute | solution.py:507
  111.3 10.1 %collective-permute-start.28 = (f32[64,128]{1,0:T(8,128)S(1)}, f32[64,128]{1,0:T(8,128)S(1)}, u32[]{:S(2)}, u32[]{:S(2)}) collective-permute-start(f32[64,128]{1,0:T(8,128)S(1)} %get-tuple-element.134.dir_cell.refs_0_.refs_25_), channel_id=1, source_target_pairs={{0,248},{8,0},{16,8},{24,16},{32,24},{40,32},{48,40},{56,48},{64,5... | collective-permute-start | bytes 98312 | tf_op jit(solution)/shard_map/ppermute | solution.py:507
  116.1 5.3 %collective-permute-start.29 = (f32[64,128]{1,0:T(8,128)S(1)}, f32[64,128]{1,0:T(8,128)S(1)}, u32[]{:S(2)}, u32[]{:S(2)}) collective-permute-start(f32[64,128]{1,0:T(8,128)S(1)} %get-tuple-element.134.dir_cell.refs_0_.refs_25_), channel_id=1, source_target_pairs={{0,1},{1,2},{2,3},{3,4},{4,5},{5,6},{6,7},{7,0},{8,9},{9,10},{10,1... | collective-permute-start | bytes 98312 | tf_op jit(solution)/shard_map/ppermute | solution.py:507
  116.1 5.3 %collective-permute-start.30 = (f32[64,128]{1,0:T(8,128)S(1)}, f32[64,128]{1,0:T(8,128)S(1)}, u32[]{:S(2)}, u32[]{:S(2)}) collective-permute-start(f32[64,128]{1,0:T(8,128)S(1)} %get-tuple-element.134.dir_cell.refs_0_.refs_25_), channel_id=1, source_target_pairs={{0,7},{1,0},{2,1},{3,2},{4,3},{5,4},{6,5},{7,6},{8,15},{9,8},{10,9... | collective-permute-start | bytes 98312 | tf_op jit(solution)/shard_map/ppermute | solution.py:507
  155.1 10.9 %collective-permute-start.31 = (f32[64,128]{1,0:T(8,128)S(1)}, f32[64,128]{1,0:T(8,128)S(1)}, u32[]{:S(2)}, u32[]{:S(2)}) collective-permute-start(f32[64,128]{1,0:T(8,128)S(1)} %get-tuple-element.146.dir_cell.refs_0_.refs_4_), channel_id=1, source_target_pairs={{0,8},{8,16},{16,24},{24,32},{32,40},{40,48},{48,56},{56,64},{64,7... | collective-permute-start | bytes 98312 | tf_op jit(solution)/shard_map/ppermute | solution.py:507
  155.2 10.8 %collective-permute-start.32 = (f32[64,128]{1,0:T(8,128)S(1)}, f32[64,128]{1,0:T(8,128)S(1)}, u32[]{:S(2)}, u32[]{:S(2)}) collective-permute-start(f32[64,128]{1,0:T(8,128)S(1)} %get-tuple-element.146.dir_cell.refs_0_.refs_4_), channel_id=1, source_target_pairs={{0,248},{8,0},{16,8},{24,16},{32,24},{40,32},{48,40},{56,48},{64,5... | collective-permute-start | bytes 98312 | tf_op jit(solution)/shard_map/ppermute | solution.py:507
  160.0 6.1 %collective-permute-start.33 = (f32[64,128]{1,0:T(8,128)S(1)}, f32[64,128]{1,0:T(8,128)S(1)}, u32[]{:S(2)}, u32[]{:S(2)}) collective-permute-start(f32[64,128]{1,0:T(8,128)S(1)} %get-tuple-element.146.dir_cell.refs_0_.refs_4_), channel_id=1, source_target_pairs={{0,1},{1,2},{2,3},{3,4},{4,5},{5,6},{6,7},{7,0},{8,9},{9,10},{10,1... | collective-permute-start | bytes 98312 | tf_op jit(solution)/shard_map/ppermute | solution.py:507
  163.7 3.6 %collective-permute-start.34 = (f32[64,128]{1,0:T(8,128)S(1)}, f32[64,128]{1,0:T(8,128)S(1)}, u32[]{:S(2)}, u32[]{:S(2)}) collective-permute-start(f32[64,128]{1,0:T(8,128)S(1)} %get-tuple-element.146.dir_cell.refs_0_.refs_4_), channel_id=1, source_target_pairs={{0,7},{1,0},{2,1},{3,2},{4,3},{5,4},{6,5},{7,6},{8,15},{9,8},{10,9... | collective-permute-start | bytes 98312 | tf_op jit(solution)/shard_map/ppermute | solution.py:507
  167.5 8.4 %collective-permute-start.35 = (f32[64,128]{1,0:T(8,128)S(1)}, f32[64,128]{1,0:T(8,128)S(1)}, u32[]{:S(2)}, u32[]{:S(2)}) collective-permute-start(f32[64,128]{1,0:T(8,128)S(1)} %get-tuple-element.159.dir_cell.refs_0_.refs_5_), channel_id=1, source_target_pairs={{0,8},{8,16},{16,24},{24,32},{32,40},{40,48},{48,56},{56,64},{64,7... | collective-permute-start | bytes 98312 | tf_op jit(solution)/shard_map/ppermute | solution.py:507
  167.6 8.3 %collective-permute-start.36 = (f32[64,128]{1,0:T(8,128)S(1)}, f32[64,128]{1,0:T(8,128)S(1)}, u32[]{:S(2)}, u32[]{:S(2)}) collective-permute-start(f32[64,128]{1,0:T(8,128)S(1)} %get-tuple-element.159.dir_cell.refs_0_.refs_5_), channel_id=1, source_target_pairs={{0,248},{8,0},{16,8},{24,16},{32,24},{40,32},{48,40},{56,48},{64,5... | collective-permute-start | bytes 98312 | tf_op jit(solution)/shard_map/ppermute | solution.py:507
  172.4 3.5 %collective-permute-start.37 = (f32[64,128]{1,0:T(8,128)S(1)}, f32[64,128]{1,0:T(8,128)S(1)}, u32[]{:S(2)}, u32[]{:S(2)}) collective-permute-start(f32[64,128]{1,0:T(8,128)S(1)} %get-tuple-element.159.dir_cell.refs_0_.refs_5_), channel_id=1, source_target_pairs={{0,1},{1,2},{2,3},{3,4},{4,5},{5,6},{6,7},{7,0},{8,9},{9,10},{10,1... | collective-permute-start | bytes 98312 | tf_op jit(solution)/shard_map/ppermute | solution.py:507
  176.6 9.6 %collective-permute-start.39 = (f32[64,128]{1,0:T(8,128)S(1)}, f32[64,128]{1,0:T(8,128)S(1)}, u32[]{:S(2)}, u32[]{:S(2)}) collective-permute-start(f32[64,128]{1,0:T(8,128)S(1)} %get-tuple-element.164.dir_cell.refs_0_.refs_6_), channel_id=1, source_target_pairs={{0,8},{8,16},{16,24},{24,32},{32,40},{40,48},{48,56},{56,64},{64,7... | collective-permute-start | bytes 98312 | tf_op jit(solution)/shard_map/ppermute | solution.py:507
  176.7 9.6 %collective-permute-start.40 = (f32[64,128]{1,0:T(8,128)S(1)}, f32[64,128]{1,0:T(8,128)S(1)}, u32[]{:S(2)}, u32[]{:S(2)}) collective-permute-start(f32[64,128]{1,0:T(8,128)S(1)} %get-tuple-element.164.dir_cell.refs_0_.refs_6_), channel_id=1, source_target_pairs={{0,248},{8,0},{16,8},{24,16},{32,24},{40,32},{48,40},{56,48},{64,5... | collective-permute-start | bytes 98312 | tf_op jit(solution)/shard_map/ppermute | solution.py:507
  181.4 4.8 %collective-permute-start.41 = (f32[64,128]{1,0:T(8,128)S(1)}, f32[64,128]{1,0:T(8,128)S(1)}, u32[]{:S(2)}, u32[]{:S(2)}) collective-permute-start(f32[64,128]{1,0:T(8,128)S(1)} %get-tuple-element.164.dir_cell.refs_0_.refs_6_), channel_id=1, source_target_pairs={{0,1},{1,2},{2,3},{3,4},{4,5},{5,6},{6,7},{7,0},{8,9},{9,10},{10,1... | collective-permute-start | bytes 98312 | tf_op jit(solution)/shard_map/ppermute | solution.py:507
  182.4 3.8 %collective-permute-start.42 = (f32[64,128]{1,0:T(8,128)S(1)}, f32[64,128]{1,0:T(8,128)S(1)}, u32[]{:S(2)}, u32[]{:S(2)}) collective-permute-start(f32[64,128]{1,0:T(8,128)S(1)} %get-tuple-element.164.dir_cell.refs_0_.refs_6_), channel_id=1, source_target_pairs={{0,7},{1,0},{2,1},{3,2},{4,3},{5,4},{6,5},{7,6},{8,15},{9,8},{10,9... | collective-permute-start | bytes 98312 | tf_op jit(solution)/shard_map/ppermute | solution.py:507
  186.4 10.4 %collective-permute-start.43 = (f32[64,128]{1,0:T(8,128)S(1)}, f32[64,128]{1,0:T(8,128)S(1)}, u32[]{:S(2)}, u32[]{:S(2)}) collective-permute-start(f32[64,128]{1,0:T(8,128)S(1)} %get-tuple-element.169.dir_cell.refs_0_.refs_7_), channel_id=1, source_target_pairs={{0,8},{8,16},{16,24},{24,32},{32,40},{40,48},{48,56},{56,64},{64,7... | collective-permute-start | bytes 98312 | tf_op jit(solution)/shard_map/ppermute | solution.py:507
  186.7 10.1 %collective-permute-start.44 = (f32[64,128]{1,0:T(8,128)S(1)}, f32[64,128]{1,0:T(8,128)S(1)}, u32[]{:S(2)}, u32[]{:S(2)}) collective-permute-start(f32[64,128]{1,0:T(8,128)S(1)} %get-tuple-element.169.dir_cell.refs_0_.refs_7_), channel_id=1, source_target_pairs={{0,248},{8,0},{16,8},{24,16},{32,24},{40,32},{48,40},{56,48},{64,5... | collective-permute-start | bytes 98312 | tf_op jit(solution)/shard_map/ppermute | solution.py:507
  191.5 5.3 %collective-permute-start.45 = (f32[64,128]{1,0:T(8,128)S(1)}, f32[64,128]{1,0:T(8,128)S(1)}, u32[]{:S(2)}, u32[]{:S(2)}) collective-permute-start(f32[64,128]{1,0:T(8,128)S(1)} %get-tuple-element.169.dir_cell.refs_0_.refs_7_), channel_id=1, source_target_pairs={{0,1},{1,2},{2,3},{3,4},{4,5},{5,6},{6,7},{7,0},{8,9},{9,10},{10,1... | collective-permute-start | bytes 98312 | tf_op jit(solution)/shard_map/ppermute | solution.py:507
  192.0 4.8 %collective-permute-start.46 = (f32[64,128]{1,0:T(8,128)S(1)}, f32[64,128]{1,0:T(8,128)S(1)}, u32[]{:S(2)}, u32[]{:S(2)}) collective-permute-start(f32[64,128]{1,0:T(8,128)S(1)} %get-tuple-element.169.dir_cell.refs_0_.refs_7_), channel_id=1, source_target_pairs={{0,7},{1,0},{2,1},{3,2},{4,3},{5,4},{6,5},{7,6},{8,15},{9,8},{10,9... | collective-permute-start | bytes 98312 | tf_op jit(solution)/shard_map/ppermute | solution.py:507
  196.9 10.1 %collective-permute-start.47 = (f32[64,128]{1,0:T(8,128)S(1)}, f32[64,128]{1,0:T(8,128)S(1)}, u32[]{:S(2)}, u32[]{:S(2)}) collective-permute-start(f32[64,128]{1,0:T(8,128)S(1)} %get-tuple-element.174.dir_cell.refs_0_.refs_8_), channel_id=1, source_target_pairs={{0,8},{8,16},{16,24},{24,32},{32,40},{40,48},{48,56},{56,64},{64,7... | collective-permute-start | bytes 98312 | tf_op jit(solution)/shard_map/ppermute | solution.py:507
  197.0 10.1 %collective-permute-start.48 = (f32[64,128]{1,0:T(8,128)S(1)}, f32[64,128]{1,0:T(8,128)S(1)}, u32[]{:S(2)}, u32[]{:S(2)}) collective-permute-start(f32[64,128]{1,0:T(8,128)S(1)} %get-tuple-element.174.dir_cell.refs_0_.refs_8_), channel_id=1, source_target_pairs={{0,248},{8,0},{16,8},{24,16},{32,24},{40,32},{48,40},{56,48},{64,5... | collective-permute-start | bytes 98312 | tf_op jit(solution)/shard_map/ppermute | solution.py:507
  201.8 5.3 %collective-permute-start.49 = (f32[64,128]{1,0:T(8,128)S(1)}, f32[64,128]{1,0:T(8,128)S(1)}, u32[]{:S(2)}, u32[]{:S(2)}) collective-permute-start(f32[64,128]{1,0:T(8,128)S(1)} %get-tuple-element.174.dir_cell.refs_0_.refs_8_), channel_id=1, source_target_pairs={{0,1},{1,2},{2,3},{3,4},{4,5},{5,6},{6,7},{7,0},{8,9},{9,10},{10,1... | collective-permute-start | bytes 98312 | tf_op jit(solution)/shard_map/ppermute | solution.py:507
  201.8 5.3 %collective-permute-start.50 = (f32[64,128]{1,0:T(8,128)S(1)}, f32[64,128]{1,0:T(8,128)S(1)}, u32[]{:S(2)}, u32[]{:S(2)}) collective-permute-start(f32[64,128]{1,0:T(8,128)S(1)} %get-tuple-element.174.dir_cell.refs_0_.refs_8_), channel_id=1, source_target_pairs={{0,7},{1,0},{2,1},{3,2},{4,3},{5,4},{6,5},{7,6},{8,15},{9,8},{10,9... | collective-permute-start | bytes 98312 | tf_op jit(solution)/shard_map/ppermute | solution.py:507
  (8 other events, 240.1 us)

commit v2 on v1

--- a/solution.py
+++ b/solution.py
@@ -12,7 +12,6 @@
 SCALE = 1.0 / 16.0
 UNROLL = 4
 PAIRS = [(i, j) for i in range(SWEEPS + 1) for j in range(i, SWEEPS + 1)]
-DOTS = 24
 F32 = jnp.float32
 VMEM_LIMIT = 24 * 2**20
 
@@ -22,7 +21,7 @@
 
 
 def smem_i32(*shape):
-    return jax.ShapeDtypeStruct(shape, jnp.int32)
+    return pltpu.SMEM(shape, jnp.int32)
 
 
 def call(body, outs, args, spaces, scratch=(), out_spaces=None, flops=20000, name=None):
@@ -30,8 +29,12 @@
     for arg, space in zip(args, spaces):
         if space == "v":
             arg = pltpu.with_memory_space_constraint(arg, pltpu.VMEM)
+        elif space == "H":
+            arg = pltpu.with_memory_space_constraint(arg, pltpu.HBM)
+        elif space == "S":
+            arg = pltpu.with_memory_space_constraint(arg, pltpu.SMEM)
         ins.append(arg)
-    kinds = {"v": pltpu.VMEM, "s": pltpu.SMEM, "a": pl.ANY}
+    kinds = {"v": pltpu.VMEM, "h": pltpu.VMEM, "s": pltpu.SMEM, "S": pltpu.SMEM, "a": pl.ANY, "H": pltpu.HBM}
     out_spaces = out_spaces or "v" * len(outs)
     return pl.pallas_call(
         body,
@@ -90,7 +93,7 @@
         faces_ref[32 * f : 32 * f + 32] = jnp.where(inside[f], harmonic(here, perm[f]), 0.0)
     flag_z = block[0][96:128]
     flag_x = block[0][128:160]
-    y_here = flag_y[...].astype(F32)
+    y_here = flag_y[...]
     z_prev = block[1][96:128]
     y_prev = pltpu.roll(y_here, 1, 0)
     x_prev = neighbours(flag_x, flag_x, flag_x, block[3][128:160], flag_x)[5]
@@ -101,80 +104,155 @@
         own_up_ref[32 * f : 32 * f + 32] = upstream if forward else 1.0 - upstream
 
 
-def collect(
-    ids, codes, *refs
+def pack(
+    ids, parts, rows, live, pres, satur, perm, flags, q, r, trans, ups, store,
+    ids_out, message, record, cell, flag_y, flag_room, up_room, store_room, sems,
 ):
-    pieces = refs[:8]
-    record = refs[8]
-    weights, slots, rows, count, seg_old, seg_face, seg_up, seg_store, seg_live, sems = refs[9:]
+    copies = [
+        pltpu.make_async_copy(src, dst, sems.at[n])
+        for n, (src, dst) in enumerate(
+            (
+                (pres.at[0], cell.at[0:32]),
+                (satur.at[0], cell.at[32:64]),
+                (perm.at[0], message.at[64:96]),
+                (flags, flag_room),
+                (q, record.at[0:8]),
+                (r, record.at[8:16]),
+                (trans, record.at[16:24]),
+                (ups, up_room),
+                (store, store_room),
+            )
+        )
+    ]
+    for copy in copies:
+        copy.start()
+    for k in range(4):
+        ids_out[k] = ids[k]
+    lane = lax.broadcasted_iota(jnp.int32, (8, 128), 1)
+    codes = jnp.full((8, 128), -1.0, F32)
+    for k in range(16):
+        code = jnp.where(k < live[0], parts[k] * 32 + rows[k], -1)
+        codes = jnp.where(lane == k, code.astype(F32), codes)
+    record[48:56] = codes
+    for copy in copies:
+        copy.wait()
+    message[0:64] = cell[...]
+    message[96:128] = flag_room[0, 0].astype(F32)
+    message[128:160] = flag_room[2, 0].astype(F32)
+    flag_y[...] = flag_room[1, 0].astype(F32)
+    record[24:32] = up_room[...].astype(F32)
+    for k in range(8):
+        for c in range(2):
+            row = 32 + 8 * c + k
+            record[row : row + 1] = store_room[c : c + 1, 128 * k : 128 * k + 128]
+    first = message[0:128].T
+    rest = jnp.concatenate([message[128:160], jnp.zeros((96, 128), F32)], axis=0).T
+    record[56:57] = first[127:128]
+    record[57:58] = rest[127:128]
+    record[58:59] = first[0:1]
+    record[59:60] = rest[0:1]
+    record[60:64] = jnp.zeros((4, 128), F32)
+
+
+def owner_of(piece, me):
+    base = me if piece < 4 else me + 1 - 2 * (me & 1)
+    return (base - 2 * (piece % 4) + 8) & 7
+
+
+def halves(first, second):
+    low = lax.broadcasted_iota(jnp.int32, first.shape, 1) < 64
+    return (
+        jnp.where(low, first, pltpu.roll(second, 64, 1)),
+        jnp.where(low, pltpu.roll(first, 64, 1), second),
+    )
+
+
+def survey(
+    ids, records,
+    slots, rows, places, count, seg_old, seg_face, seg_up, seg_store, seg_live, left, right,
+    code_room, codes, sem,
+):
     me = ids[1]
-    blocks = 128
-
-    def source(owner, slot, act):
-        other = lax.rem(owner + me, 2)
-        base = jnp.where(other == 1, me + 1 - 2 * lax.rem(me, 2), me)
-        turn = lax.rem(base - owner + 8, 8) // 2
-        which = other * 4 + turn
+    lane = lax.broadcasted_iota(jnp.int32, (8, 128), 1)
+    places_of = [pl.multiple_of(owner_of(k, me) * 64, 64) for k in range(8)]
+    for k in range(8):
+        code_room[k : k + 1] = records[pl.ds(places_of[k] + 48, 8), :][:1].astype(jnp.int32)
+    copy = pltpu.make_async_copy(code_room, codes, sem)
+    copy.start()
+
+    for side, owner, row in ((left, (me + 7) & 7, 0), (right, (me + 1) & 7, 2)):
+        columns = records[pl.ds(pl.multiple_of(owner * 64, 64) + 56, 8), :]
+        side[0:128] = jnp.broadcast_to(columns[row : row + 1], (128, 128)).T
+        side[128:160] = jnp.broadcast_to(columns[row + 1 : row + 2], (128, 128)).T[:32]
+
+    copy.wait()
+
+    def visit(slot, carry):
+        n, live = carry
         for k in range(8):
-
-            @pl.when(which == k)
-            def _():
-                act(pieces[k].at[slot])
-
-    def visit(b, n):
-        mine = (codes[b] >= 0) & (codes[b] // 32 == me)
-
-        @pl.when(mine)
-        def _():
-            slots[n] = b
-            rows[n] = lax.rem(codes[b], 32)
-            source(
-                b // 16,
-                lax.rem(b, 16),
-                lambda src: pltpu.make_async_copy(src, weights.at[n], sems.at[n]).start(),
-            )
-
-        return n + mine.astype(jnp.int32)
-
-    n = lax.fori_loop(0, blocks, visit, jnp.int32(0))
-    rounds = (n + UNROLL - 1) // UNROLL
-    count[0] = rounds
-
-    def fill(i, carry):
-        slots[i] = -1
-        rows[i] = 0
-        pltpu.make_async_copy(pieces[0].at[0], weights.at[i], sems.at[i]).start()
-        return carry
-
-    lax.fori_loop(n, rounds * UNROLL, fill, 0)
-
-    turned = [record[:, 128 * k : 128 * k + 128].T for k in range(4)]
-    seg_old[...] = turned[0]
-    trans, flags = turned[1][:64], turned[1][64:]
+            code = codes[k, slot]
+            mine = (code >> 5) == me
+            place = (slot & 1) * 64 + 8 * k + (slot >> 1)
+            slots[n] = place
+            rows[n] = code & 31
+            places[n] = 16 * k + slot
+            live = jnp.where(lane == jnp.where(mine, place, -1), 1.0, live)
+            n = n + jnp.where(mine, 1, 0)
+        return n, live
+
+    n, live = lax.fori_loop(0, 16, visit, (jnp.int32(0), jnp.zeros((8, 128), F32)))
+    seg_live[...] = live
+    count[0] = (n + UNROLL - 1) // UNROLL
+    for k in range(UNROLL - 1):
+        slots[n + k] = -1
+        rows[n + k] = 0
+        places[n + k] = 0
+
+    def field(k):
+        return jnp.concatenate([records[pl.ds(p + 8 * k, 8), :] for p in places_of], axis=0)
+
+    def turned(k):
+        both = jnp.concatenate([field(k), field(k + 1)], axis=0).T
+        return halves(both[:64], both[64:])
+
+    seg_old[:64], seg_old[64:] = turned(0)
+    trans, flags = turned(2)
     at = lax.broadcasted_iota(jnp.int32, (64, 128), 0)
     seg_face[:64] = jnp.where(at < 63, trans, 0.0)
     seg_face[64:] = jnp.where(at > 0, pltpu.roll(trans, 1, 0), 0.0)
     upstream = jnp.where(flags == 1.0, 1.0, 0.0)
     seg_up[:64] = upstream
     seg_up[64:] = 1.0 - pltpu.roll(upstream, 1, 0)
-    seg_store[...] = turned[2]
-    code = turned[3][:8]
-    first = (me * 32).astype(F32)
-    seg_live[...] = jnp.where((code >= first) & (code < first + 32.0), 1.0, 0.0)
+    seg_store[:64], seg_store[64:] = turned(4)
+
+
+def collect(places, count, *refs):
+    pieces, weights, sems = refs[:10], refs[10], refs[11]
+    starts = (0, 16, 32, 40, 48, 64, 80, 96, 104, 112, 128)
+
+    def fetch(i, carry):
+        place = places[i]
+        for k in range(10):
+
+            @pl.when((place >= starts[k]) & (place < starts[k + 1]))
+            def _():
+                pltpu.make_async_copy(pieces[k].at[place - starts[k]], weights.at[i], sems.at[i]).start()
+
+        return carry
 
     def settle(i, carry):
         pltpu.make_async_copy(pieces[0].at[0], weights.at[i], sems.at[i]).wait()
         return carry
 
-    lax.fori_loop(0, rounds * UNROLL, settle, 0)
-
-
-def over_blocks(slots, rows, count, weights, lines, q, sums, returned, columns):
+    lax.fori_loop(0, count[0] * UNROLL, fetch, 0)
+    lax.fori_loop(0, count[0] * UNROLL, settle, 0)
+
+
+def survey_blocks(slots, rows, count, weights, lines, q, sums, returned, columns, levels):
     lane = lax.broadcasted_iota(jnp.int32, (64, 128), 1)
     sums[...] = jnp.zeros_like(sums)
     returned[...] = jnp.zeros_like(returned)
-    if columns is not None:
-        columns[...] = jnp.zeros_like(columns)
+    columns[...] = jnp.zeros_like(columns)
 
     def body(step, carry):
         added = [jnp.zeros((64, 128), F32) for _ in range(4)]
@@ -190,26 +268,51 @@
                 total = jnp.sum(weight * line, axis=1, keepdims=True)
                 added[v] = added[v] + jnp.where(here, total, 0.0)
             q_col = jnp.sum(jnp.where(here, q_all, 0.0), axis=1, keepdims=True)
+            levels[i] = jnp.broadcast_to(q_col, (64, 128))
             back = jnp.sum(weight * q_col, axis=0, keepdims=True)
-            col = None
-            if columns is not None:
-                valid = jnp.where(slot >= 0, 1.0, 0.0)
-                col = jnp.sum(weight, axis=0, keepdims=True) * valid
-            backs.append((row, back, col))
+            valid = jnp.where(slot >= 0, 1.0, 0.0)
+            backs.append((row, back, jnp.sum(weight, axis=0, keepdims=True) * valid))
         for v in range(4):
             sums[64 * v : 64 * v + 64] += added[v]
         for row, back, col in backs:
             returned[pl.ds(row, 1), :] += back
-            if columns is not None:
-                columns[pl.ds(row, 1), :] += col
+            columns[pl.ds(row, 1), :] += col
         return carry
 
     lax.fori_loop(0, count[0], body, 0)
 
 
+def couple_blocks(slots, rows, count, weights, levels, lines, dq, inflow, returned):
+    lane = lax.broadcasted_iota(jnp.int32, (64, 128), 1)
+    returned[...] = jnp.zeros_like(returned)
+
+    def body(step, carry):
+        added = [jnp.zeros((64, 128), F32) for _ in range(2)]
+        dq_all = dq[:64]
+        backs = []
+        for k in range(UNROLL):
+            i = step * UNROLL + k
+            slot, row = slots[i], rows[i]
+            weight, level = weights[i], levels[i]
+            here = lane == slot
+            for v in range(2):
+                first = lines[pl.ds(32 * v + row, 1), :]
+                second = lines[pl.ds(64 + 32 * v + row, 1), :]
+                total = jnp.sum(weight * (first - level * second), axis=1, keepdims=True)
+                added[v] = added[v] + jnp.where(here, total, 0.0)
+            dq_col = jnp.sum(jnp.where(here, dq_all, 0.0), axis=1, keepdims=True)
+            backs.append((row, jnp.sum(weight * dq_col, axis=0, keepdims=True)))
+        for v in range(2):
+            inflow[64 * v : 64 * v + 64] += added[v]
+        for row, back in backs:
+            returned[pl.ds(row, 1), :] += back
+        return carry
+
+    lax.fori_loop(0, count[0], body, 0)
+
+
 def combine(dots):
-    total = jnp.sum(dots, axis=1, keepdims=True)
-    total = jnp.broadcast_to(total, (DOTS, 128))
+    total = jnp.broadcast_to(dots, (128, 128)).T
     gram = {}
     for n, (i, j) in enumerate(PAIRS):
         gram[i, j] = gram[j, i] = jnp.broadcast_to(total[n : n + 1, :], (8, 128))
@@ -235,10 +338,7 @@
 
 
 def summed(parts_ref):
-    total = parts_ref[0]
-    for k in range(1, parts_ref.shape[0]):
-        total = total + parts_ref[k]
-    return total
+    return jnp.sum(parts_ref[...], axis=0)
 
 
 def face_terms(pres, satur, pres_across, satur_across, faces, own_up, coef_ref, stride):
@@ -306,13 +406,13 @@
         dir_segs = take(SWEEPS)
         dir_around = [take(4) for _ in range(SWEEPS)]
     base_cell, base_seg, dir_cell, dir_seg = take(4)
-    coef, seg_coef, lead, seg_lead, lines, reach, couple_rows = take(7)
+    coef, seg_coef, lead, seg_lead, lines, reach, couple_rows, levels = take(8)
     if newton:
         cell_out, seg_out = take(2)
     inner_lines, sums, returned, columns = refs
 
     cell = cell_in[...]
-    near = [r[...] for r in around]
+    near = [r[0:64] for r in around]
     if newton:
         factors = combine(summed(parts))
         for j in range(SWEEPS):
@@ -342,7 +442,7 @@
     inner_lines[32:64] = water
     inner_lines[64:96] = total * pres
     inner_lines[96:128] = water * pres
-    over_blocks(slots, rows, count, weights, inner_lines, seg_ref, sums, returned, columns)
+    survey_blocks(slots, rows, count, weights, inner_lines, seg_ref, sums, returned, columns, levels)
     reach[...] = sums[0:128]
     column = columns[...]
     pull = pres * column - returned[...]
@@ -392,7 +492,7 @@
 
 
 def couple_dirs(
-    slots, rows, count, dir_cell, dir_seg, seg, lines, reach, weights, inflow, returned, inner_lines, sums
+    slots, rows, count, dir_cell, dir_seg, lines, reach, weights, levels, inflow, returned, inner_lines
 ):
     dp, ds = dir_cell[:32], dir_cell[32:]
     pres = lines[128:160]
@@ -402,10 +502,10 @@
     inner_lines[32:64] = lines[32:64] * dp + lean_w * pres
     inner_lines[64:96] = lean_t
     inner_lines[96:128] = lean_w
-    over_blocks(slots, rows, count, weights, inner_lines, dir_seg, sums, returned, None)
-    q, dq = seg[:64], dir_seg[:64]
-    inflow[0:64] = sums[0:64] - q * sums[128:192] - dq * reach[0:64]
-    inflow[64:128] = sums[64:128] - q * sums[192:256] - dq * reach[64:128]
+    dq = dir_seg[:64]
+    inflow[0:64] = -dq * reach[0:64]
+    inflow[64:128] = -dq * reach[64:128]
+    couple_blocks(slots, rows, count, weights, levels, inner_lines, dir_seg, inflow, returned)
 
 
 def advance(last, *refs):
@@ -475,23 +575,16 @@
     for i, j in PAIRS:
         part = jnp.sum(cells[i][...] * cells[j][...], axis=0, keepdims=True)
         lines.append(part + jnp.sum(segs[i][...] * segs[j][...], axis=0, keepdims=True))
-    lines.append(jnp.zeros((DOTS - len(PAIRS), 128), F32))
-    total = jnp.concatenate(lines, axis=0)
-    for k in range(out.shape[0]):
-        out[k] = total
-
-
-def add_parts(parts, out):
-    total = summed(parts)
-    for k in range(out.shape[0]):
-        out[k] = total
+    lines.append(jnp.zeros((128 - len(PAIRS), 128), F32))
+    total = jnp.sum(jnp.concatenate(lines, axis=0).T, axis=0, keepdims=True)
+    out[...] = jnp.broadcast_to(total[None], out.shape)
 
 
 def finish(*refs):
-    parts, cell, seg, seg_old = refs[:4]
-    dir_cells = refs[4 : 4 + SWEEPS]
-    dir_segs = refs[4 + SWEEPS : 4 + 2 * SWEEPS]
-    cell_out, moved = refs[4 + 2 * SWEEPS :]
+    ids, parts, cell, seg, seg_old = refs[:5]
+    dir_cells = refs[5 : 5 + SWEEPS]
+    dir_segs = refs[5 + SWEEPS : 5 + 2 * SWEEPS]
+    cell_out, moved = refs[5 + 2 * SWEEPS :]
     factors = combine(summed(parts))
     total = cell[...]
     shift = seg[...] - seg_old[...]
@@ -499,7 +592,12 @@
         total = total + spread(factors[j], 64) * dir_cells[j][...]
         shift = shift + spread(factors[j], 128) * dir_segs[j][...]
     cell_out[...] = total
-    moved[...] = shift.T
+    turned = jnp.concatenate(halves(shift[:64], shift[64:]), axis=0).T
+    me = ids[1]
+    for k in range(8):
+        owner = owner_of(k, me)
+        moved[owner, 0:8] = turned[8 * k : 8 * k + 8]
+        moved[owner, 8:16] = turned[64 + 8 * k : 64 + 8 * k + 8]
 
 
 def ring(block, axis, distance):
@@ -512,22 +610,12 @@
 
 
 def exchanged(block):
-    return [
-        ring(block, "region", 1),
-        ring(block, "region", -1),
-        ring(block, "frac", 1),
-        ring(block, "frac", -1),
-    ]
-
-
-def reduced(parts):
-    y_groups = [[4 * z + y for y in range(4)] for z in range(8)]
-    z_groups = [[4 * z + y for z in range(8)] for y in range(4)]
-    parts = lax.all_to_all(parts, "frac", 0, 0)
-    [parts] = call(add_parts, [vmem(4, DOTS, 128)], [parts], "v")
-    parts = lax.all_to_all(parts, "region", 0, 0, axis_index_groups=y_groups)
-    [parts] = call(add_parts, [vmem(8, DOTS, 128)], [parts], "v")
-    return lax.all_to_all(parts, "region", 0, 0, axis_index_groups=z_groups)
+    left, right = ring(block, "frac", 1), ring(block, "frac", -1)
+    return [ring(block, "region", 1), ring(block, "region", -1), left, right]
+
+
+def after(first, *others):
+    return lax.optimization_barrier((first, *others))
 
 
 def on_device(
@@ -556,50 +644,48 @@
             jnp.int32(lax.axis_size("frac")),
         ]
     ).astype(jnp.int32)
-    cell_old = jnp.concatenate([pres_old[0], satur_old[0]], axis=0)
-    message = jnp.concatenate(
+    one_right = ring(coupling, "frac", 2)
+    one_left = ring(coupling, "frac", -2)
+    ids, message, record, cell_old, flag_y = call(
+        pack,
+        [smem_i32(4), vmem(160, 128), vmem(64, 128), vmem(64, 128), vmem(32, 128)],
         [
-            cell_old,
-            permeability[0],
-            face_upwind[0, 0].astype(F32),
-            face_upwind[2, 0].astype(F32),
+            ids,
+            target_part,
+            target_row,
+            live_count,
+            pres_old,
+            satur_old,
+            permeability,
+            face_upwind,
+            frac_pres_old.reshape(8, 128),
+            frac_satur_old.reshape(8, 128),
+            frac_trans.reshape(8, 128),
+            frac_upwind.reshape(8, 128),
+            frac_storage,
         ],
-        axis=0,
-    )
-    live = jnp.arange(blocks, dtype=jnp.int32) < live_count[0]
-    code = jnp.where(live, target_part * 32 + target_row, -1)
-    record = jnp.concatenate(
+        "ssss" + "H" * 9,
+        out_spaces="svvvv",
+        scratch=[
+            pltpu.VMEM((3, 1, 32, 128), jnp.int32),
+            pltpu.VMEM((8, 128), jnp.int32),
+            pltpu.VMEM((2, 1024), F32),
+            pltpu.SemaphoreType.DMA((9,)),
+        ],
+        name="pack",
+    )
+    records = lax.all_gather(record, "frac", axis=0, tiled=True)
+    one_right, one_left, records = after(one_right, one_left, records)
+    below, above = ring(message, "region", 1), ring(message, "region", -1)
+    half = blocks // 2
+    two = [ring(one_right[:half], "frac", 2), ring(one_left[half:], "frac", -2)]
+    same = [coupling, one_right, *two, one_left]
+    pieces = same + [swapped(x, "frac") for x in same]
+    room = 8 * blocks + UNROLL
+    slots, rows, places, count, seg_old, seg_face, seg_up, seg_store, seg_live, left, right = call(
+        survey,
         [
-            x.reshape(blocks, 64)
-            for x in (
-                frac_pres_old,
-                frac_satur_old,
-                frac_trans,
-                frac_upwind.astype(F32),
-                frac_storage[0],
-                frac_storage[1],
-            )
-        ]
-        + [jnp.broadcast_to(code.astype(F32)[:, None], (blocks, 128))],
-        axis=1,
-    )
-    around = exchanged(message)
-    same = [coupling] + [ring(coupling, "frac", 2 * k) for k in (1, 2, 3)]
-    pieces = same + [swapped(x, "frac") for x in same]
-    record_all = lax.all_gather(record, "frac", axis=0, tiled=True)
-    codes = record_all[:, 384].astype(jnp.int32)
-
-    faces, own_up = call(
-        geometry,
-        [vmem(192, 128), vmem(192, 128)],
-        [ids, message, *around, face_upwind[1, 0]],
-        "svvvvvv",
-    )
-    room = 8 * blocks + UNROLL
-    weights, slots, rows, count, seg_old, seg_face, seg_up, seg_store, seg_live = call(
-        collect,
-        [
-            vmem(room, 64, 128),
+            smem_i32(room),
             smem_i32(room),
             smem_i32(room),
             smem_i32(1),
@@ -608,19 +694,43 @@
             vmem(128, 128),
             vmem(128, 128),
             vmem(8, 128),
+            vmem(160, 128),
+            vmem(160, 128),
         ],
-        [ids, codes, *pieces, record_all],
-        "ss" + "a" * 8 + "v",
+        [ids, records],
+        "Sv",
+        out_spaces="ssss" + "v" * 7,
+        scratch=[
+            pltpu.VMEM((8, 128), jnp.int32),
+            pltpu.SMEM((8, 128), jnp.int32),
+            pltpu.SemaphoreType.DMA,
+        ],
+        name="survey",
+    )
+    around = [below, above, left, right]
+    faces, own_up = call(
+        geometry,
+        [vmem(192, 128), vmem(192, 128)],
+        [ids, message, *around, flag_y],
+        "Svvvvvv",
+        name="geometry",
+    )
+    [weights] = call(
+        collect,
+        [vmem(room, 64, 128)],
+        [places, count, *pieces],
+        "SS" + "a" * 10,
         scratch=[pltpu.SemaphoreType.DMA((room,))],
-        out_spaces="vsss" + "v" * 5,
+        name="collect",
     )
     lists = [slots, rows, count]
     store = storage.reshape(64, 128)
     wells = source.reshape(64, 128)
     inner = [vmem(128, 128), vmem(256, 128)]
+    devices = lax.axis_size("region") * lax.axis_size("frac")
 
     cell, seg = cell_old, seg_old
-    near = [x[:64] for x in around]
+    near = around
     parts = None
     for newton in range(NEWTON):
         args = [
@@ -652,6 +762,7 @@
             vmem(160, 128),
             vmem(128, 128),
             vmem(64, 128),
+            vmem(room, 64, 128),
         ]
         if newton:
             args += [parts, *dir_cells, *dir_segs, *[x for group in dir_around for x in group]]
@@ -660,14 +771,14 @@
             lambda *refs, newton=newton: linearise(newton, *refs),
             outs,
             args,
-            "sss" + "v" * (len(args) - 3),
+            "SSS" + "v" * (len(args) - 3),
             scratch=[*inner, vmem(32, 128), vmem(32, 128)],
             name="linearise",
         )
         base_cell, base_seg, dir_cell, dir_seg = made[:4]
-        coef, seg_coef, lead, seg_lead, lines, reach, couple_rows = made[4:11]
+        coef, seg_coef, lead, seg_lead, lines, reach, couple_rows, levels = made[4:12]
         if newton:
-            cell, seg = made[11:]
+            cell, seg = made[12:]
         base_cells, base_segs = [base_cell], [base_seg]
         dir_cells, dir_segs, dir_around = [], [], []
         for sweep in range(SWEEPS):
@@ -676,9 +787,9 @@
             inflow, returned = call(
                 couple_dirs,
                 [vmem(128, 128), vmem(32, 128)],
-                [*lists, dir_cell, dir_seg, seg, lines, reach, weights],
-                "sss" + "v" * 6,
-                scratch=inner,
+                [*lists, dir_cell, dir_seg, lines, reach, weights, levels],
+                "SSS" + "v" * 6,
+                scratch=inner[:1],
                 name="couple",
             )
             dir_cells.append(dir_cell)
@@ -715,29 +826,23 @@
                 dir_cell, dir_seg = made[2:]
         [parts] = call(
             inner_products,
-            [vmem(8, DOTS, 128)],
+            [vmem(devices, 1, 128)],
             [*base_cells, *base_segs],
             "v" * (2 * SWEEPS + 2),
             name="inner_products",
         )
-        parts = reduced(parts)
-
-    args = [parts, cell, seg, seg_old, *dir_cells, *dir_segs]
+        parts = lax.all_to_all(parts, ("region", "frac"), 0, 0)
+
+    args = [ids, parts, cell, seg, seg_old, *dir_cells, *dir_segs]
     cell_state, moved = call(
         finish,
-        [jax.ShapeDtypeStruct((64, 128), F32), vmem(128, 128)],
+        [jax.ShapeDtypeStruct((64, 128), F32), vmem(8, 16, 128)],
         args,
-        "v" * len(args),
+        "S" + "v" * (len(args) - 1),
         name="finish",
     )
-    moved = lax.all_to_all(moved.reshape(8, blocks, 128), "frac", 0, 0)
-    moved = jnp.sum(moved, axis=0)
-    seg_state = jnp.stack(
-        [
-            frac_pres_old + moved[:, :64].reshape(-1),
-            frac_satur_old + moved[:, 64:].reshape(-1),
-        ]
-    )
+    moved = jnp.sum(lax.all_to_all(moved, "frac", 0, 0), axis=0)
+    seg_state = jnp.stack([frac_pres_old, frac_satur_old]) + moved.reshape(2, -1)
     return (cell_state.reshape(2, 1, 32, 128), seg_state)
 
 

time: 248 us -> 194 us (0.78)
  starting transfers between devices: 98.3 us -> 58 us
  waiting for transfers between devices: 15.7 us -> 47.9 us
  blocking collectives: 82.5 us -> 63.3 us
  Pallas kernels: 37.5 us -> 20 us
  local copies, waits for them, and re-layouts: 7.58 us -> 2.42 us
  other arithmetic: 4.36 us -> 0.7 us
    ppermute x47 -> x46, starting transfers between devices: 95 us -> 54 us  [ring(): lax.ppermute(block, axis, [(i, (i + distance) % count) for i in range(cou...]
    ppermute x47 -> x46, waiting for transfers between devices: 15.7 us -> 47.9 us  [ring(): lax.ppermute(block, axis, [(i, (i + distance) % count) for i in range(cou...]
    all_to_all x7 -> x3, blocking collectives: 69.4 us -> 50.1 us  [the longest x2 42.2 us: on_device(): parts = lax.all_to_all(parts, ('region', 'frac'), 0, 0)]
    pallas_call x31 -> x29, Pallas kernels: 37.5 us -> 20 us  [call(): pl.pallas_call(body, out_shape=list(outs), in_specs=[pl.BlockSpec(memory_...]
  transfers between devices with their start and end apart: 51 -> 51, of which waited for: 7 -> 22; matrix products, arithmetic and copies ran while one was open for 4% -> 0% of each run, Pallas kernels for 9% -> 6%
where the time goes in v2:
time: 194 us
  blocking collectives  63.3 us (33%)
  starting transfers between devices  58 us (30%)
  waiting for transfers between devices  47.9 us (25%)
  Pallas kernels  20 us (10%)
  local copies, waits for them, and re-layouts  2.42 us (1%)
    ppermute x46, starting transfers between devices, ring(): lax.ppermute(block, axis, [(i, (i + distance) % count) for i in range(cou...  54 us
    ppermute x46, waiting for transfers between devices, ring(): lax.ppermute(block, axis, [(i, (i + distance) % count) for i in range(cou...  47.9 us
    all_to_all x2, blocking collectives, on_device(): parts = lax.all_to_all(parts, ('region', 'frac'), 0, 0)  42.2 us
    pallas_call x29, Pallas kernels, call(): pl.pallas_call(body, out_shape=list(outs), in_specs=[pl.BlockSpec(memory_...  20 us
    all_gather x1, blocking collectives, on_device(): records = lax.all_gather(record, 'frac', axis=0, tiled=True)  13.2 us
    all_to_all x1, blocking collectives, on_device(): moved = jnp.sum(lax.all_to_all(moved, 'frac', 0, 0), axis=0)  7.93 us
    ppermute x5, starting transfers between devices, swapped(): lax.ppermute(block, axis, [(i, i ^ 1) for i in range(lax.axis_size(axis))])  4.04 us
  transfers between devices with their start and end apart: 51, of which 22 were waited for; matrix products, arithmetic and copies ran while one was open for 0% of the time, Pallas kernels for 6%

profile of v2, /device:TPU:1, one launch (start us, length us, event | category | flops | bytes accessed | tf_op | source)
XLA Modules:
  0.0 194.2 jit_solution(10362032106730559258)
XLA Ops:
  0.6 3.4 %collective-permute-start.1 = (f32[16,64,128]{2,1,0:T(8,128)}, f32[16,64,128]{2,1,0:T(8,128)S(1)}, u32[]{:S(2)}, u32[]{:S(2)}) collective-permute-start(f32[16,64,128]{2,1,0:T(8,128)} %refs_0_.1), channel_id=1, source_target_pairs={{0,6},{1,7},{2,0},{3,1},{4,2},{5,3},{6,4},{7,5},{8,14},{9,15},{10,... | collective-permute-start | bytes 1572872 | tf_op jit(solution)/shard_map/ppermute | solution.py:605
  6.1 1.6 pack.1
  7.7 8.1 %collective-permute-start.3 = (f32[160,128]{1,0:T(8,128)S(1)}, f32[160,128]{1,0:T(8,128)S(1)}, u32[]{:S(2)}, u32[]{:S(2)}) collective-permute-start(f32[160,128]{1,0:T(8,128)S(1)} %get-tuple-element.114.own), channel_id=1, source_target_pairs={{0,248},{8,0},{16,8},{24,16},{32,24},{40,32},{48,40},{56,48},{64,5... | collective-permute-start | bytes 245768 | tf_op jit(solution)/shard_map/ppermute | solution.py:605
  15.8 1.2 collective-permute-start.6
  17.0 13.2 %all_gather.3.records = f32[512,128]{1,0:T(8,128)S(1)} all-gather(f32[64,128]{1,0:T(8,128)S(1)} %get-tuple-element.108), channel_id=1, replica_groups=mesh['region'=32,'frac'=8] {'frac'}, dimensions={0}, use_global_device_ids=true | all-gather | bytes 294912 | tf_op jit(solution)/shard_map/all_gather | solution.py:677
  30.2 2.5 %collective-permute-start.5 = (f32[8,64,128]{2,1,0:T(8,128)S(1)}, f32[8,64,128]{2,1,0:T(8,128)S(1)}, u32[]{:S(2)}, u32[]{:S(2)}) collective-permute-start(f32[8,64,128]{2,1,0:T(8,128)S(1)} %slice.7), channel_id=1, source_target_pairs={{0,6},{1,7},{2,0},{3,1},{4,2},{5,3},{6,4},{7,5},{8,14},{9,15},{10,... | collective-permute-start | bytes 786440 | tf_op jit(solution)/shard_map/ppermute | solution.py:605
  33.3 5.0 %collective-permute-done.5.refs_3_ = f32[8,64,128]{2,1,0:T(8,128)S(1)} collective-permute-done((f32[8,64,128]{2,1,0:T(8,128)S(1)}, f32[8,64,128]{2,1,0:T(8,128)S(1)}, u32[]{:S(2)}, u32[]{:S(2)}) %collective-permute-start.5) | collective-permute-done | bytes 262176 | tf_op jit(solution)/shard_map/ppermute | solution.py:605
  39.3 2.1 %collective-permute-done.4.refs_2_ = f32[8,64,128]{2,1,0:T(8,128)S(1)} collective-permute-done((f32[8,64,128]{2,1,0:T(8,128)S(1)}, f32[8,64,128]{2,1,0:T(8,128)S(1)}, u32[]{:S(2)}, u32[]{:S(2)}) %collective-permute-start.4) | collective-permute-done | bytes 262176 | tf_op jit(solution)/shard_map/ppermute | solution.py:605
  41.4 1.3 collective-permute-start.8
  42.7 1.6 survey.1
  44.5 1.0 copy-done.1
  45.5 2.9 %collect.1.refs_13_.weights = f32[132,64,128]{2,1,0:T(8,128)S(1)} custom-call(s32[132]{0:T(256)S(4)} %get-tuple-element.125.places, s32[1]{0:T(128)S(4)} %get-tuple-element.112.count.refs_2_, f32[16,64,128]{2,1,0:T(8,128)S(1)} %copy-done.1, f32[16,64,128]{2,1,0:T(8,128)S(1)} %collective-permute-done.refs_1_, ...), custom_call_target="tpu_custom_call" | custom-call | flops 20000 | bytes 20000 | tf_op jit(solution)/shard_map/collect/pallas_call | solution.py:39
  48.5 1.2 linearise.2
  50.4 1.0 collective-permute-start.13
  51.5 4.4 %collective-permute-start.12 = (f32[64,128]{1,0:T(8,128)S(1)}, f32[64,128]{1,0:T(8,128)S(1)}, u32[]{:S(2)}, u32[]{:S(2)}) collective-permute-start(f32[64,128]{1,0:T(8,128)S(1)} %get-tuple-element.129.dir_cell.refs_0_.refs_21_), channel_id=1, source_target_pairs={{0,248},{8,0},{16,8},{24,16},{32,24},{40,32},{48,40},{56,48},{64,5... | collective-permute-start | bytes 98312 | tf_op jit(solution)/shard_map/ppermute | solution.py:605
  56.9 5.1 %collective-permute-done.11.refs_1_.refs_31_ = f32[64,128]{1,0:T(8,128)S(1)} collective-permute-done((f32[64,128]{1,0:T(8,128)S(1)}, f32[64,128]{1,0:T(8,128)S(1)}, u32[]{:S(2)}, u32[]{:S(2)}) %collective-permute-start.11) | collective-permute-done | bytes 32800 | tf_op jit(solution)/shard_map/ppermute | solution.py:605
  62.3 1.5 collective-permute-start.17
  63.8 1.5 collective-permute-start.15
  66.6 3.3 %collective-permute-done.15.refs_1_.refs_35_ = f32[64,128]{1,0:T(8,128)S(1)} collective-permute-done((f32[64,128]{1,0:T(8,128)S(1)}, f32[64,128]{1,0:T(8,128)S(1)}, u32[]{:S(2)}, u32[]{:S(2)}) %collective-permute-start.15) | collective-permute-done | bytes 32800 | tf_op jit(solution)/shard_map/ppermute | solution.py:605
  70.1 1.8 collective-permute-start.22
  71.9 1.5 collective-permute-start.19
  74.6 3.3 %collective-permute-done.19.refs_1_.refs_39_ = f32[64,128]{1,0:T(8,128)S(1)} collective-permute-done((f32[64,128]{1,0:T(8,128)S(1)}, f32[64,128]{1,0:T(8,128)S(1)}, u32[]{:S(2)}, u32[]{:S(2)}) %collective-permute-start.19) | collective-permute-done | bytes 32800 | tf_op jit(solution)/shard_map/ppermute | solution.py:605
  78.1 3.0 %collective-permute-start.26 = (f32[64,128]{1,0:T(8,128)S(1)}, f32[64,128]{1,0:T(8,128)S(1)}, u32[]{:S(2)}, u32[]{:S(2)}) collective-permute-start(f32[64,128]{1,0:T(8,128)S(1)} %get-tuple-element.152.dir_cell.refs_0_.refs_24_), channel_id=1, source_target_pairs={{0,7},{1,0},{2,1},{3,2},{4,3},{5,4},{6,5},{7,6},{8,15},{9,8},{10,9... | collective-permute-start | bytes 98312 | tf_op jit(solution)/shard_map/ppermute | solution.py:605
  81.0 1.5 collective-permute-start.23
  83.8 3.3 %collective-permute-done.23.refs_1_.refs_43_ = f32[64,128]{1,0:T(8,128)S(1)} collective-permute-done((f32[64,128]{1,0:T(8,128)S(1)}, f32[64,128]{1,0:T(8,128)S(1)}, u32[]{:S(2)}, u32[]{:S(2)}) %collective-permute-start.23) | collective-permute-done | bytes 32800 | tf_op jit(solution)/shard_map/ppermute | solution.py:605
  87.3 3.0 %collective-permute-start.30 = (f32[64,128]{1,0:T(8,128)S(1)}, f32[64,128]{1,0:T(8,128)S(1)}, u32[]{:S(2)}, u32[]{:S(2)}) collective-permute-start(f32[64,128]{1,0:T(8,128)S(1)} %get-tuple-element.157.dir_cell.refs_0_.refs_25_), channel_id=1, source_target_pairs={{0,7},{1,0},{2,1},{3,2},{4,3},{5,4},{6,5},{7,6},{8,15},{9,8},{10,9... | collective-permute-start | bytes 98312 | tf_op jit(solution)/shard_map/ppermute | solution.py:605
  90.2 1.5 collective-permute-start.27
  93.0 3.3 %collective-permute-done.27.refs_1_.refs_47_ = f32[64,128]{1,0:T(8,128)S(1)} collective-permute-done((f32[64,128]{1,0:T(8,128)S(1)}, f32[64,128]{1,0:T(8,128)S(1)}, u32[]{:S(2)}, u32[]{:S(2)}) %collective-permute-start.27) | collective-permute-done | bytes 32800 | tf_op jit(solution)/shard_map/ppermute | solution.py:605
  96.8 20.8 %all_to_all.15.refs_20_ = f32[256,1,128]{2,1,0:T(1,128)S(1)} all-to-all(f32[256,1,128]{2,1,0:T(1,128)S(1)} %inner_products.2), channel_id=1, replica_groups=mesh['region'=32,'frac'=8] {'region','frac'}, dimensions={0} | all-to-all | bytes 262144 | tf_op jit(solution)/shard_map/all_to_all | solution.py:834
  117.6 1.8 linearise.3
  120.1 1.0 collective-permute-start.33
  123.4 1.1 collective-permute-done.32.refs_2_
  124.5 3.7 %collective-permute-done.31.refs_1_ = f32[64,128]{1,0:T(8,128)S(1)} collective-permute-done((f32[64,128]{1,0:T(8,128)S(1)}, f32[64,128]{1,0:T(8,128)S(1)}, u32[]{:S(2)}, u32[]{:S(2)}) %collective-permute-start.31) | collective-permute-done | bytes 32800 | tf_op jit(solution)/shard_map/ppermute | solution.py:605
  128.9 1.1 collective-permute-start.37
  130.2 1.4 collective-permute-start.35
  132.8 3.4 %collective-permute-done.35.refs_1_ = f32[64,128]{1,0:T(8,128)S(1)} collective-permute-done((f32[64,128]{1,0:T(8,128)S(1)}, f32[64,128]{1,0:T(8,128)S(1)}, u32[]{:S(2)}, u32[]{:S(2)}) %collective-permute-start.35) | collective-permute-done | bytes 32800 | tf_op jit(solution)/shard_map/ppermute | solution.py:605
  136.4 1.6 collective-permute-start.42
  138.2 1.5 collective-permute-start.39
  140.9 3.3 %collective-permute-done.39.refs_1_ = f32[64,128]{1,0:T(8,128)S(1)} collective-permute-done((f32[64,128]{1,0:T(8,128)S(1)}, f32[64,128]{1,0:T(8,128)S(1)}, u32[]{:S(2)}, u32[]{:S(2)}) %collective-permute-start.39) | collective-permute-done | bytes 32800 | tf_op jit(solution)/shard_map/ppermute | solution.py:605
  144.4 2.9 %collective-permute-start.46 = (f32[64,128]{1,0:T(8,128)S(1)}, f32[64,128]{1,0:T(8,128)S(1)}, u32[]{:S(2)}, u32[]{:S(2)}) collective-permute-start(f32[64,128]{1,0:T(8,128)S(1)} %get-tuple-element.192.dir_cell.refs_0_.refs_8_), channel_id=1, source_target_pairs={{0,7},{1,0},{2,1},{3,2},{4,3},{5,4},{6,5},{7,6},{8,15},{9,8},{10,9... | collective-permute-start | bytes 98312 | tf_op jit(solution)/shard_map/ppermute | solution.py:605
  147.3 1.5 collective-permute-start.43
  150.1 3.3 %collective-permute-done.43.refs_1_ = f32[64,128]{1,0:T(8,128)S(1)} collective-permute-done((f32[64,128]{1,0:T(8,128)S(1)}, f32[64,128]{1,0:T(8,128)S(1)}, u32[]{:S(2)}, u32[]{:S(2)}) %collective-permute-start.43) | collective-permute-done | bytes 32800 | tf_op jit(solution)/shard_map/ppermute | solution.py:605
  153.5 3.0 %collective-permute-start.50 = (f32[64,128]{1,0:T(8,128)S(1)}, f32[64,128]{1,0:T(8,128)S(1)}, u32[]{:S(2)}, u32[]{:S(2)}) collective-permute-start(f32[64,128]{1,0:T(8,128)S(1)} %get-tuple-element.197.dir_cell.refs_0_.refs_9_), channel_id=1, source_target_pairs={{0,7},{1,0},{2,1},{3,2},{4,3},{5,4},{6,5},{7,6},{8,15},{9,8},{10,9... | collective-permute-start | bytes 98312 | tf_op jit(solution)/shard_map/ppermute | solution.py:605
  156.5 1.5 collective-permute-start.47
  159.2 3.3 %collective-permute-done.47.refs_1_ = f32[64,128]{1,0:T(8,128)S(1)} collective-permute-done((f32[64,128]{1,0:T(8,128)S(1)}, f32[64,128]{1,0:T(8,128)S(1)}, u32[]{:S(2)}, u32[]{:S(2)}) %collective-permute-start.47) | collective-permute-done | bytes 32800 | tf_op jit(solution)/shard_map/ppermute | solution.py:605
  163.1 21.4 %all_to_all.16.refs_1_ = f32[256,1,128]{2,1,0:T(1,128)S(1)} all-to-all(f32[256,1,128]{2,1,0:T(1,128)S(1)} %inner_products.3), channel_id=1, replica_groups=mesh['region'=32,'frac'=8] {'region','frac'}, dimensions={0} | all-to-all | bytes 262144 | tf_op jit(solution)/shard_map/all_to_all | solution.py:834
  184.5 1.1 finish.1
  185.6 7.9 %all_to_all.17 = f32[8,16,128]{2,1,0:T(8,128)S(1)} all-to-all(f32[8,16,128]{2,1,0:T(8,128)S(1)} %get-tuple-element.211), channel_id=1, replica_groups=mesh['region'=32,'frac'=8] {'frac'}, dimensions={0} | all-to-all | bytes 131072 | tf_op jit(solution)/shard_map/all_to_all | solution.py:844
  (107 shorter events, 21.7 us)
Async XLA Ops:
  0.6 29.5 %collective-permute-start.1 = (f32[16,64,128]{2,1,0:T(8,128)}, f32[16,64,128]{2,1,0:T(8,128)S(1)}, u32[]{:S(2)}, u32[]{:S(2)}) collective-permute-start(f32[16,64,128]{2,1,0:T(8,128)} %refs_0_.1), channel_id=1, source_target_pairs={{0,6},{1,7},{2,0},{3,1},{4,2},{5,3},{6,4},{7,5},{8,14},{9,15},{10,... | collective-permute-start | bytes 1572872 | tf_op jit(solution)/shard_map/ppermute | solution.py:605
  4.0 26.2 %collective-permute-start = (f32[16,64,128]{2,1,0:T(8,128)}, f32[16,64,128]{2,1,0:T(8,128)S(1)}, u32[]{:S(2)}, u32[]{:S(2)}) collective-permute-start(f32[16,64,128]{2,1,0:T(8,128)} %refs_0_.1), channel_id=1, source_target_pairs={{0,2},{1,3},{2,4},{3,5},{4,6},{5,7},{6,0},{7,1},{8,10},{9,11},{10,... | collective-permute-start | bytes 1572872 | tf_op jit(solution)/shard_map/ppermute | solution.py:605
  7.7 25.1 %collective-permute-start.3 = (f32[160,128]{1,0:T(8,128)S(1)}, f32[160,128]{1,0:T(8,128)S(1)}, u32[]{:S(2)}, u32[]{:S(2)}) collective-permute-start(f32[160,128]{1,0:T(8,128)S(1)} %get-tuple-element.114.own), channel_id=1, source_target_pairs={{0,248},{8,0},{16,8},{24,16},{32,24},{40,32},{48,40},{56,48},{64,5... | collective-permute-start | bytes 245768 | tf_op jit(solution)/shard_map/ppermute | solution.py:605
  15.8 17.4 %collective-permute-start.2 = (f32[160,128]{1,0:T(8,128)S(1)}, f32[160,128]{1,0:T(8,128)S(1)}, u32[]{:S(2)}, u32[]{:S(2)}) collective-permute-start(f32[160,128]{1,0:T(8,128)S(1)} %get-tuple-element.114.own), channel_id=1, source_target_pairs={{0,8},{8,16},{16,24},{24,32},{32,40},{40,48},{48,56},{56,64},{64,7... | collective-permute-start | bytes 245768 | tf_op jit(solution)/shard_map/ppermute | solution.py:605
  15.8 28.7 %collective-permute-start.6 = (f32[16,64,128]{2,1,0:T(8,128)}, f32[16,64,128]{2,1,0:T(8,128)S(1)}, u32[]{:S(2)}, u32[]{:S(2)}) collective-permute-start(f32[16,64,128]{2,1,0:T(8,128)} %refs_0_.1), channel_id=1, source_target_pairs={{0,1},{1,0},{2,3},{3,2},{4,5},{5,4},{6,7},{7,6},{8,9},{9,8},{10,11... | collective-permute-start | bytes 1572872 | tf_op jit(solution)/shard_map/ppermute | solution.py:609
  30.2 8.1 %collective-permute-start.5 = (f32[8,64,128]{2,1,0:T(8,128)S(1)}, f32[8,64,128]{2,1,0:T(8,128)S(1)}, u32[]{:S(2)}, u32[]{:S(2)}) collective-permute-start(f32[8,64,128]{2,1,0:T(8,128)S(1)} %slice.7), channel_id=1, source_target_pairs={{0,6},{1,7},{2,0},{3,1},{4,2},{5,3},{6,4},{7,5},{8,14},{9,15},{10,... | collective-permute-start | bytes 786440 | tf_op jit(solution)/shard_map/ppermute | solution.py:605
  32.7 8.6 %collective-permute-start.4 = (f32[8,64,128]{2,1,0:T(8,128)S(1)}, f32[8,64,128]{2,1,0:T(8,128)S(1)}, u32[]{:S(2)}, u32[]{:S(2)}) collective-permute-start(f32[8,64,128]{2,1,0:T(8,128)S(1)} %slice.6), channel_id=1, source_target_pairs={{0,2},{1,3},{2,4},{3,5},{4,6},{5,7},{6,0},{7,1},{8,10},{9,11},{10,... | collective-permute-start | bytes 786440 | tf_op jit(solution)/shard_map/ppermute | solution.py:605
  32.8 11.7 %collective-permute-start.7 = (f32[16,64,128]{2,1,0:T(8,128)S(1)}, f32[16,64,128]{2,1,0:T(8,128)S(1)}, u32[]{:S(2)}, u32[]{:S(2)}) collective-permute-start(f32[16,64,128]{2,1,0:T(8,128)S(1)} %collective-permute-done.refs_1_), channel_id=1, source_target_pairs={{0,1},{1,0},{2,3},{3,2},{4,5},{5,4},{6,7},{7,6},{8,9},{9,8},{10,11... | collective-permute-start | bytes 1572872 | tf_op jit(solution)/shard_map/ppermute | solution.py:609
  33.2 11.3 %collective-permute-start.10 = (f32[16,64,128]{2,1,0:T(8,128)S(1)}, f32[16,64,128]{2,1,0:T(8,128)S(1)}, u32[]{:S(2)}, u32[]{:S(2)}) collective-permute-start(f32[16,64,128]{2,1,0:T(8,128)S(1)} %collective-permute-done.1.refs_4_), channel_id=1, source_target_pairs={{0,1},{1,0},{2,3},{3,2},{4,5},{5,4},{6,7},{7,6},{8,9},{9,8},{10,11... | collective-permute-start | bytes 1572872 | tf_op jit(solution)/shard_map/ppermute | solution.py:609
  38.3 6.1 %collective-permute-start.9 = (f32[8,64,128]{2,1,0:T(8,128)S(1)}, f32[8,64,128]{2,1,0:T(8,128)S(1)}, u32[]{:S(2)}, u32[]{:S(2)}) collective-permute-start(f32[8,64,128]{2,1,0:T(8,128)S(1)} %collective-permute-done.5.refs_3_), channel_id=1, source_target_pairs={{0,1},{1,0},{2,3},{3,2},{4,5},{5,4},{6,7},{7,6},{8,9},{9,8},{10,11... | collective-permute-start | bytes 786440 | tf_op jit(solution)/shard_map/ppermute | solution.py:609
  41.4 3.1 %collective-permute-start.8 = (f32[8,64,128]{2,1,0:T(8,128)S(1)}, f32[8,64,128]{2,1,0:T(8,128)S(1)}, u32[]{:S(2)}, u32[]{:S(2)}) collective-permute-start(f32[8,64,128]{2,1,0:T(8,128)S(1)} %collective-permute-done.4.refs_2_), channel_id=1, source_target_pairs={{0,1},{1,0},{2,3},{3,2},{4,5},{5,4},{6,7},{7,6},{8,9},{9,8},{10,11... | collective-permute-start | bytes 786440 | tf_op jit(solution)/shard_map/ppermute | solution.py:609
  49.7 6.9 %collective-permute-start.14 = (f32[64,128]{1,0:T(8,128)S(1)}, f32[64,128]{1,0:T(8,128)S(1)}, u32[]{:S(2)}, u32[]{:S(2)}) collective-permute-start(f32[64,128]{1,0:T(8,128)S(1)} %get-tuple-element.129.dir_cell.refs_0_.refs_21_), channel_id=1, source_target_pairs={{0,7},{1,0},{2,1},{3,2},{4,3},{5,4},{6,5},{7,6},{8,15},{9,8},{10,9... | collective-permute-start | bytes 98312 | tf_op jit(solution)/shard_map/ppermute | solution.py:605
  50.4 6.2 %collective-permute-start.13 = (f32[64,128]{1,0:T(8,128)S(1)}, f32[64,128]{1,0:T(8,128)S(1)}, u32[]{:S(2)}, u32[]{:S(2)}) collective-permute-start(f32[64,128]{1,0:T(8,128)S(1)} %get-tuple-element.129.dir_cell.refs_0_.refs_21_), channel_id=1, source_target_pairs={{0,1},{1,2},{2,3},{3,4},{4,5},{5,6},{6,7},{7,0},{8,9},{9,10},{10,1... | collective-permute-start | bytes 98312 | tf_op jit(solution)/shard_map/ppermute | solution.py:605
  51.5 5.4 %collective-permute-start.12 = (f32[64,128]{1,0:T(8,128)S(1)}, f32[64,128]{1,0:T(8,128)S(1)}, u32[]{:S(2)}, u32[]{:S(2)}) collective-permute-start(f32[64,128]{1,0:T(8,128)S(1)} %get-tuple-element.129.dir_cell.refs_0_.refs_21_), channel_id=1, source_target_pairs={{0,248},{8,0},{16,8},{24,16},{32,24},{40,32},{48,40},{56,48},{64,5... | collective-permute-start | bytes 98312 | tf_op jit(solution)/shard_map/ppermute | solution.py:605
  55.9 6.1 %collective-permute-start.11 = (f32[64,128]{1,0:T(8,128)S(1)}, f32[64,128]{1,0:T(8,128)S(1)}, u32[]{:S(2)}, u32[]{:S(2)}) collective-permute-start(f32[64,128]{1,0:T(8,128)S(1)} %get-tuple-element.129.dir_cell.refs_0_.refs_21_), channel_id=1, source_target_pairs={{0,8},{8,16},{16,24},{24,32},{32,40},{40,48},{48,56},{56,64},{64,7... | collective-permute-start | bytes 98312 | tf_op jit(solution)/shard_map/ppermute | solution.py:605
  62.1 4.0 %collective-permute-start.18 = (f32[64,128]{1,0:T(8,128)S(1)}, f32[64,128]{1,0:T(8,128)S(1)}, u32[]{:S(2)}, u32[]{:S(2)}) collective-permute-start(f32[64,128]{1,0:T(8,128)S(1)} %get-tuple-element.142.dir_cell.refs_0_.refs_22_), channel_id=1, source_target_pairs={{0,7},{1,0},{2,1},{3,2},{4,3},{5,4},{6,5},{7,6},{8,15},{9,8},{10,9... | collective-permute-start | bytes 98312 | tf_op jit(solution)/shard_map/ppermute | solution.py:605
  62.3 3.8 %collective-permute-start.17 = (f32[64,128]{1,0:T(8,128)S(1)}, f32[64,128]{1,0:T(8,128)S(1)}, u32[]{:S(2)}, u32[]{:S(2)}) collective-permute-start(f32[64,128]{1,0:T(8,128)S(1)} %get-tuple-element.142.dir_cell.refs_0_.refs_22_), channel_id=1, source_target_pairs={{0,1},{1,2},{2,3},{3,4},{4,5},{5,6},{6,7},{7,0},{8,9},{9,10},{10,1... | collective-permute-start | bytes 98312 | tf_op jit(solution)/shard_map/ppermute | solution.py:605
  63.8 2.8 %collective-permute-start.16 = (f32[64,128]{1,0:T(8,128)S(1)}, f32[64,128]{1,0:T(8,128)S(1)}, u32[]{:S(2)}, u32[]{:S(2)}) collective-permute-start(f32[64,128]{1,0:T(8,128)S(1)} %get-tuple-element.142.dir_cell.refs_0_.refs_22_), channel_id=1, source_target_pairs={{0,248},{8,0},{16,8},{24,16},{32,24},{40,32},{48,40},{56,48},{64,5... | collective-permute-start | bytes 98312 | tf_op jit(solution)/shard_map/ppermute | solution.py:605
  63.8 6.1 %collective-permute-start.15 = (f32[64,128]{1,0:T(8,128)S(1)}, f32[64,128]{1,0:T(8,128)S(1)}, u32[]{:S(2)}, u32[]{:S(2)}) collective-permute-start(f32[64,128]{1,0:T(8,128)S(1)} %get-tuple-element.142.dir_cell.refs_0_.refs_22_), channel_id=1, source_target_pairs={{0,8},{8,16},{16,24},{24,32},{32,40},{40,48},{48,56},{56,64},{64,7... | collective-permute-start | bytes 98312 | tf_op jit(solution)/shard_map/ppermute | solution.py:605
  70.1 4.0 %collective-permute-start.22 = (f32[64,128]{1,0:T(8,128)S(1)}, f32[64,128]{1,0:T(8,128)S(1)}, u32[]{:S(2)}, u32[]{:S(2)}) collective-permute-start(f32[64,128]{1,0:T(8,128)S(1)} %get-tuple-element.147.dir_cell.refs_0_.refs_23_), channel_id=1, source_target_pairs={{0,7},{1,0},{2,1},{3,2},{4,3},{5,4},{6,5},{7,6},{8,15},{9,8},{10,9... | collective-permute-start | bytes 98312 | tf_op jit(solution)/shard_map/ppermute | solution.py:605
  71.9 2.8 %collective-permute-start.20 = (f32[64,128]{1,0:T(8,128)S(1)}, f32[64,128]{1,0:T(8,128)S(1)}, u32[]{:S(2)}, u32[]{:S(2)}) collective-permute-start(f32[64,128]{1,0:T(8,128)S(1)} %get-tuple-element.147.dir_cell.refs_0_.refs_23_), channel_id=1, source_target_pairs={{0,248},{8,0},{16,8},{24,16},{32,24},{40,32},{48,40},{56,48},{64,5... | collective-permute-start | bytes 98312 | tf_op jit(solution)/shard_map/ppermute | solution.py:605
  71.9 6.1 %collective-permute-start.19 = (f32[64,128]{1,0:T(8,128)S(1)}, f32[64,128]{1,0:T(8,128)S(1)}, u32[]{:S(2)}, u32[]{:S(2)}) collective-permute-start(f32[64,128]{1,0:T(8,128)S(1)} %get-tuple-element.147.dir_cell.refs_0_.refs_23_), channel_id=1, source_target_pairs={{0,8},{8,16},{16,24},{24,32},{32,40},{40,48},{48,56},{56,64},{64,7... | collective-permute-start | bytes 98312 | tf_op jit(solution)/shard_map/ppermute | solution.py:605
  78.1 5.2 %collective-permute-start.26 = (f32[64,128]{1,0:T(8,128)S(1)}, f32[64,128]{1,0:T(8,128)S(1)}, u32[]{:S(2)}, u32[]{:S(2)}) collective-permute-start(f32[64,128]{1,0:T(8,128)S(1)} %get-tuple-element.152.dir_cell.refs_0_.refs_24_), channel_id=1, source_target_pairs={{0,7},{1,0},{2,1},{3,2},{4,3},{5,4},{6,5},{7,6},{8,15},{9,8},{10,9... | collective-permute-start | bytes 98312 | tf_op jit(solution)/shard_map/ppermute | solution.py:605
  81.0 2.8 %collective-permute-start.24 = (f32[64,128]{1,0:T(8,128)S(1)}, f32[64,128]{1,0:T(8,128)S(1)}, u32[]{:S(2)}, u32[]{:S(2)}) collective-permute-start(f32[64,128]{1,0:T(8,128)S(1)} %get-tuple-element.152.dir_cell.refs_0_.refs_24_), channel_id=1, source_target_pairs={{0,248},{8,0},{16,8},{24,16},{32,24},{40,32},{48,40},{56,48},{64,5... | collective-permute-start | bytes 98312 | tf_op jit(solution)/shard_map/ppermute | solution.py:605
  81.0 6.1 %collective-permute-start.23 = (f32[64,128]{1,0:T(8,128)S(1)}, f32[64,128]{1,0:T(8,128)S(1)}, u32[]{:S(2)}, u32[]{:S(2)}) collective-permute-start(f32[64,128]{1,0:T(8,128)S(1)} %get-tuple-element.152.dir_cell.refs_0_.refs_24_), channel_id=1, source_target_pairs={{0,8},{8,16},{16,24},{24,32},{32,40},{40,48},{48,56},{56,64},{64,7... | collective-permute-start | bytes 98312 | tf_op jit(solution)/shard_map/ppermute | solution.py:605
  87.3 5.2 %collective-permute-start.30 = (f32[64,128]{1,0:T(8,128)S(1)}, f32[64,128]{1,0:T(8,128)S(1)}, u32[]{:S(2)}, u32[]{:S(2)}) collective-permute-start(f32[64,128]{1,0:T(8,128)S(1)} %get-tuple-element.157.dir_cell.refs_0_.refs_25_), channel_id=1, source_target_pairs={{0,7},{1,0},{2,1},{3,2},{4,3},{5,4},{6,5},{7,6},{8,15},{9,8},{10,9... | collective-permute-start | bytes 98312 | tf_op jit(solution)/shard_map/ppermute | solution.py:605
  90.2 2.2 %collective-permute-start.29 = (f32[64,128]{1,0:T(8,128)S(1)}, f32[64,128]{1,0:T(8,128)S(1)}, u32[]{:S(2)}, u32[]{:S(2)}) collective-permute-start(f32[64,128]{1,0:T(8,128)S(1)} %get-tuple-element.157.dir_cell.refs_0_.refs_25_), channel_id=1, source_target_pairs={{0,1},{1,2},{2,3},{3,4},{4,5},{5,6},{6,7},{7,0},{8,9},{9,10},{10,1... | collective-permute-start | bytes 98312 | tf_op jit(solution)/shard_map/ppermute | solution.py:605
  90.2 2.8 %collective-permute-start.28 = (f32[64,128]{1,0:T(8,128)S(1)}, f32[64,128]{1,0:T(8,128)S(1)}, u32[]{:S(2)}, u32[]{:S(2)}) collective-permute-start(f32[64,128]{1,0:T(8,128)S(1)} %get-tuple-element.157.dir_cell.refs_0_.refs_25_), channel_id=1, source_target_pairs={{0,248},{8,0},{16,8},{24,16},{32,24},{40,32},{48,40},{56,48},{64,5... | collective-permute-start | bytes 98312 | tf_op jit(solution)/shard_map/ppermute | solution.py:605
  90.2 6.1 %collective-permute-start.27 = (f32[64,128]{1,0:T(8,128)S(1)}, f32[64,128]{1,0:T(8,128)S(1)}, u32[]{:S(2)}, u32[]{:S(2)}) collective-permute-start(f32[64,128]{1,0:T(8,128)S(1)} %get-tuple-element.157.dir_cell.refs_0_.refs_25_), channel_id=1, source_target_pairs={{0,8},{8,16},{16,24},{24,32},{32,40},{40,48},{48,56},{56,64},{64,7... | collective-permute-start | bytes 98312 | tf_op jit(solution)/shard_map/ppermute | solution.py:605
  119.4 4.0 %collective-permute-start.34 = (f32[64,128]{1,0:T(8,128)S(1)}, f32[64,128]{1,0:T(8,128)S(1)}, u32[]{:S(2)}, u32[]{:S(2)}) collective-permute-start(f32[64,128]{1,0:T(8,128)S(1)} %get-tuple-element.169.dir_cell.refs_0_.refs_5_), channel_id=1, source_target_pairs={{0,7},{1,0},{2,1},{3,2},{4,3},{5,4},{6,5},{7,6},{8,15},{9,8},{10,9... | collective-permute-start | bytes 98312 | tf_op jit(solution)/shard_map/ppermute | solution.py:605
  120.1 3.2 %collective-permute-start.33 = (f32[64,128]{1,0:T(8,128)S(1)}, f32[64,128]{1,0:T(8,128)S(1)}, u32[]{:S(2)}, u32[]{:S(2)}) collective-permute-start(f32[64,128]{1,0:T(8,128)S(1)} %get-tuple-element.169.dir_cell.refs_0_.refs_5_), channel_id=1, source_target_pairs={{0,1},{1,2},{2,3},{3,4},{4,5},{5,6},{6,7},{7,0},{8,9},{9,10},{10,1... | collective-permute-start | bytes 98312 | tf_op jit(solution)/shard_map/ppermute | solution.py:605
  121.1 3.4 %collective-permute-start.32 = (f32[64,128]{1,0:T(8,128)S(1)}, f32[64,128]{1,0:T(8,128)S(1)}, u32[]{:S(2)}, u32[]{:S(2)}) collective-permute-start(f32[64,128]{1,0:T(8,128)S(1)} %get-tuple-element.169.dir_cell.refs_0_.refs_5_), channel_id=1, source_target_pairs={{0,248},{8,0},{16,8},{24,16},{32,24},{40,32},{48,40},{56,48},{64,5... | collective-permute-start | bytes 98312 | tf_op jit(solution)/shard_map/ppermute | solution.py:605
  121.7 6.5 %collective-permute-start.31 = (f32[64,128]{1,0:T(8,128)S(1)}, f32[64,128]{1,0:T(8,128)S(1)}, u32[]{:S(2)}, u32[]{:S(2)}) collective-permute-start(f32[64,128]{1,0:T(8,128)S(1)} %get-tuple-element.169.dir_cell.refs_0_.refs_5_), channel_id=1, source_target_pairs={{0,8},{8,16},{16,24},{24,32},{32,40},{40,48},{48,56},{56,64},{64,7... | collective-permute-start | bytes 98312 | tf_op jit(solution)/shard_map/ppermute | solution.py:605
  128.3 4.2 %collective-permute-start.38 = (f32[64,128]{1,0:T(8,128)S(1)}, f32[64,128]{1,0:T(8,128)S(1)}, u32[]{:S(2)}, u32[]{:S(2)}) collective-permute-start(f32[64,128]{1,0:T(8,128)S(1)} %get-tuple-element.182.dir_cell.refs_0_.refs_6_), channel_id=1, source_target_pairs={{0,7},{1,0},{2,1},{3,2},{4,3},{5,4},{6,5},{7,6},{8,15},{9,8},{10,9... | collective-permute-start | bytes 98312 | tf_op jit(solution)/shard_map/ppermute | solution.py:605
  128.9 3.6 %collective-permute-start.37 = (f32[64,128]{1,0:T(8,128)S(1)}, f32[64,128]{1,0:T(8,128)S(1)}, u32[]{:S(2)}, u32[]{:S(2)}) collective-permute-start(f32[64,128]{1,0:T(8,128)S(1)} %get-tuple-element.182.dir_cell.refs_0_.refs_6_), channel_id=1, source_target_pairs={{0,1},{1,2},{2,3},{3,4},{4,5},{5,6},{6,7},{7,0},{8,9},{9,10},{10,1... | collective-permute-start | bytes 98312 | tf_op jit(solution)/shard_map/ppermute | solution.py:605
  130.1 2.8 %collective-permute-start.36 = (f32[64,128]{1,0:T(8,128)S(1)}, f32[64,128]{1,0:T(8,128)S(1)}, u32[]{:S(2)}, u32[]{:S(2)}) collective-permute-start(f32[64,128]{1,0:T(8,128)S(1)} %get-tuple-element.182.dir_cell.refs_0_.refs_6_), channel_id=1, source_target_pairs={{0,248},{8,0},{16,8},{24,16},{32,24},{40,32},{48,40},{56,48},{64,5... | collective-permute-start | bytes 98312 | tf_op jit(solution)/shard_map/ppermute | solution.py:605
  130.2 6.1 %collective-permute-start.35 = (f32[64,128]{1,0:T(8,128)S(1)}, f32[64,128]{1,0:T(8,128)S(1)}, u32[]{:S(2)}, u32[]{:S(2)}) collective-permute-start(f32[64,128]{1,0:T(8,128)S(1)} %get-tuple-element.182.dir_cell.refs_0_.refs_6_), channel_id=1, source_target_pairs={{0,8},{8,16},{16,24},{24,32},{32,40},{40,48},{48,56},{56,64},{64,7... | collective-permute-start | bytes 98312 | tf_op jit(solution)/shard_map/ppermute | solution.py:605
  136.4 4.0 %collective-permute-start.42 = (f32[64,128]{1,0:T(8,128)S(1)}, f32[64,128]{1,0:T(8,128)S(1)}, u32[]{:S(2)}, u32[]{:S(2)}) collective-permute-start(f32[64,128]{1,0:T(8,128)S(1)} %get-tuple-element.187.dir_cell.refs_0_.refs_7_), channel_id=1, source_target_pairs={{0,7},{1,0},{2,1},{3,2},{4,3},{5,4},{6,5},{7,6},{8,15},{9,8},{10,9... | collective-permute-start | bytes 98312 | tf_op jit(solution)/shard_map/ppermute | solution.py:605
  138.0 2.4 %collective-permute-start.41 = (f32[64,128]{1,0:T(8,128)S(1)}, f32[64,128]{1,0:T(8,128)S(1)}, u32[]{:S(2)}, u32[]{:S(2)}) collective-permute-start(f32[64,128]{1,0:T(8,128)S(1)} %get-tuple-element.187.dir_cell.refs_0_.refs_7_), channel_id=1, source_target_pairs={{0,1},{1,2},{2,3},{3,4},{4,5},{5,6},{6,7},{7,0},{8,9},{9,10},{10,1... | collective-permute-start | bytes 98312 | tf_op jit(solution)/shard_map/ppermute | solution.py:605
  138.2 2.8 %collective-permute-start.40 = (f32[64,128]{1,0:T(8,128)S(1)}, f32[64,128]{1,0:T(8,128)S(1)}, u32[]{:S(2)}, u32[]{:S(2)}) collective-permute-start(f32[64,128]{1,0:T(8,128)S(1)} %get-tuple-element.187.dir_cell.refs_0_.refs_7_), channel_id=1, source_target_pairs={{0,248},{8,0},{16,8},{24,16},{32,24},{40,32},{48,40},{56,48},{64,5... | collective-permute-start | bytes 98312 | tf_op jit(solution)/shard_map/ppermute | solution.py:605
  138.2 6.1 %collective-permute-start.39 = (f32[64,128]{1,0:T(8,128)S(1)}, f32[64,128]{1,0:T(8,128)S(1)}, u32[]{:S(2)}, u32[]{:S(2)}) collective-permute-start(f32[64,128]{1,0:T(8,128)S(1)} %get-tuple-element.187.dir_cell.refs_0_.refs_7_), channel_id=1, source_target_pairs={{0,8},{8,16},{16,24},{24,32},{32,40},{40,48},{48,56},{56,64},{64,7... | collective-permute-start | bytes 98312 | tf_op jit(solution)/shard_map/ppermute | solution.py:605
  144.4 5.1 %collective-permute-start.46 = (f32[64,128]{1,0:T(8,128)S(1)}, f32[64,128]{1,0:T(8,128)S(1)}, u32[]{:S(2)}, u32[]{:S(2)}) collective-permute-start(f32[64,128]{1,0:T(8,128)S(1)} %get-tuple-element.192.dir_cell.refs_0_.refs_8_), channel_id=1, source_target_pairs={{0,7},{1,0},{2,1},{3,2},{4,3},{5,4},{6,5},{7,6},{8,15},{9,8},{10,9... | collective-permute-start | bytes 98312 | tf_op jit(solution)/shard_map/ppermute | solution.py:605
  147.3 2.8 %collective-permute-start.44 = (f32[64,128]{1,0:T(8,128)S(1)}, f32[64,128]{1,0:T(8,128)S(1)}, u32[]{:S(2)}, u32[]{:S(2)}) collective-permute-start(f32[64,128]{1,0:T(8,128)S(1)} %get-tuple-element.192.dir_cell.refs_0_.refs_8_), channel_id=1, source_target_pairs={{0,248},{8,0},{16,8},{24,16},{32,24},{40,32},{48,40},{56,48},{64,5... | collective-permute-start | bytes 98312 | tf_op jit(solution)/shard_map/ppermute | solution.py:605
  147.3 6.1 %collective-permute-start.43 = (f32[64,128]{1,0:T(8,128)S(1)}, f32[64,128]{1,0:T(8,128)S(1)}, u32[]{:S(2)}, u32[]{:S(2)}) collective-permute-start(f32[64,128]{1,0:T(8,128)S(1)} %get-tuple-element.192.dir_cell.refs_0_.refs_8_), channel_id=1, source_target_pairs={{0,8},{8,16},{16,24},{24,32},{32,40},{40,48},{48,56},{56,64},{64,7... | collective-permute-start | bytes 98312 | tf_op jit(solution)/shard_map/ppermute | solution.py:605
  153.5 5.2 %collective-permute-start.50 = (f32[64,128]{1,0:T(8,128)S(1)}, f32[64,128]{1,0:T(8,128)S(1)}, u32[]{:S(2)}, u32[]{:S(2)}) collective-permute-start(f32[64,128]{1,0:T(8,128)S(1)} %get-tuple-element.197.dir_cell.refs_0_.refs_9_), channel_id=1, source_target_pairs={{0,7},{1,0},{2,1},{3,2},{4,3},{5,4},{6,5},{7,6},{8,15},{9,8},{10,9... | collective-permute-start | bytes 98312 | tf_op jit(solution)/shard_map/ppermute | solution.py:605
  156.5 2.3 %collective-permute-start.49 = (f32[64,128]{1,0:T(8,128)S(1)}, f32[64,128]{1,0:T(8,128)S(1)}, u32[]{:S(2)}, u32[]{:S(2)}) collective-permute-start(f32[64,128]{1,0:T(8,128)S(1)} %get-tuple-element.197.dir_cell.refs_0_.refs_9_), channel_id=1, source_target_pairs={{0,1},{1,2},{2,3},{3,4},{4,5},{5,6},{6,7},{7,0},{8,9},{9,10},{10,1... | collective-permute-start | bytes 98312 | tf_op jit(solution)/shard_map/ppermute | solution.py:605
  156.5 2.8 %collective-permute-start.48 = (f32[64,128]{1,0:T(8,128)S(1)}, f32[64,128]{1,0:T(8,128)S(1)}, u32[]{:S(2)}, u32[]{:S(2)}) collective-permute-start(f32[64,128]{1,0:T(8,128)S(1)} %get-tuple-element.197.dir_cell.refs_0_.refs_9_), channel_id=1, source_target_pairs={{0,248},{8,0},{16,8},{24,16},{32,24},{40,32},{48,40},{56,48},{64,5... | collective-permute-start | bytes 98312 | tf_op jit(solution)/shard_map/ppermute | solution.py:605
  156.5 6.1 %collective-permute-start.47 = (f32[64,128]{1,0:T(8,128)S(1)}, f32[64,128]{1,0:T(8,128)S(1)}, u32[]{:S(2)}, u32[]{:S(2)}) collective-permute-start(f32[64,128]{1,0:T(8,128)S(1)} %get-tuple-element.197.dir_cell.refs_0_.refs_9_), channel_id=1, source_target_pairs={{0,8},{8,16},{16,24},{24,32},{32,40},{40,48},{48,56},{56,64},{64,7... | collective-permute-start | bytes 98312 | tf_op jit(solution)/shard_map/ppermute | solution.py:605
  (10 other events, 88.5 us)

commit v3 on v2

--- a/solution.py
+++ b/solution.py
@@ -106,7 +106,7 @@
 
 def pack(
     ids, parts, rows, live, pres, satur, perm, flags, q, r, trans, ups, store,
-    ids_out, message, record, cell, flag_y, flag_room, up_room, store_room, sems,
+    ids_out, message, records, cell, flag_y, record, flag_room, up_room, store_room, sems,
 ):
     copies = [
         pltpu.make_async_copy(src, dst, sems.at[n])
@@ -147,11 +147,13 @@
             record[row : row + 1] = store_room[c : c + 1, 128 * k : 128 * k + 128]
     first = message[0:128].T
     rest = jnp.concatenate([message[128:160], jnp.zeros((96, 128), F32)], axis=0).T
-    record[56:57] = first[127:128]
-    record[57:58] = rest[127:128]
-    record[58:59] = first[0:1]
-    record[59:60] = rest[0:1]
-    record[60:64] = jnp.zeros((4, 128), F32)
+    record[49:50] = first[127:128]
+    record[50:51] = rest[127:128]
+    record[51:52] = first[0:1]
+    record[52:53] = rest[0:1]
+    copied = record[...]
+    for k in range(8):
+        records[k] = copied
 
 
 def owner_of(piece, me):
@@ -174,14 +176,14 @@
 ):
     me = ids[1]
     lane = lax.broadcasted_iota(jnp.int32, (8, 128), 1)
-    places_of = [pl.multiple_of(owner_of(k, me) * 64, 64) for k in range(8)]
+    places_of = [pl.multiple_of(owner_of(k, me) * 56, 8) for k in range(8)]
     for k in range(8):
         code_room[k : k + 1] = records[pl.ds(places_of[k] + 48, 8), :][:1].astype(jnp.int32)
     copy = pltpu.make_async_copy(code_room, codes, sem)
     copy.start()
 
-    for side, owner, row in ((left, (me + 7) & 7, 0), (right, (me + 1) & 7, 2)):
-        columns = records[pl.ds(pl.multiple_of(owner * 64, 64) + 56, 8), :]
+    for side, owner, row in ((left, (me + 7) & 7, 1), (right, (me + 1) & 7, 3)):
+        columns = records[pl.ds(pl.multiple_of(owner * 56, 8) + 48, 8), :]
         side[0:128] = jnp.broadcast_to(columns[row : row + 1], (128, 128)).T
         side[128:160] = jnp.broadcast_to(columns[row + 1 : row + 2], (128, 128)).T[:32]
 
@@ -648,7 +650,7 @@
     one_left = ring(coupling, "frac", -2)
     ids, message, record, cell_old, flag_y = call(
         pack,
-        [smem_i32(4), vmem(160, 128), vmem(64, 128), vmem(64, 128), vmem(32, 128)],
+        [smem_i32(4), vmem(160, 128), vmem(8, 56, 128), vmem(64, 128), vmem(32, 128)],
         [
             ids,
             target_part,
@@ -667,6 +669,7 @@
         "ssss" + "H" * 9,
         out_spaces="svvvv",
         scratch=[
+            vmem(56, 128),
             pltpu.VMEM((3, 1, 32, 128), jnp.int32),
             pltpu.VMEM((8, 128), jnp.int32),
             pltpu.VMEM((2, 1024), F32),
@@ -674,7 +677,7 @@
         ],
         name="pack",
     )
-    records = lax.all_gather(record, "frac", axis=0, tiled=True)
+    records = lax.all_to_all(record, "frac", 0, 0).reshape(448, 128)
     one_right, one_left, records = after(one_right, one_left, records)
     below, above = ring(message, "region", 1), ring(message, "region", -1)
     half = blocks // 2
@@ -705,6 +708,7 @@
             pltpu.SMEM((8, 128), jnp.int32),
             pltpu.SemaphoreType.DMA,
         ],
+        flops=6_000_000,
         name="survey",
     )
     around = [below, above, left, right]
@@ -713,13 +717,14 @@
         [vmem(192, 128), vmem(192, 128)],
         [ids, message, *around, flag_y],
         "Svvvvvv",
+        flops=2_000_000,
         name="geometry",
     )
     [weights] = call(
         collect,
         [vmem(room, 64, 128)],
         [places, count, *pieces],
-        "SS" + "a" * 10,
+        "SSH" + "a" * 9,
         scratch=[pltpu.SemaphoreType.DMA((room,))],
         name="collect",
     )

time: 194 us -> 186 us (0.959)
  blocking collectives: 63.3 us -> 50.2 us
  starting transfers between devices: 58 us -> 64.7 us
    all_gather x1 -> x0, blocking collectives: 13.2 us -> none  [on_device(): records = lax.all_gather(record, 'frac', axis=0, tiled=True)]
    all_to_all x0 -> x1, starting transfers between devices: none -> 5.47 us  [on_device(): records = lax.all_to_all(record, 'frac', 0, 0).reshape(448, 128)]
  transfers between devices with their start and end apart: 51 -> 52, of which waited for: 22 -> 29; matrix products, arithmetic and copies ran while one was open for 0% -> 0% of each run, Pallas kernels for 6% -> 5%
where the time goes in v3:
time: 186 us
  starting transfers between devices  64.7 us (35%)
  blocking collectives  50.2 us (27%)
  waiting for transfers between devices  49.3 us (27%)
  Pallas kernels  18.3 us (10%)
    ppermute x46, starting transfers between devices, ring(): lax.ppermute(block, axis, [(i, (i + distance) % count) for i in range(cou...  55.7 us
    ppermute x46, waiting for transfers between devices, ring(): lax.ppermute(block, axis, [(i, (i + distance) % count) for i in range(cou...  49.3 us
    all_to_all x2, blocking collectives, on_device(): parts = lax.all_to_all(parts, ('region', 'frac'), 0, 0)  42.3 us
    pallas_call x29, Pallas kernels, call(): pl.pallas_call(body, out_shape=list(outs), in_specs=[pl.BlockSpec(memory_...  18.3 us
    all_to_all x1, blocking collectives, on_device(): moved = jnp.sum(lax.all_to_all(moved, 'frac', 0, 0), axis=0)  7.93 us
    all_to_all x1, starting transfers between devices, on_device(): records = lax.all_to_all(record, 'frac', 0, 0).reshape(448, 128)  5.47 us
  transfers between devices with their start and end apart: 52, of which 29 were waited for; matrix products, arithmetic and copies ran while one was open for 0% of the time, Pallas kernels for 5%

profile of v3, /device:TPU:1, one launch (start us, length us, event | category | flops | bytes accessed | tf_op | source)
XLA Modules:
  0.0 186.4 jit_solution(12823160900052191642)
XLA Ops:
  0.6 3.4 %collective-permute-start.1 = (f32[16,64,128]{2,1,0:T(8,128)}, f32[16,64,128]{2,1,0:T(8,128)S(1)}, u32[]{:S(2)}, u32[]{:S(2)}) collective-permute-start(f32[16,64,128]{2,1,0:T(8,128)} %refs_0_.1), channel_id=1, source_target_pairs={{0,6},{1,7},{2,0},{3,1},{4,2},{5,3},{6,4},{7,5},{8,14},{9,15},{10,... | collective-permute-start | bytes 1572872 | tf_op jit(solution)/shard_map/ppermute | solution.py:607
  6.1 2.3 %pack.1 = (s32[4]{0:T(128)S(4)}, f32[160,128]{1,0:T(8,128)S(1)}, f32[8,56,128]{2,1,0:T(8,128)}, f32[64,128]{1,0:T(8,128)S(1)}, f32[32,128]{1,0:T(8,128)S(1)}) custom-call(s32[4]{0:T(128)S(1)} %pad_add_fusion.ids, s32[16]{0:T(128)S(1)} %copy-done.2, s32[16]{0:T(128)S(1)} %copy-done.3, s32[1]{0:T(128)S(6)} %copy.18.live, f32[1,32,128]{2,1,0:T(8,128)} %pres.1, ...), custom_call_target="tpu_custom_call" | custom-call | flops 20000 | bytes 20000 | tf_op jit(solution)/shard_map/pack/pallas_call | solution.py:39
  8.4 5.5 %all-to-all-start = ((f32[8,56,128]{2,1,0:T(8,128)}), f32[8,56,128]{2,1,0:T(8,128)S(1)}, u32[]{:S(2)}, u32[]{:S(2)}) async-start(f32[8,56,128]{2,1,0:T(8,128)} %get-tuple-element.108), calls=%async_computation | async-start | bytes 458752 | tf_op jit(solution)/shard_map/all_to_all | solution.py:680
  13.8 8.0 %collective-permute-start.3 = (f32[160,128]{1,0:T(8,128)S(1)}, f32[160,128]{1,0:T(8,128)S(1)}, u32[]{:S(2)}, u32[]{:S(2)}) collective-permute-start(f32[160,128]{1,0:T(8,128)S(1)} %get-tuple-element.114.own), channel_id=1, source_target_pairs={{0,248},{8,0},{16,8},{24,16},{32,24},{40,32},{48,40},{56,48},{64,5... | collective-permute-start | bytes 245768 | tf_op jit(solution)/shard_map/ppermute | solution.py:607
  22.2 3.0 %collective-permute-start.5 = (f32[8,64,128]{2,1,0:T(8,128)S(1)}, f32[8,64,128]{2,1,0:T(8,128)S(1)}, u32[]{:S(2)}, u32[]{:S(2)}) collective-permute-start(f32[8,64,128]{2,1,0:T(8,128)S(1)} %slice.7), channel_id=1, source_target_pairs={{0,6},{1,7},{2,0},{3,1},{4,2},{5,3},{6,4},{7,5},{8,14},{9,15},{10,... | collective-permute-start | bytes 786440 | tf_op jit(solution)/shard_map/ppermute | solution.py:607
  25.6 3.4 %collective-permute-done.2.below.refs_15_ = f32[160,128]{1,0:T(8,128)S(1)} collective-permute-done((f32[160,128]{1,0:T(8,128)S(1)}, f32[160,128]{1,0:T(8,128)S(1)}, u32[]{:S(2)}, u32[]{:S(2)}) %collective-permute-start.2) | collective-permute-done | bytes 81952 | tf_op jit(solution)/shard_map/ppermute | solution.py:607
  29.0 1.1 collective-permute-start.10
  30.1 0.9 collective-permute-done.5.refs_3_
  31.8 2.3 %collective-permute-done.4.refs_2_ = f32[8,64,128]{2,1,0:T(8,128)S(1)} collective-permute-done((f32[8,64,128]{2,1,0:T(8,128)S(1)}, f32[8,64,128]{2,1,0:T(8,128)S(1)}, u32[]{:S(2)}, u32[]{:S(2)}) %collective-permute-start.4) | collective-permute-done | bytes 262176 | tf_op jit(solution)/shard_map/ppermute | solution.py:607
  34.1 1.1 collective-permute-start.8
  35.2 1.6 survey.1
  37.0 3.0 %collect.1.refs_13_.weights = f32[132,64,128]{2,1,0:T(8,128)S(1)} custom-call(s32[132]{0:T(256)S(4)} %get-tuple-element.125.places, s32[1]{0:T(128)S(4)} %get-tuple-element.112.count.refs_2_, f32[16,64,128]{2,1,0:T(8,128)} %refs_0_.1, f32[16,64,128]{2,1,0:T(8,128)S(1)} %collective-permute-done.refs_1_, f32[8,64,128]{2,1,0:T(8,128)S(1)} %collective-permute-done.4.refs_2_, ...), custom_call_target="tpu_custom_call" | custom-call | flops 20000 | bytes 20000 | tf_op jit(solution)/shard_map/collect/pallas_call | solution.py:39
  40.1 1.0 linearise.2
  41.1 1.7 collective-permute-start.13
  42.8 4.4 %collective-permute-start.12 = (f32[64,128]{1,0:T(8,128)S(1)}, f32[64,128]{1,0:T(8,128)S(1)}, u32[]{:S(2)}, u32[]{:S(2)}) collective-permute-start(f32[64,128]{1,0:T(8,128)S(1)} %get-tuple-element.129.dir_cell.refs_0_.refs_21_), channel_id=1, source_target_pairs={{0,248},{8,0},{16,8},{24,16},{32,24},{40,32},{48,40},{56,48},{64,5... | collective-permute-start | bytes 98312 | tf_op jit(solution)/shard_map/ppermute | solution.py:607
  48.2 5.1 %collective-permute-done.11.refs_1_.refs_31_ = f32[64,128]{1,0:T(8,128)S(1)} collective-permute-done((f32[64,128]{1,0:T(8,128)S(1)}, f32[64,128]{1,0:T(8,128)S(1)}, u32[]{:S(2)}, u32[]{:S(2)}) %collective-permute-start.11) | collective-permute-done | bytes 32800 | tf_op jit(solution)/shard_map/ppermute | solution.py:607
  53.4 1.2 collective-permute-start.18
  55.6 1.1 collective-permute-start.15
  58.0 3.7 %collective-permute-done.15.refs_1_.refs_35_ = f32[64,128]{1,0:T(8,128)S(1)} collective-permute-done((f32[64,128]{1,0:T(8,128)S(1)}, f32[64,128]{1,0:T(8,128)S(1)}, u32[]{:S(2)}, u32[]{:S(2)}) %collective-permute-start.15) | collective-permute-done | bytes 32800 | tf_op jit(solution)/shard_map/ppermute | solution.py:607
  61.8 2.1 %collective-permute-start.22 = (f32[64,128]{1,0:T(8,128)S(1)}, f32[64,128]{1,0:T(8,128)S(1)}, u32[]{:S(2)}, u32[]{:S(2)}) collective-permute-start(f32[64,128]{1,0:T(8,128)S(1)} %get-tuple-element.147.dir_cell.refs_0_.refs_23_), channel_id=1, source_target_pairs={{0,7},{1,0},{2,1},{3,2},{4,3},{5,4},{6,5},{7,6},{8,15},{9,8},{10,9... | collective-permute-start | bytes 98312 | tf_op jit(solution)/shard_map/ppermute | solution.py:607
  63.9 1.5 collective-permute-start.19
  66.6 3.3 %collective-permute-done.19.refs_1_.refs_39_ = f32[64,128]{1,0:T(8,128)S(1)} collective-permute-done((f32[64,128]{1,0:T(8,128)S(1)}, f32[64,128]{1,0:T(8,128)S(1)}, u32[]{:S(2)}, u32[]{:S(2)}) %collective-permute-start.19) | collective-permute-done | bytes 32800 | tf_op jit(solution)/shard_map/ppermute | solution.py:607
  70.1 3.0 %collective-permute-start.26 = (f32[64,128]{1,0:T(8,128)S(1)}, f32[64,128]{1,0:T(8,128)S(1)}, u32[]{:S(2)}, u32[]{:S(2)}) collective-permute-start(f32[64,128]{1,0:T(8,128)S(1)} %get-tuple-element.152.dir_cell.refs_0_.refs_24_), channel_id=1, source_target_pairs={{0,7},{1,0},{2,1},{3,2},{4,3},{5,4},{6,5},{7,6},{8,15},{9,8},{10,9... | collective-permute-start | bytes 98312 | tf_op jit(solution)/shard_map/ppermute | solution.py:607
  73.1 1.5 collective-permute-start.23
  75.8 3.3 %collective-permute-done.23.refs_1_.refs_43_ = f32[64,128]{1,0:T(8,128)S(1)} collective-permute-done((f32[64,128]{1,0:T(8,128)S(1)}, f32[64,128]{1,0:T(8,128)S(1)}, u32[]{:S(2)}, u32[]{:S(2)}) %collective-permute-start.23) | collective-permute-done | bytes 32800 | tf_op jit(solution)/shard_map/ppermute | solution.py:607
  79.3 3.0 %collective-permute-start.30 = (f32[64,128]{1,0:T(8,128)S(1)}, f32[64,128]{1,0:T(8,128)S(1)}, u32[]{:S(2)}, u32[]{:S(2)}) collective-permute-start(f32[64,128]{1,0:T(8,128)S(1)} %get-tuple-element.157.dir_cell.refs_0_.refs_25_), channel_id=1, source_target_pairs={{0,7},{1,0},{2,1},{3,2},{4,3},{5,4},{6,5},{7,6},{8,15},{9,8},{10,9... | collective-permute-start | bytes 98312 | tf_op jit(solution)/shard_map/ppermute | solution.py:607
  82.2 1.5 collective-permute-start.27
  85.0 3.3 %collective-permute-done.27.refs_1_.refs_47_ = f32[64,128]{1,0:T(8,128)S(1)} collective-permute-done((f32[64,128]{1,0:T(8,128)S(1)}, f32[64,128]{1,0:T(8,128)S(1)}, u32[]{:S(2)}, u32[]{:S(2)}) %collective-permute-start.27) | collective-permute-done | bytes 32800 | tf_op jit(solution)/shard_map/ppermute | solution.py:607
  88.8 20.8 %all_to_all.20.refs_20_ = f32[256,1,128]{2,1,0:T(1,128)S(1)} all-to-all(f32[256,1,128]{2,1,0:T(1,128)S(1)} %inner_products.2), channel_id=1, replica_groups=mesh['region'=32,'frac'=8] {'region','frac'}, dimensions={0} | all-to-all | bytes 262144 | tf_op jit(solution)/shard_map/all_to_all | solution.py:839
  109.6 1.5 linearise.3
  111.7 1.2 collective-permute-start.33
  114.9 1.1 collective-permute-done.32.refs_2_
  116.0 3.5 %collective-permute-done.31.refs_1_ = f32[64,128]{1,0:T(8,128)S(1)} collective-permute-done((f32[64,128]{1,0:T(8,128)S(1)}, f32[64,128]{1,0:T(8,128)S(1)}, u32[]{:S(2)}, u32[]{:S(2)}) %collective-permute-start.31) | collective-permute-done | bytes 32800 | tf_op jit(solution)/shard_map/ppermute | solution.py:607
  119.7 1.4 collective-permute-start.38
  121.4 1.5 collective-permute-start.35
  124.2 3.3 %collective-permute-done.35.refs_1_ = f32[64,128]{1,0:T(8,128)S(1)} collective-permute-done((f32[64,128]{1,0:T(8,128)S(1)}, f32[64,128]{1,0:T(8,128)S(1)}, u32[]{:S(2)}, u32[]{:S(2)}) %collective-permute-start.35) | collective-permute-done | bytes 32800 | tf_op jit(solution)/shard_map/ppermute | solution.py:607
  127.6 2.6 %collective-permute-start.42 = (f32[64,128]{1,0:T(8,128)S(1)}, f32[64,128]{1,0:T(8,128)S(1)}, u32[]{:S(2)}, u32[]{:S(2)}) collective-permute-start(f32[64,128]{1,0:T(8,128)S(1)} %get-tuple-element.187.dir_cell.refs_0_.refs_7_), channel_id=1, source_target_pairs={{0,7},{1,0},{2,1},{3,2},{4,3},{5,4},{6,5},{7,6},{8,15},{9,8},{10,9... | collective-permute-start | bytes 98312 | tf_op jit(solution)/shard_map/ppermute | solution.py:607
  130.3 1.5 collective-permute-start.39
  133.0 3.3 %collective-permute-done.39.refs_1_ = f32[64,128]{1,0:T(8,128)S(1)} collective-permute-done((f32[64,128]{1,0:T(8,128)S(1)}, f32[64,128]{1,0:T(8,128)S(1)}, u32[]{:S(2)}, u32[]{:S(2)}) %collective-permute-start.39) | collective-permute-done | bytes 32800 | tf_op jit(solution)/shard_map/ppermute | solution.py:607
  136.5 3.0 %collective-permute-start.46 = (f32[64,128]{1,0:T(8,128)S(1)}, f32[64,128]{1,0:T(8,128)S(1)}, u32[]{:S(2)}, u32[]{:S(2)}) collective-permute-start(f32[64,128]{1,0:T(8,128)S(1)} %get-tuple-element.192.dir_cell.refs_0_.refs_8_), channel_id=1, source_target_pairs={{0,7},{1,0},{2,1},{3,2},{4,3},{5,4},{6,5},{7,6},{8,15},{9,8},{10,9... | collective-permute-start | bytes 98312 | tf_op jit(solution)/shard_map/ppermute | solution.py:607
  139.5 1.5 collective-permute-start.43
  142.2 3.3 %collective-permute-done.43.refs_1_ = f32[64,128]{1,0:T(8,128)S(1)} collective-permute-done((f32[64,128]{1,0:T(8,128)S(1)}, f32[64,128]{1,0:T(8,128)S(1)}, u32[]{:S(2)}, u32[]{:S(2)}) %collective-permute-start.43) | collective-permute-done | bytes 32800 | tf_op jit(solution)/shard_map/ppermute | solution.py:607
  145.7 3.0 %collective-permute-start.50 = (f32[64,128]{1,0:T(8,128)S(1)}, f32[64,128]{1,0:T(8,128)S(1)}, u32[]{:S(2)}, u32[]{:S(2)}) collective-permute-start(f32[64,128]{1,0:T(8,128)S(1)} %get-tuple-element.197.dir_cell.refs_0_.refs_9_), channel_id=1, source_target_pairs={{0,7},{1,0},{2,1},{3,2},{4,3},{5,4},{6,5},{7,6},{8,15},{9,8},{10,9... | collective-permute-start | bytes 98312 | tf_op jit(solution)/shard_map/ppermute | solution.py:607
  148.6 1.5 collective-permute-start.47
  151.4 3.3 %collective-permute-done.47.refs_1_ = f32[64,128]{1,0:T(8,128)S(1)} collective-permute-done((f32[64,128]{1,0:T(8,128)S(1)}, f32[64,128]{1,0:T(8,128)S(1)}, u32[]{:S(2)}, u32[]{:S(2)}) %collective-permute-start.47) | collective-permute-done | bytes 32800 | tf_op jit(solution)/shard_map/ppermute | solution.py:607
  155.2 21.5 %all_to_all.21.refs_1_ = f32[256,1,128]{2,1,0:T(1,128)S(1)} all-to-all(f32[256,1,128]{2,1,0:T(1,128)S(1)} %inner_products.3), channel_id=1, replica_groups=mesh['region'=32,'frac'=8] {'region','frac'}, dimensions={0} | all-to-all | bytes 262144 | tf_op jit(solution)/shard_map/all_to_all | solution.py:839
  176.7 1.1 finish.1
  177.8 7.9 %all_to_all.22 = f32[8,16,128]{2,1,0:T(8,128)S(1)} all-to-all(f32[8,16,128]{2,1,0:T(8,128)S(1)} %get-tuple-element.211), channel_id=1, replica_groups=mesh['region'=32,'frac'=8] {'frac'}, dimensions={0} | all-to-all | bytes 131072 | tf_op jit(solution)/shard_map/all_to_all | solution.py:849
  (106 shorter events, 20.6 us)
Async XLA Ops:
  0.6 21.5 %collective-permute-start.1 = (f32[16,64,128]{2,1,0:T(8,128)}, f32[16,64,128]{2,1,0:T(8,128)S(1)}, u32[]{:S(2)}, u32[]{:S(2)}) collective-permute-start(f32[16,64,128]{2,1,0:T(8,128)} %refs_0_.1), channel_id=1, source_target_pairs={{0,6},{1,7},{2,0},{3,1},{4,2},{5,3},{6,4},{7,5},{8,14},{9,15},{10,... | collective-permute-start | bytes 1572872 | tf_op jit(solution)/shard_map/ppermute | solution.py:607
  4.0 18.2 %collective-permute-start = (f32[16,64,128]{2,1,0:T(8,128)}, f32[16,64,128]{2,1,0:T(8,128)S(1)}, u32[]{:S(2)}, u32[]{:S(2)}) collective-permute-start(f32[16,64,128]{2,1,0:T(8,128)} %refs_0_.1), channel_id=1, source_target_pairs={{0,2},{1,3},{2,4},{3,5},{4,6},{5,7},{6,0},{7,1},{8,10},{9,11},{10,... | collective-permute-start | bytes 1572872 | tf_op jit(solution)/shard_map/ppermute | solution.py:607
  8.4 13.8 %all-to-all-start = ((f32[8,56,128]{2,1,0:T(8,128)}), f32[8,56,128]{2,1,0:T(8,128)S(1)}, u32[]{:S(2)}, u32[]{:S(2)}) async-start(f32[8,56,128]{2,1,0:T(8,128)} %get-tuple-element.108), calls=%async_computation | async-start | bytes 458752 | tf_op jit(solution)/shard_map/all_to_all | solution.py:680
  13.8 11.4 %collective-permute-start.3 = (f32[160,128]{1,0:T(8,128)S(1)}, f32[160,128]{1,0:T(8,128)S(1)}, u32[]{:S(2)}, u32[]{:S(2)}) collective-permute-start(f32[160,128]{1,0:T(8,128)S(1)} %get-tuple-element.114.own), channel_id=1, source_target_pairs={{0,248},{8,0},{16,8},{24,16},{32,24},{40,32},{48,40},{56,48},{64,5... | collective-permute-start | bytes 245768 | tf_op jit(solution)/shard_map/ppermute | solution.py:607
  21.9 7.1 %collective-permute-start.2 = (f32[160,128]{1,0:T(8,128)S(1)}, f32[160,128]{1,0:T(8,128)S(1)}, u32[]{:S(2)}, u32[]{:S(2)}) collective-permute-start(f32[160,128]{1,0:T(8,128)S(1)} %get-tuple-element.114.own), channel_id=1, source_target_pairs={{0,8},{8,16},{16,24},{24,32},{32,40},{40,48},{48,56},{56,64},{64,7... | collective-permute-start | bytes 245768 | tf_op jit(solution)/shard_map/ppermute | solution.py:607
  21.9 15.1 %collective-permute-start.6 = (f32[16,64,128]{2,1,0:T(8,128)}, f32[16,64,128]{2,1,0:T(8,128)S(1)}, u32[]{:S(2)}, u32[]{:S(2)}) collective-permute-start(f32[16,64,128]{2,1,0:T(8,128)} %refs_0_.1), channel_id=1, source_target_pairs={{0,1},{1,0},{2,3},{3,2},{4,5},{5,4},{6,7},{7,6},{8,9},{9,8},{10,11... | collective-permute-start | bytes 1572872 | tf_op jit(solution)/shard_map/ppermute | solution.py:611
  22.2 8.8 %collective-permute-start.5 = (f32[8,64,128]{2,1,0:T(8,128)S(1)}, f32[8,64,128]{2,1,0:T(8,128)S(1)}, u32[]{:S(2)}, u32[]{:S(2)}) collective-permute-start(f32[8,64,128]{2,1,0:T(8,128)S(1)} %slice.7), channel_id=1, source_target_pairs={{0,6},{1,7},{2,0},{3,1},{4,2},{5,3},{6,4},{7,5},{8,14},{9,15},{10,... | collective-permute-start | bytes 786440 | tf_op jit(solution)/shard_map/ppermute | solution.py:607
  25.3 8.8 %collective-permute-start.4 = (f32[8,64,128]{2,1,0:T(8,128)S(1)}, f32[8,64,128]{2,1,0:T(8,128)S(1)}, u32[]{:S(2)}, u32[]{:S(2)}) collective-permute-start(f32[8,64,128]{2,1,0:T(8,128)S(1)} %slice.6), channel_id=1, source_target_pairs={{0,2},{1,3},{2,4},{3,5},{4,6},{5,7},{6,0},{7,1},{8,10},{9,11},{10,... | collective-permute-start | bytes 786440 | tf_op jit(solution)/shard_map/ppermute | solution.py:607
  25.3 11.7 %collective-permute-start.7 = (f32[16,64,128]{2,1,0:T(8,128)S(1)}, f32[16,64,128]{2,1,0:T(8,128)S(1)}, u32[]{:S(2)}, u32[]{:S(2)}) collective-permute-start(f32[16,64,128]{2,1,0:T(8,128)S(1)} %collective-permute-done.refs_1_), channel_id=1, source_target_pairs={{0,1},{1,0},{2,3},{3,2},{4,5},{5,4},{6,7},{7,6},{8,9},{9,8},{10,11... | collective-permute-start | bytes 1572872 | tf_op jit(solution)/shard_map/ppermute | solution.py:611
  29.0 8.0 %collective-permute-start.10 = (f32[16,64,128]{2,1,0:T(8,128)S(1)}, f32[16,64,128]{2,1,0:T(8,128)S(1)}, u32[]{:S(2)}, u32[]{:S(2)}) collective-permute-start(f32[16,64,128]{2,1,0:T(8,128)S(1)} %collective-permute-done.1.refs_4_), channel_id=1, source_target_pairs={{0,1},{1,0},{2,3},{3,2},{4,5},{5,4},{6,7},{7,6},{8,9},{9,8},{10,11... | collective-permute-start | bytes 1572872 | tf_op jit(solution)/shard_map/ppermute | solution.py:611
  31.0 6.0 %collective-permute-start.9 = (f32[8,64,128]{2,1,0:T(8,128)S(1)}, f32[8,64,128]{2,1,0:T(8,128)S(1)}, u32[]{:S(2)}, u32[]{:S(2)}) collective-permute-start(f32[8,64,128]{2,1,0:T(8,128)S(1)} %collective-permute-done.5.refs_3_), channel_id=1, source_target_pairs={{0,1},{1,0},{2,3},{3,2},{4,5},{5,4},{6,7},{7,6},{8,9},{9,8},{10,11... | collective-permute-start | bytes 786440 | tf_op jit(solution)/shard_map/ppermute | solution.py:611
  34.1 2.9 %collective-permute-start.8 = (f32[8,64,128]{2,1,0:T(8,128)S(1)}, f32[8,64,128]{2,1,0:T(8,128)S(1)}, u32[]{:S(2)}, u32[]{:S(2)}) collective-permute-start(f32[8,64,128]{2,1,0:T(8,128)S(1)} %collective-permute-done.4.refs_2_), channel_id=1, source_target_pairs={{0,1},{1,0},{2,3},{3,2},{4,5},{5,4},{6,7},{7,6},{8,9},{9,8},{10,11... | collective-permute-start | bytes 786440 | tf_op jit(solution)/shard_map/ppermute | solution.py:611
  41.1 6.7 %collective-permute-start.14 = (f32[64,128]{1,0:T(8,128)S(1)}, f32[64,128]{1,0:T(8,128)S(1)}, u32[]{:S(2)}, u32[]{:S(2)}) collective-permute-start(f32[64,128]{1,0:T(8,128)S(1)} %get-tuple-element.129.dir_cell.refs_0_.refs_21_), channel_id=1, source_target_pairs={{0,7},{1,0},{2,1},{3,2},{4,3},{5,4},{6,5},{7,6},{8,15},{9,8},{10,9... | collective-permute-start | bytes 98312 | tf_op jit(solution)/shard_map/ppermute | solution.py:607
  41.1 6.7 %collective-permute-start.13 = (f32[64,128]{1,0:T(8,128)S(1)}, f32[64,128]{1,0:T(8,128)S(1)}, u32[]{:S(2)}, u32[]{:S(2)}) collective-permute-start(f32[64,128]{1,0:T(8,128)S(1)} %get-tuple-element.129.dir_cell.refs_0_.refs_21_), channel_id=1, source_target_pairs={{0,1},{1,2},{2,3},{3,4},{4,5},{5,6},{6,7},{7,0},{8,9},{9,10},{10,1... | collective-permute-start | bytes 98312 | tf_op jit(solution)/shard_map/ppermute | solution.py:607
  42.8 5.4 %collective-permute-start.12 = (f32[64,128]{1,0:T(8,128)S(1)}, f32[64,128]{1,0:T(8,128)S(1)}, u32[]{:S(2)}, u32[]{:S(2)}) collective-permute-start(f32[64,128]{1,0:T(8,128)S(1)} %get-tuple-element.129.dir_cell.refs_0_.refs_21_), channel_id=1, source_target_pairs={{0,248},{8,0},{16,8},{24,16},{32,24},{40,32},{48,40},{56,48},{64,5... | collective-permute-start | bytes 98312 | tf_op jit(solution)/shard_map/ppermute | solution.py:607
  47.2 6.1 %collective-permute-start.11 = (f32[64,128]{1,0:T(8,128)S(1)}, f32[64,128]{1,0:T(8,128)S(1)}, u32[]{:S(2)}, u32[]{:S(2)}) collective-permute-start(f32[64,128]{1,0:T(8,128)S(1)} %get-tuple-element.129.dir_cell.refs_0_.refs_21_), channel_id=1, source_target_pairs={{0,8},{8,16},{16,24},{24,32},{32,40},{40,48},{48,56},{56,64},{64,7... | collective-permute-start | bytes 98312 | tf_op jit(solution)/shard_map/ppermute | solution.py:607
  53.4 3.8 %collective-permute-start.18 = (f32[64,128]{1,0:T(8,128)S(1)}, f32[64,128]{1,0:T(8,128)S(1)}, u32[]{:S(2)}, u32[]{:S(2)}) collective-permute-start(f32[64,128]{1,0:T(8,128)S(1)} %get-tuple-element.142.dir_cell.refs_0_.refs_22_), channel_id=1, source_target_pairs={{0,7},{1,0},{2,1},{3,2},{4,3},{5,4},{6,5},{7,6},{8,15},{9,8},{10,9... | collective-permute-start | bytes 98312 | tf_op jit(solution)/shard_map/ppermute | solution.py:607
  54.7 2.6 %collective-permute-start.17 = (f32[64,128]{1,0:T(8,128)S(1)}, f32[64,128]{1,0:T(8,128)S(1)}, u32[]{:S(2)}, u32[]{:S(2)}) collective-permute-start(f32[64,128]{1,0:T(8,128)S(1)} %get-tuple-element.142.dir_cell.refs_0_.refs_22_), channel_id=1, source_target_pairs={{0,1},{1,2},{2,3},{3,4},{4,5},{5,6},{6,7},{7,0},{8,9},{9,10},{10,1... | collective-permute-start | bytes 98312 | tf_op jit(solution)/shard_map/ppermute | solution.py:607
  55.2 2.8 %collective-permute-start.16 = (f32[64,128]{1,0:T(8,128)S(1)}, f32[64,128]{1,0:T(8,128)S(1)}, u32[]{:S(2)}, u32[]{:S(2)}) collective-permute-start(f32[64,128]{1,0:T(8,128)S(1)} %get-tuple-element.142.dir_cell.refs_0_.refs_22_), channel_id=1, source_target_pairs={{0,248},{8,0},{16,8},{24,16},{32,24},{40,32},{48,40},{56,48},{64,5... | collective-permute-start | bytes 98312 | tf_op jit(solution)/shard_map/ppermute | solution.py:607
  55.6 6.1 %collective-permute-start.15 = (f32[64,128]{1,0:T(8,128)S(1)}, f32[64,128]{1,0:T(8,128)S(1)}, u32[]{:S(2)}, u32[]{:S(2)}) collective-permute-start(f32[64,128]{1,0:T(8,128)S(1)} %get-tuple-element.142.dir_cell.refs_0_.refs_22_), channel_id=1, source_target_pairs={{0,8},{8,16},{16,24},{24,32},{32,40},{40,48},{48,56},{56,64},{64,7... | collective-permute-start | bytes 98312 | tf_op jit(solution)/shard_map/ppermute | solution.py:607
  61.8 4.2 %collective-permute-start.22 = (f32[64,128]{1,0:T(8,128)S(1)}, f32[64,128]{1,0:T(8,128)S(1)}, u32[]{:S(2)}, u32[]{:S(2)}) collective-permute-start(f32[64,128]{1,0:T(8,128)S(1)} %get-tuple-element.147.dir_cell.refs_0_.refs_23_), channel_id=1, source_target_pairs={{0,7},{1,0},{2,1},{3,2},{4,3},{5,4},{6,5},{7,6},{8,15},{9,8},{10,9... | collective-permute-start | bytes 98312 | tf_op jit(solution)/shard_map/ppermute | solution.py:607
  63.9 2.8 %collective-permute-start.20 = (f32[64,128]{1,0:T(8,128)S(1)}, f32[64,128]{1,0:T(8,128)S(1)}, u32[]{:S(2)}, u32[]{:S(2)}) collective-permute-start(f32[64,128]{1,0:T(8,128)S(1)} %get-tuple-element.147.dir_cell.refs_0_.refs_23_), channel_id=1, source_target_pairs={{0,248},{8,0},{16,8},{24,16},{32,24},{40,32},{48,40},{56,48},{64,5... | collective-permute-start | bytes 98312 | tf_op jit(solution)/shard_map/ppermute | solution.py:607
  63.9 6.1 %collective-permute-start.19 = (f32[64,128]{1,0:T(8,128)S(1)}, f32[64,128]{1,0:T(8,128)S(1)}, u32[]{:S(2)}, u32[]{:S(2)}) collective-permute-start(f32[64,128]{1,0:T(8,128)S(1)} %get-tuple-element.147.dir_cell.refs_0_.refs_23_), channel_id=1, source_target_pairs={{0,8},{8,16},{16,24},{24,32},{32,40},{40,48},{48,56},{56,64},{64,7... | collective-permute-start | bytes 98312 | tf_op jit(solution)/shard_map/ppermute | solution.py:607
  70.1 5.0 %collective-permute-start.26 = (f32[64,128]{1,0:T(8,128)S(1)}, f32[64,128]{1,0:T(8,128)S(1)}, u32[]{:S(2)}, u32[]{:S(2)}) collective-permute-start(f32[64,128]{1,0:T(8,128)S(1)} %get-tuple-element.152.dir_cell.refs_0_.refs_24_), channel_id=1, source_target_pairs={{0,7},{1,0},{2,1},{3,2},{4,3},{5,4},{6,5},{7,6},{8,15},{9,8},{10,9... | collective-permute-start | bytes 98312 | tf_op jit(solution)/shard_map/ppermute | solution.py:607
  73.1 2.2 %collective-permute-start.25 = (f32[64,128]{1,0:T(8,128)S(1)}, f32[64,128]{1,0:T(8,128)S(1)}, u32[]{:S(2)}, u32[]{:S(2)}) collective-permute-start(f32[64,128]{1,0:T(8,128)S(1)} %get-tuple-element.152.dir_cell.refs_0_.refs_24_), channel_id=1, source_target_pairs={{0,1},{1,2},{2,3},{3,4},{4,5},{5,6},{6,7},{7,0},{8,9},{9,10},{10,1... | collective-permute-start | bytes 98312 | tf_op jit(solution)/shard_map/ppermute | solution.py:607
  73.1 2.8 %collective-permute-start.24 = (f32[64,128]{1,0:T(8,128)S(1)}, f32[64,128]{1,0:T(8,128)S(1)}, u32[]{:S(2)}, u32[]{:S(2)}) collective-permute-start(f32[64,128]{1,0:T(8,128)S(1)} %get-tuple-element.152.dir_cell.refs_0_.refs_24_), channel_id=1, source_target_pairs={{0,248},{8,0},{16,8},{24,16},{32,24},{40,32},{48,40},{56,48},{64,5... | collective-permute-start | bytes 98312 | tf_op jit(solution)/shard_map/ppermute | solution.py:607
  73.1 6.1 %collective-permute-start.23 = (f32[64,128]{1,0:T(8,128)S(1)}, f32[64,128]{1,0:T(8,128)S(1)}, u32[]{:S(2)}, u32[]{:S(2)}) collective-permute-start(f32[64,128]{1,0:T(8,128)S(1)} %get-tuple-element.152.dir_cell.refs_0_.refs_24_), channel_id=1, source_target_pairs={{0,8},{8,16},{16,24},{24,32},{32,40},{40,48},{48,56},{56,64},{64,7... | collective-permute-start | bytes 98312 | tf_op jit(solution)/shard_map/ppermute | solution.py:607
  79.3 5.0 %collective-permute-start.30 = (f32[64,128]{1,0:T(8,128)S(1)}, f32[64,128]{1,0:T(8,128)S(1)}, u32[]{:S(2)}, u32[]{:S(2)}) collective-permute-start(f32[64,128]{1,0:T(8,128)S(1)} %get-tuple-element.157.dir_cell.refs_0_.refs_25_), channel_id=1, source_target_pairs={{0,7},{1,0},{2,1},{3,2},{4,3},{5,4},{6,5},{7,6},{8,15},{9,8},{10,9... | collective-permute-start | bytes 98312 | tf_op jit(solution)/shard_map/ppermute | solution.py:607
  82.2 2.2 %collective-permute-start.29 = (f32[64,128]{1,0:T(8,128)S(1)}, f32[64,128]{1,0:T(8,128)S(1)}, u32[]{:S(2)}, u32[]{:S(2)}) collective-permute-start(f32[64,128]{1,0:T(8,128)S(1)} %get-tuple-element.157.dir_cell.refs_0_.refs_25_), channel_id=1, source_target_pairs={{0,1},{1,2},{2,3},{3,4},{4,5},{5,6},{6,7},{7,0},{8,9},{9,10},{10,1... | collective-permute-start | bytes 98312 | tf_op jit(solution)/shard_map/ppermute | solution.py:607
  82.2 2.8 %collective-permute-start.28 = (f32[64,128]{1,0:T(8,128)S(1)}, f32[64,128]{1,0:T(8,128)S(1)}, u32[]{:S(2)}, u32[]{:S(2)}) collective-permute-start(f32[64,128]{1,0:T(8,128)S(1)} %get-tuple-element.157.dir_cell.refs_0_.refs_25_), channel_id=1, source_target_pairs={{0,248},{8,0},{16,8},{24,16},{32,24},{40,32},{48,40},{56,48},{64,5... | collective-permute-start | bytes 98312 | tf_op jit(solution)/shard_map/ppermute | solution.py:607
  82.2 6.1 %collective-permute-start.27 = (f32[64,128]{1,0:T(8,128)S(1)}, f32[64,128]{1,0:T(8,128)S(1)}, u32[]{:S(2)}, u32[]{:S(2)}) collective-permute-start(f32[64,128]{1,0:T(8,128)S(1)} %get-tuple-element.157.dir_cell.refs_0_.refs_25_), channel_id=1, source_target_pairs={{0,8},{8,16},{16,24},{24,32},{32,40},{40,48},{48,56},{56,64},{64,7... | collective-permute-start | bytes 98312 | tf_op jit(solution)/shard_map/ppermute | solution.py:607
  111.1 3.8 %collective-permute-start.34 = (f32[64,128]{1,0:T(8,128)S(1)}, f32[64,128]{1,0:T(8,128)S(1)}, u32[]{:S(2)}, u32[]{:S(2)}) collective-permute-start(f32[64,128]{1,0:T(8,128)S(1)} %get-tuple-element.169.dir_cell.refs_0_.refs_5_), channel_id=1, source_target_pairs={{0,7},{1,0},{2,1},{3,2},{4,3},{5,4},{6,5},{7,6},{8,15},{9,8},{10,9... | collective-permute-start | bytes 98312 | tf_op jit(solution)/shard_map/ppermute | solution.py:607
  111.7 3.3 %collective-permute-start.33 = (f32[64,128]{1,0:T(8,128)S(1)}, f32[64,128]{1,0:T(8,128)S(1)}, u32[]{:S(2)}, u32[]{:S(2)}) collective-permute-start(f32[64,128]{1,0:T(8,128)S(1)} %get-tuple-element.169.dir_cell.refs_0_.refs_5_), channel_id=1, source_target_pairs={{0,1},{1,2},{2,3},{3,4},{4,5},{5,6},{6,7},{7,0},{8,9},{9,10},{10,1... | collective-permute-start | bytes 98312 | tf_op jit(solution)/shard_map/ppermute | solution.py:607
  112.9 3.1 %collective-permute-start.32 = (f32[64,128]{1,0:T(8,128)S(1)}, f32[64,128]{1,0:T(8,128)S(1)}, u32[]{:S(2)}, u32[]{:S(2)}) collective-permute-start(f32[64,128]{1,0:T(8,128)S(1)} %get-tuple-element.169.dir_cell.refs_0_.refs_5_), channel_id=1, source_target_pairs={{0,248},{8,0},{16,8},{24,16},{32,24},{40,32},{48,40},{56,48},{64,5... | collective-permute-start | bytes 98312 | tf_op jit(solution)/shard_map/ppermute | solution.py:607
  113.4 6.1 %collective-permute-start.31 = (f32[64,128]{1,0:T(8,128)S(1)}, f32[64,128]{1,0:T(8,128)S(1)}, u32[]{:S(2)}, u32[]{:S(2)}) collective-permute-start(f32[64,128]{1,0:T(8,128)S(1)} %get-tuple-element.169.dir_cell.refs_0_.refs_5_), channel_id=1, source_target_pairs={{0,8},{8,16},{16,24},{24,32},{32,40},{40,48},{48,56},{56,64},{64,7... | collective-permute-start | bytes 98312 | tf_op jit(solution)/shard_map/ppermute | solution.py:607
  119.7 3.8 %collective-permute-start.38 = (f32[64,128]{1,0:T(8,128)S(1)}, f32[64,128]{1,0:T(8,128)S(1)}, u32[]{:S(2)}, u32[]{:S(2)}) collective-permute-start(f32[64,128]{1,0:T(8,128)S(1)} %get-tuple-element.182.dir_cell.refs_0_.refs_6_), channel_id=1, source_target_pairs={{0,7},{1,0},{2,1},{3,2},{4,3},{5,4},{6,5},{7,6},{8,15},{9,8},{10,9... | collective-permute-start | bytes 98312 | tf_op jit(solution)/shard_map/ppermute | solution.py:607
  121.1 2.4 %collective-permute-start.37 = (f32[64,128]{1,0:T(8,128)S(1)}, f32[64,128]{1,0:T(8,128)S(1)}, u32[]{:S(2)}, u32[]{:S(2)}) collective-permute-start(f32[64,128]{1,0:T(8,128)S(1)} %get-tuple-element.182.dir_cell.refs_0_.refs_6_), channel_id=1, source_target_pairs={{0,1},{1,2},{2,3},{3,4},{4,5},{5,6},{6,7},{7,0},{8,9},{9,10},{10,1... | collective-permute-start | bytes 98312 | tf_op jit(solution)/shard_map/ppermute | solution.py:607
  121.4 2.8 %collective-permute-start.36 = (f32[64,128]{1,0:T(8,128)S(1)}, f32[64,128]{1,0:T(8,128)S(1)}, u32[]{:S(2)}, u32[]{:S(2)}) collective-permute-start(f32[64,128]{1,0:T(8,128)S(1)} %get-tuple-element.182.dir_cell.refs_0_.refs_6_), channel_id=1, source_target_pairs={{0,248},{8,0},{16,8},{24,16},{32,24},{40,32},{48,40},{56,48},{64,5... | collective-permute-start | bytes 98312 | tf_op jit(solution)/shard_map/ppermute | solution.py:607
  121.4 6.1 %collective-permute-start.35 = (f32[64,128]{1,0:T(8,128)S(1)}, f32[64,128]{1,0:T(8,128)S(1)}, u32[]{:S(2)}, u32[]{:S(2)}) collective-permute-start(f32[64,128]{1,0:T(8,128)S(1)} %get-tuple-element.182.dir_cell.refs_0_.refs_6_), channel_id=1, source_target_pairs={{0,8},{8,16},{16,24},{24,32},{32,40},{40,48},{48,56},{56,64},{64,7... | collective-permute-start | bytes 98312 | tf_op jit(solution)/shard_map/ppermute | solution.py:607
  127.6 4.7 %collective-permute-start.42 = (f32[64,128]{1,0:T(8,128)S(1)}, f32[64,128]{1,0:T(8,128)S(1)}, u32[]{:S(2)}, u32[]{:S(2)}) collective-permute-start(f32[64,128]{1,0:T(8,128)S(1)} %get-tuple-element.187.dir_cell.refs_0_.refs_7_), channel_id=1, source_target_pairs={{0,7},{1,0},{2,1},{3,2},{4,3},{5,4},{6,5},{7,6},{8,15},{9,8},{10,9... | collective-permute-start | bytes 98312 | tf_op jit(solution)/shard_map/ppermute | solution.py:607
  130.3 2.8 %collective-permute-start.40 = (f32[64,128]{1,0:T(8,128)S(1)}, f32[64,128]{1,0:T(8,128)S(1)}, u32[]{:S(2)}, u32[]{:S(2)}) collective-permute-start(f32[64,128]{1,0:T(8,128)S(1)} %get-tuple-element.187.dir_cell.refs_0_.refs_7_), channel_id=1, source_target_pairs={{0,248},{8,0},{16,8},{24,16},{32,24},{40,32},{48,40},{56,48},{64,5... | collective-permute-start | bytes 98312 | tf_op jit(solution)/shard_map/ppermute | solution.py:607
  130.3 6.1 %collective-permute-start.39 = (f32[64,128]{1,0:T(8,128)S(1)}, f32[64,128]{1,0:T(8,128)S(1)}, u32[]{:S(2)}, u32[]{:S(2)}) collective-permute-start(f32[64,128]{1,0:T(8,128)S(1)} %get-tuple-element.187.dir_cell.refs_0_.refs_7_), channel_id=1, source_target_pairs={{0,8},{8,16},{16,24},{24,32},{32,40},{40,48},{48,56},{56,64},{64,7... | collective-permute-start | bytes 98312 | tf_op jit(solution)/shard_map/ppermute | solution.py:607
  136.5 5.0 %collective-permute-start.46 = (f32[64,128]{1,0:T(8,128)S(1)}, f32[64,128]{1,0:T(8,128)S(1)}, u32[]{:S(2)}, u32[]{:S(2)}) collective-permute-start(f32[64,128]{1,0:T(8,128)S(1)} %get-tuple-element.192.dir_cell.refs_0_.refs_8_), channel_id=1, source_target_pairs={{0,7},{1,0},{2,1},{3,2},{4,3},{5,4},{6,5},{7,6},{8,15},{9,8},{10,9... | collective-permute-start | bytes 98312 | tf_op jit(solution)/shard_map/ppermute | solution.py:607
  139.5 2.8 %collective-permute-start.44 = (f32[64,128]{1,0:T(8,128)S(1)}, f32[64,128]{1,0:T(8,128)S(1)}, u32[]{:S(2)}, u32[]{:S(2)}) collective-permute-start(f32[64,128]{1,0:T(8,128)S(1)} %get-tuple-element.192.dir_cell.refs_0_.refs_8_), channel_id=1, source_target_pairs={{0,248},{8,0},{16,8},{24,16},{32,24},{40,32},{48,40},{56,48},{64,5... | collective-permute-start | bytes 98312 | tf_op jit(solution)/shard_map/ppermute | solution.py:607
  139.5 6.1 %collective-permute-start.43 = (f32[64,128]{1,0:T(8,128)S(1)}, f32[64,128]{1,0:T(8,128)S(1)}, u32[]{:S(2)}, u32[]{:S(2)}) collective-permute-start(f32[64,128]{1,0:T(8,128)S(1)} %get-tuple-element.192.dir_cell.refs_0_.refs_8_), channel_id=1, source_target_pairs={{0,8},{8,16},{16,24},{24,32},{32,40},{40,48},{48,56},{56,64},{64,7... | collective-permute-start | bytes 98312 | tf_op jit(solution)/shard_map/ppermute | solution.py:607
  145.7 5.0 %collective-permute-start.50 = (f32[64,128]{1,0:T(8,128)S(1)}, f32[64,128]{1,0:T(8,128)S(1)}, u32[]{:S(2)}, u32[]{:S(2)}) collective-permute-start(f32[64,128]{1,0:T(8,128)S(1)} %get-tuple-element.197.dir_cell.refs_0_.refs_9_), channel_id=1, source_target_pairs={{0,7},{1,0},{2,1},{3,2},{4,3},{5,4},{6,5},{7,6},{8,15},{9,8},{10,9... | collective-permute-start | bytes 98312 | tf_op jit(solution)/shard_map/ppermute | solution.py:607
  148.6 2.8 %collective-permute-start.48 = (f32[64,128]{1,0:T(8,128)S(1)}, f32[64,128]{1,0:T(8,128)S(1)}, u32[]{:S(2)}, u32[]{:S(2)}) collective-permute-start(f32[64,128]{1,0:T(8,128)S(1)} %get-tuple-element.197.dir_cell.refs_0_.refs_9_), channel_id=1, source_target_pairs={{0,248},{8,0},{16,8},{24,16},{32,24},{40,32},{48,40},{56,48},{64,5... | collective-permute-start | bytes 98312 | tf_op jit(solution)/shard_map/ppermute | solution.py:607
  148.6 6.1 %collective-permute-start.47 = (f32[64,128]{1,0:T(8,128)S(1)}, f32[64,128]{1,0:T(8,128)S(1)}, u32[]{:S(2)}, u32[]{:S(2)}) collective-permute-start(f32[64,128]{1,0:T(8,128)S(1)} %get-tuple-element.197.dir_cell.refs_0_.refs_9_), channel_id=1, source_target_pairs={{0,8},{8,16},{16,24},{24,32},{32,40},{40,48},{48,56},{56,64},{64,7... | collective-permute-start | bytes 98312 | tf_op jit(solution)/shard_map/ppermute | solution.py:607
  (10 other events, 87.9 us)

commit v4 on v3

--- a/solution.py
+++ b/solution.py
@@ -582,24 +582,32 @@
     out[...] = jnp.broadcast_to(total[None], out.shape)
 
 
+def address(*refs):
+    ids, seg, seg_old = refs[:3]
+    dir_segs, out = refs[3 : 3 + SWEEPS], refs[-1]
+    me = ids[1]
+    fields = [seg[...] - seg_old[...]] + [d[...] for d in dir_segs]
+    for n, field in enumerate(fields):
+        turned = jnp.concatenate(halves(field[:64], field[64:]), axis=0).T
+        for k in range(8):
+            owner = owner_of(k, me)
+            out[owner, 16 * n : 16 * n + 8] = turned[8 * k : 8 * k + 8]
+            out[owner, 16 * n + 8 : 16 * n + 16] = turned[64 + 8 * k : 64 + 8 * k + 8]
+
+
 def finish(*refs):
-    ids, parts, cell, seg, seg_old = refs[:5]
-    dir_cells = refs[5 : 5 + SWEEPS]
-    dir_segs = refs[5 + SWEEPS : 5 + 2 * SWEEPS]
-    cell_out, moved = refs[5 + 2 * SWEEPS :]
+    parts, cell, home = refs[:3]
+    dir_cells = refs[3 : 3 + SWEEPS]
+    cell_out, moved = refs[3 + SWEEPS :]
     factors = combine(summed(parts))
     total = cell[...]
-    shift = seg[...] - seg_old[...]
+    arrived = jnp.sum(home[...], axis=0)
+    shift = arrived[0:16]
     for j in range(SWEEPS):
         total = total + spread(factors[j], 64) * dir_cells[j][...]
-        shift = shift + spread(factors[j], 128) * dir_segs[j][...]
+        shift = shift + spread(factors[j], 16) * arrived[16 * j + 16 : 16 * j + 32]
     cell_out[...] = total
-    turned = jnp.concatenate(halves(shift[:64], shift[64:]), axis=0).T
-    me = ids[1]
-    for k in range(8):
-        owner = owner_of(k, me)
-        moved[owner, 0:8] = turned[8 * k : 8 * k + 8]
-        moved[owner, 8:16] = turned[64 + 8 * k : 64 + 8 * k + 8]
+    moved[...] = shift
 
 
 def ring(block, axis, distance):
@@ -818,6 +826,16 @@
                 lines,
                 couple_rows,
             ]
+            if last and newton == NEWTON - 1:
+                inflow, seg_now = after(inflow, seg)
+                [home] = call(
+                    address,
+                    [vmem(8, 16 * SWEEPS + 16, 128)],
+                    [ids, seg_now, seg_old, *dir_segs],
+                    "S" + "v" * (2 + SWEEPS),
+                    name="address",
+                )
+                home = lax.all_to_all(home, "frac", 0, 0)
             made = call(
                 lambda *refs, last=last: advance(last, *refs),
                 [vmem(64, 128), vmem(128, 128)] * (1 if last else 2),
@@ -825,6 +843,9 @@
                 "v" * len(args),
                 name="advance",
             )
+            if last and newton == NEWTON - 1:
+                made = list(after(*made, home))
+                home = made.pop()
             base_cells.append(made[0])
             base_segs.append(made[1])
             if not last:
@@ -838,15 +859,14 @@
         )
         parts = lax.all_to_all(parts, ("region", "frac"), 0, 0)
 
-    args = [ids, parts, cell, seg, seg_old, *dir_cells, *dir_segs]
+    args = [parts, cell, home, *dir_cells]
     cell_state, moved = call(
         finish,
-        [jax.ShapeDtypeStruct((64, 128), F32), vmem(8, 16, 128)],
+        [jax.ShapeDtypeStruct((64, 128), F32), vmem(16, 128)],
         args,
-        "S" + "v" * (len(args) - 1),
+        "v" * len(args),
         name="finish",
     )
-    moved = jnp.sum(lax.all_to_all(moved, "frac", 0, 0), axis=0)
     seg_state = jnp.stack([frac_pres_old, frac_satur_old]) + moved.reshape(2, -1)
     return (cell_state.reshape(2, 1, 32, 128), seg_state)
 

time: 186 us -> 185 us (level)
  blocking collectives: 50.2 us -> 41.7 us
  starting transfers between devices: 64.7 us -> 71 us
  waiting for transfers between devices: 49.3 us -> 52.7 us
    all_to_all x1 -> x0, blocking collectives: 7.93 us -> none  [on_device(): moved = jnp.sum(lax.all_to_all(moved, 'frac', 0, 0), axis=0)]
    all_to_all x0 -> x1, starting transfers between devices: none -> 6.68 us  [on_device(): home = lax.all_to_all(home, 'frac', 0, 0)]
    ppermute x46, waiting for transfers between devices: 49.3 us -> 52.5 us  [ring(): lax.ppermute(block, axis, [(i, (i + distance) % count) for i in range(cou...]
    pallas_call x29 -> x30, Pallas kernels: 18.3 us -> 16.6 us  [call(): pl.pallas_call(body, out_shape=list(outs), in_specs=[pl.BlockSpec(memory_...]
  transfers between devices with their start and end apart: 52 -> 53, of which waited for: 29 -> 28; matrix products, arithmetic and copies ran while one was open for 0% -> 0% of each run, Pallas kernels for 5% -> 4%
where the time goes in v4:
time: 185 us; the launch traced here: 186 us
  starting transfers between devices  71 us (38%)
  waiting for transfers between devices  52.7 us (28%)
  blocking collectives  41.7 us (23%)
  Pallas kernels  16.6 us (9%)
    ppermute x46, starting transfers between devices, ring(): lax.ppermute(block, axis, [(i, (i + distance) % count) for i in range(cou...  55.2 us
    ppermute x46, waiting for transfers between devices, ring(): lax.ppermute(block, axis, [(i, (i + distance) % count) for i in range(cou...  52.5 us
    all_to_all x2, blocking collectives, on_device(): parts = lax.all_to_all(parts, ('region', 'frac'), 0, 0)  41.7 us
    pallas_call x30, Pallas kernels, call(): pl.pallas_call(body, out_shape=list(outs), in_specs=[pl.BlockSpec(memory_...  16.6 us
    all_to_all x1, starting transfers between devices, on_device(): home = lax.all_to_all(home, 'frac', 0, 0)  6.68 us
    all_to_all x1, starting transfers between devices, on_device(): records = lax.all_to_all(record, 'frac', 0, 0).reshape(448, 128)  5.47 us
  transfers between devices with their start and end apart: 53, of which 28 were waited for; matrix products, arithmetic and copies ran while one was open for 0% of the time, Pallas kernels for 4%

profile of v4, /device:TPU:1, one launch (start us, length us, event | category | flops | bytes accessed | tf_op | source)
XLA Modules:
  0.0 185.7 jit_solution(14882640740357842129)
XLA Ops:
  0.6 3.4 %collective-permute-start.1 = (f32[16,64,128]{2,1,0:T(8,128)}, f32[16,64,128]{2,1,0:T(8,128)S(1)}, u32[]{:S(2)}, u32[]{:S(2)}) collective-permute-start(f32[16,64,128]{2,1,0:T(8,128)} %refs_0_.1), channel_id=1, source_target_pairs={{0,6},{1,7},{2,0},{3,1},{4,2},{5,3},{6,4},{7,5},{8,14},{9,15},{10,... | collective-permute-start | bytes 1572872 | tf_op jit(solution)/shard_map/ppermute | solution.py:615
  6.1 2.3 %pack.1 = (s32[4]{0:T(128)S(4)}, f32[160,128]{1,0:T(8,128)S(1)}, f32[8,56,128]{2,1,0:T(8,128)}, f32[64,128]{1,0:T(8,128)S(1)}, f32[32,128]{1,0:T(8,128)S(1)}) custom-call(s32[4]{0:T(128)S(1)} %pad_add_fusion.ids, s32[16]{0:T(128)S(1)} %copy-done.2, s32[16]{0:T(128)S(1)} %copy-done.3, s32[1]{0:T(128)S(6)} %copy.18.live, f32[1,32,128]{2,1,0:T(8,128)} %pres.1, ...), custom_call_target="tpu_custom_call" | custom-call | flops 20000 | bytes 20000 | tf_op jit(solution)/shard_map/pack/pallas_call | solution.py:39
  8.4 5.5 %all-to-all-start = ((f32[8,56,128]{2,1,0:T(8,128)}), f32[8,56,128]{2,1,0:T(8,128)S(1)}, u32[]{:S(2)}, u32[]{:S(2)}) async-start(f32[8,56,128]{2,1,0:T(8,128)} %get-tuple-element.112), calls=%async_computation | async-start | bytes 458752 | tf_op jit(solution)/shard_map/all_to_all | solution.py:688
  13.8 8.0 %collective-permute-start.3 = (f32[160,128]{1,0:T(8,128)S(1)}, f32[160,128]{1,0:T(8,128)S(1)}, u32[]{:S(2)}, u32[]{:S(2)}) collective-permute-start(f32[160,128]{1,0:T(8,128)S(1)} %get-tuple-element.118.own), channel_id=1, source_target_pairs={{0,248},{8,0},{16,8},{24,16},{32,24},{40,32},{48,40},{56,48},{64,5... | collective-permute-start | bytes 245768 | tf_op jit(solution)/shard_map/ppermute | solution.py:615
  22.2 3.0 %collective-permute-start.5 = (f32[8,64,128]{2,1,0:T(8,128)S(1)}, f32[8,64,128]{2,1,0:T(8,128)S(1)}, u32[]{:S(2)}, u32[]{:S(2)}) collective-permute-start(f32[8,64,128]{2,1,0:T(8,128)S(1)} %slice.7), channel_id=1, source_target_pairs={{0,6},{1,7},{2,0},{3,1},{4,2},{5,3},{6,4},{7,5},{8,14},{9,15},{10,... | collective-permute-start | bytes 786440 | tf_op jit(solution)/shard_map/ppermute | solution.py:615
  25.6 3.4 %collective-permute-done.2.below.refs_15_ = f32[160,128]{1,0:T(8,128)S(1)} collective-permute-done((f32[160,128]{1,0:T(8,128)S(1)}, f32[160,128]{1,0:T(8,128)S(1)}, u32[]{:S(2)}, u32[]{:S(2)}) %collective-permute-start.2) | collective-permute-done | bytes 81952 | tf_op jit(solution)/shard_map/ppermute | solution.py:615
  28.9 1.1 collective-permute-start.10
  30.0 0.9 collective-permute-done.5.refs_3_
  31.8 2.3 %collective-permute-done.4.refs_2_ = f32[8,64,128]{2,1,0:T(8,128)S(1)} collective-permute-done((f32[8,64,128]{2,1,0:T(8,128)S(1)}, f32[8,64,128]{2,1,0:T(8,128)S(1)}, u32[]{:S(2)}, u32[]{:S(2)}) %collective-permute-start.4) | collective-permute-done | bytes 262176 | tf_op jit(solution)/shard_map/ppermute | solution.py:615
  34.1 1.1 collective-permute-start.8
  35.2 1.6 survey.1
  37.0 2.7 %collect.1.refs_13_.weights = f32[132,64,128]{2,1,0:T(8,128)S(1)} custom-call(s32[132]{0:T(256)S(4)} %get-tuple-element.129.places, s32[1]{0:T(128)S(4)} %get-tuple-element.116.count.refs_2_, f32[16,64,128]{2,1,0:T(8,128)} %refs_0_.1, f32[16,64,128]{2,1,0:T(8,128)S(1)} %collective-permute-done.refs_1_, f32[8,64,128]{2,1,0:T(8,128)S(1)} %collective-permute-done.4.refs_2_, ...), custom_call_target="tpu_custom_call" | custom-call | flops 20000 | bytes 20000 | tf_op jit(solution)/shard_map/collect/pallas_call | solution.py:39
  40.4 1.3 collective-permute-start.14
  42.2 6.3 %collective-permute-start.12 = (f32[64,128]{1,0:T(8,128)S(1)}, f32[64,128]{1,0:T(8,128)S(1)}, u32[]{:S(2)}, u32[]{:S(2)}) collective-permute-start(f32[64,128]{1,0:T(8,128)S(1)} %get-tuple-element.133.dir_cell.refs_0_.refs_21_), channel_id=1, source_target_pairs={{0,248},{8,0},{16,8},{24,16},{32,24},{40,32},{48,40},{56,48},{64,5... | collective-permute-start | bytes 98312 | tf_op jit(solution)/shard_map/ppermute | solution.py:615
  49.5 5.1 %collective-permute-done.11.refs_1_.refs_31_ = f32[64,128]{1,0:T(8,128)S(1)} collective-permute-done((f32[64,128]{1,0:T(8,128)S(1)}, f32[64,128]{1,0:T(8,128)S(1)}, u32[]{:S(2)}, u32[]{:S(2)}) %collective-permute-start.11) | collective-permute-done | bytes 32800 | tf_op jit(solution)/shard_map/ppermute | solution.py:615
  54.7 1.5 collective-permute-start.18
  56.5 1.5 collective-permute-start.15
  59.2 3.3 %collective-permute-done.15.refs_1_.refs_35_ = f32[64,128]{1,0:T(8,128)S(1)} collective-permute-done((f32[64,128]{1,0:T(8,128)S(1)}, f32[64,128]{1,0:T(8,128)S(1)}, u32[]{:S(2)}, u32[]{:S(2)}) %collective-permute-start.15) | collective-permute-done | bytes 32800 | tf_op jit(solution)/shard_map/ppermute | solution.py:615
  62.7 2.2 %collective-permute-start.22 = (f32[64,128]{1,0:T(8,128)S(1)}, f32[64,128]{1,0:T(8,128)S(1)}, u32[]{:S(2)}, u32[]{:S(2)}) collective-permute-start(f32[64,128]{1,0:T(8,128)S(1)} %get-tuple-element.151.dir_cell.refs_0_.refs_23_), channel_id=1, source_target_pairs={{0,7},{1,0},{2,1},{3,2},{4,3},{5,4},{6,5},{7,6},{8,15},{9,8},{10,9... | collective-permute-start | bytes 98312 | tf_op jit(solution)/shard_map/ppermute | solution.py:615
  64.9 1.5 collective-permute-start.19
  67.7 3.3 %collective-permute-done.19.refs_1_.refs_39_ = f32[64,128]{1,0:T(8,128)S(1)} collective-permute-done((f32[64,128]{1,0:T(8,128)S(1)}, f32[64,128]{1,0:T(8,128)S(1)}, u32[]{:S(2)}, u32[]{:S(2)}) %collective-permute-start.19) | collective-permute-done | bytes 32800 | tf_op jit(solution)/shard_map/ppermute | solution.py:615
  71.1 3.0 %collective-permute-start.26 = (f32[64,128]{1,0:T(8,128)S(1)}, f32[64,128]{1,0:T(8,128)S(1)}, u32[]{:S(2)}, u32[]{:S(2)}) collective-permute-start(f32[64,128]{1,0:T(8,128)S(1)} %get-tuple-element.156.dir_cell.refs_0_.refs_24_), channel_id=1, source_target_pairs={{0,7},{1,0},{2,1},{3,2},{4,3},{5,4},{6,5},{7,6},{8,15},{9,8},{10,9... | collective-permute-start | bytes 98312 | tf_op jit(solution)/shard_map/ppermute | solution.py:615
  74.1 1.5 collective-permute-start.23
  76.9 3.3 %collective-permute-done.23.refs_1_.refs_43_ = f32[64,128]{1,0:T(8,128)S(1)} collective-permute-done((f32[64,128]{1,0:T(8,128)S(1)}, f32[64,128]{1,0:T(8,128)S(1)}, u32[]{:S(2)}, u32[]{:S(2)}) %collective-permute-start.23) | collective-permute-done | bytes 32800 | tf_op jit(solution)/shard_map/ppermute | solution.py:615
  80.3 3.0 %collective-permute-start.30 = (f32[64,128]{1,0:T(8,128)S(1)}, f32[64,128]{1,0:T(8,128)S(1)}, u32[]{:S(2)}, u32[]{:S(2)}) collective-permute-start(f32[64,128]{1,0:T(8,128)S(1)} %get-tuple-element.161.dir_cell.refs_0_.refs_25_), channel_id=1, source_target_pairs={{0,7},{1,0},{2,1},{3,2},{4,3},{5,4},{6,5},{7,6},{8,15},{9,8},{10,9... | collective-permute-start | bytes 98312 | tf_op jit(solution)/shard_map/ppermute | solution.py:615
  83.3 1.5 collective-permute-start.27
  86.1 3.3 %collective-permute-done.27.refs_1_.refs_47_ = f32[64,128]{1,0:T(8,128)S(1)} collective-permute-done((f32[64,128]{1,0:T(8,128)S(1)}, f32[64,128]{1,0:T(8,128)S(1)}, u32[]{:S(2)}, u32[]{:S(2)}) %collective-permute-start.27) | collective-permute-done | bytes 32800 | tf_op jit(solution)/shard_map/ppermute | solution.py:615
  89.9 20.8 %all_to_all.20.refs_20_ = f32[256,1,128]{2,1,0:T(1,128)S(1)} all-to-all(f32[256,1,128]{2,1,0:T(1,128)S(1)} %inner_products.2), channel_id=1, replica_groups=mesh['region'=32,'frac'=8] {'region','frac'}, dimensions={0} | all-to-all | bytes 262144 | tf_op jit(solution)/shard_map/all_to_all | solution.py:860
  110.7 1.3 linearise.3
  111.9 1.0 collective-permute-start.34
  113.7 1.3 collective-permute-start.32
  116.4 4.6 %collective-permute-done.31.refs_1_ = f32[64,128]{1,0:T(8,128)S(1)} collective-permute-done((f32[64,128]{1,0:T(8,128)S(1)}, f32[64,128]{1,0:T(8,128)S(1)}, u32[]{:S(2)}, u32[]{:S(2)}) %collective-permute-start.31) | collective-permute-done | bytes 32800 | tf_op jit(solution)/shard_map/ppermute | solution.py:615
  121.2 1.1 collective-permute-start.38
  123.4 1.0 collective-permute-start.35
  125.7 3.8 %collective-permute-done.35.refs_1_ = f32[64,128]{1,0:T(8,128)S(1)} collective-permute-done((f32[64,128]{1,0:T(8,128)S(1)}, f32[64,128]{1,0:T(8,128)S(1)}, u32[]{:S(2)}, u32[]{:S(2)}) %collective-permute-start.35) | collective-permute-done | bytes 32800 | tf_op jit(solution)/shard_map/ppermute | solution.py:615
  129.6 1.4 collective-permute-start.42
  131.4 1.5 collective-permute-start.39
  134.2 3.3 %collective-permute-done.39.refs_1_ = f32[64,128]{1,0:T(8,128)S(1)} collective-permute-done((f32[64,128]{1,0:T(8,128)S(1)}, f32[64,128]{1,0:T(8,128)S(1)}, u32[]{:S(2)}, u32[]{:S(2)}) %collective-permute-start.39) | collective-permute-done | bytes 32800 | tf_op jit(solution)/shard_map/ppermute | solution.py:615
  137.6 2.6 %collective-permute-start.46 = (f32[64,128]{1,0:T(8,128)S(1)}, f32[64,128]{1,0:T(8,128)S(1)}, u32[]{:S(2)}, u32[]{:S(2)}) collective-permute-start(f32[64,128]{1,0:T(8,128)S(1)} %get-tuple-element.196.dir_cell.refs_0_.refs_6_), channel_id=1, source_target_pairs={{0,7},{1,0},{2,1},{3,2},{4,3},{5,4},{6,5},{7,6},{8,15},{9,8},{10,9... | collective-permute-start | bytes 98312 | tf_op jit(solution)/shard_map/ppermute | solution.py:615
  140.2 1.5 collective-permute-start.43
  143.0 3.3 %collective-permute-done.43.refs_1_ = f32[64,128]{1,0:T(8,128)S(1)} collective-permute-done((f32[64,128]{1,0:T(8,128)S(1)}, f32[64,128]{1,0:T(8,128)S(1)}, u32[]{:S(2)}, u32[]{:S(2)}) %collective-permute-start.43) | collective-permute-done | bytes 32800 | tf_op jit(solution)/shard_map/ppermute | solution.py:615
  146.9 1.1 address.1
  147.9 6.7 %all-to-all-start.2 = ((f32[8,96,128]{2,1,0:T(8,128)}), f32[8,96,128]{2,1,0:T(8,128)S(1)}, u32[]{:S(2)}, u32[]{:S(2)}) async-start(f32[8,96,128]{2,1,0:T(8,128)} %address.1), calls=%async_computation.2 | async-start | bytes 786432 | tf_op jit(solution)/shard_map/all_to_all | solution.py:838
  154.7 1.6 collective-permute-start.49
  156.4 1.4 collective-permute-start.47
  157.8 4.2 %collective-permute-done.50.refs_4_ = f32[64,128]{1,0:T(8,128)S(1)} collective-permute-done((f32[64,128]{1,0:T(8,128)S(1)}, f32[64,128]{1,0:T(8,128)S(1)}, u32[]{:S(2)}, u32[]{:S(2)}) %collective-permute-start.50) | collective-permute-done | bytes 32800 | tf_op jit(solution)/shard_map/ppermute | solution.py:615
  163.1 20.9 %all_to_all.21.refs_0_ = f32[256,1,128]{2,1,0:T(1,128)S(1)} all-to-all(f32[256,1,128]{2,1,0:T(1,128)S(1)} %inner_products.3), channel_id=1, replica_groups=mesh['region'=32,'frac'=8] {'region','frac'}, dimensions={0} | all-to-all | bytes 262144 | tf_op jit(solution)/shard_map/all_to_all | solution.py:860
  184.0 1.1 finish.1
  (107 shorter events, 21.8 us)
Async XLA Ops:
  0.6 21.5 %collective-permute-start.1 = (f32[16,64,128]{2,1,0:T(8,128)}, f32[16,64,128]{2,1,0:T(8,128)S(1)}, u32[]{:S(2)}, u32[]{:S(2)}) collective-permute-start(f32[16,64,128]{2,1,0:T(8,128)} %refs_0_.1), channel_id=1, source_target_pairs={{0,6},{1,7},{2,0},{3,1},{4,2},{5,3},{6,4},{7,5},{8,14},{9,15},{10,... | collective-permute-start | bytes 1572872 | tf_op jit(solution)/shard_map/ppermute | solution.py:615
  4.0 18.1 %collective-permute-start = (f32[16,64,128]{2,1,0:T(8,128)}, f32[16,64,128]{2,1,0:T(8,128)S(1)}, u32[]{:S(2)}, u32[]{:S(2)}) collective-permute-start(f32[16,64,128]{2,1,0:T(8,128)} %refs_0_.1), channel_id=1, source_target_pairs={{0,2},{1,3},{2,4},{3,5},{4,6},{5,7},{6,0},{7,1},{8,10},{9,11},{10,... | collective-permute-start | bytes 1572872 | tf_op jit(solution)/shard_map/ppermute | solution.py:615
  8.4 13.8 %all-to-all-start = ((f32[8,56,128]{2,1,0:T(8,128)}), f32[8,56,128]{2,1,0:T(8,128)S(1)}, u32[]{:S(2)}, u32[]{:S(2)}) async-start(f32[8,56,128]{2,1,0:T(8,128)} %get-tuple-element.112), calls=%async_computation | async-start | bytes 458752 | tf_op jit(solution)/shard_map/all_to_all | solution.py:688
  13.8 11.4 %collective-permute-start.3 = (f32[160,128]{1,0:T(8,128)S(1)}, f32[160,128]{1,0:T(8,128)S(1)}, u32[]{:S(2)}, u32[]{:S(2)}) collective-permute-start(f32[160,128]{1,0:T(8,128)S(1)} %get-tuple-element.118.own), channel_id=1, source_target_pairs={{0,248},{8,0},{16,8},{24,16},{32,24},{40,32},{48,40},{56,48},{64,5... | collective-permute-start | bytes 245768 | tf_op jit(solution)/shard_map/ppermute | solution.py:615
  21.9 7.1 %collective-permute-start.2 = (f32[160,128]{1,0:T(8,128)S(1)}, f32[160,128]{1,0:T(8,128)S(1)}, u32[]{:S(2)}, u32[]{:S(2)}) collective-permute-start(f32[160,128]{1,0:T(8,128)S(1)} %get-tuple-element.118.own), channel_id=1, source_target_pairs={{0,8},{8,16},{16,24},{24,32},{32,40},{40,48},{48,56},{56,64},{64,7... | collective-permute-start | bytes 245768 | tf_op jit(solution)/shard_map/ppermute | solution.py:615
  21.9 15.1 %collective-permute-start.6 = (f32[16,64,128]{2,1,0:T(8,128)}, f32[16,64,128]{2,1,0:T(8,128)S(1)}, u32[]{:S(2)}, u32[]{:S(2)}) collective-permute-start(f32[16,64,128]{2,1,0:T(8,128)} %refs_0_.1), channel_id=1, source_target_pairs={{0,1},{1,0},{2,3},{3,2},{4,5},{5,4},{6,7},{7,6},{8,9},{9,8},{10,11... | collective-permute-start | bytes 1572872 | tf_op jit(solution)/shard_map/ppermute | solution.py:619
  22.2 8.8 %collective-permute-start.5 = (f32[8,64,128]{2,1,0:T(8,128)S(1)}, f32[8,64,128]{2,1,0:T(8,128)S(1)}, u32[]{:S(2)}, u32[]{:S(2)}) collective-permute-start(f32[8,64,128]{2,1,0:T(8,128)S(1)} %slice.7), channel_id=1, source_target_pairs={{0,6},{1,7},{2,0},{3,1},{4,2},{5,3},{6,4},{7,5},{8,14},{9,15},{10,... | collective-permute-start | bytes 786440 | tf_op jit(solution)/shard_map/ppermute | solution.py:615
  25.3 8.8 %collective-permute-start.4 = (f32[8,64,128]{2,1,0:T(8,128)S(1)}, f32[8,64,128]{2,1,0:T(8,128)S(1)}, u32[]{:S(2)}, u32[]{:S(2)}) collective-permute-start(f32[8,64,128]{2,1,0:T(8,128)S(1)} %slice.6), channel_id=1, source_target_pairs={{0,2},{1,3},{2,4},{3,5},{4,6},{5,7},{6,0},{7,1},{8,10},{9,11},{10,... | collective-permute-start | bytes 786440 | tf_op jit(solution)/shard_map/ppermute | solution.py:615
  25.3 11.7 %collective-permute-start.7 = (f32[16,64,128]{2,1,0:T(8,128)S(1)}, f32[16,64,128]{2,1,0:T(8,128)S(1)}, u32[]{:S(2)}, u32[]{:S(2)}) collective-permute-start(f32[16,64,128]{2,1,0:T(8,128)S(1)} %collective-permute-done.refs_1_), channel_id=1, source_target_pairs={{0,1},{1,0},{2,3},{3,2},{4,5},{5,4},{6,7},{7,6},{8,9},{9,8},{10,11... | collective-permute-start | bytes 1572872 | tf_op jit(solution)/shard_map/ppermute | solution.py:619
  28.9 8.0 %collective-permute-start.10 = (f32[16,64,128]{2,1,0:T(8,128)S(1)}, f32[16,64,128]{2,1,0:T(8,128)S(1)}, u32[]{:S(2)}, u32[]{:S(2)}) collective-permute-start(f32[16,64,128]{2,1,0:T(8,128)S(1)} %collective-permute-done.1.refs_4_), channel_id=1, source_target_pairs={{0,1},{1,0},{2,3},{3,2},{4,5},{5,4},{6,7},{7,6},{8,9},{9,8},{10,11... | collective-permute-start | bytes 1572872 | tf_op jit(solution)/shard_map/ppermute | solution.py:619
  31.0 6.0 %collective-permute-start.9 = (f32[8,64,128]{2,1,0:T(8,128)S(1)}, f32[8,64,128]{2,1,0:T(8,128)S(1)}, u32[]{:S(2)}, u32[]{:S(2)}) collective-permute-start(f32[8,64,128]{2,1,0:T(8,128)S(1)} %collective-permute-done.5.refs_3_), channel_id=1, source_target_pairs={{0,1},{1,0},{2,3},{3,2},{4,5},{5,4},{6,7},{7,6},{8,9},{9,8},{10,11... | collective-permute-start | bytes 786440 | tf_op jit(solution)/shard_map/ppermute | solution.py:619
  34.1 2.9 %collective-permute-start.8 = (f32[8,64,128]{2,1,0:T(8,128)S(1)}, f32[8,64,128]{2,1,0:T(8,128)S(1)}, u32[]{:S(2)}, u32[]{:S(2)}) collective-permute-start(f32[8,64,128]{2,1,0:T(8,128)S(1)} %collective-permute-done.4.refs_2_), channel_id=1, source_target_pairs={{0,1},{1,0},{2,3},{3,2},{4,5},{5,4},{6,7},{7,6},{8,9},{9,8},{10,11... | collective-permute-start | bytes 786440 | tf_op jit(solution)/shard_map/ppermute | solution.py:619
  40.4 8.5 %collective-permute-start.14 = (f32[64,128]{1,0:T(8,128)S(1)}, f32[64,128]{1,0:T(8,128)S(1)}, u32[]{:S(2)}, u32[]{:S(2)}) collective-permute-start(f32[64,128]{1,0:T(8,128)S(1)} %get-tuple-element.133.dir_cell.refs_0_.refs_21_), channel_id=1, source_target_pairs={{0,7},{1,0},{2,1},{3,2},{4,3},{5,4},{6,5},{7,6},{8,15},{9,8},{10,9... | collective-permute-start | bytes 98312 | tf_op jit(solution)/shard_map/ppermute | solution.py:615
  41.7 7.2 %collective-permute-start.13 = (f32[64,128]{1,0:T(8,128)S(1)}, f32[64,128]{1,0:T(8,128)S(1)}, u32[]{:S(2)}, u32[]{:S(2)}) collective-permute-start(f32[64,128]{1,0:T(8,128)S(1)} %get-tuple-element.133.dir_cell.refs_0_.refs_21_), channel_id=1, source_target_pairs={{0,1},{1,2},{2,3},{3,4},{4,5},{5,6},{6,7},{7,0},{8,9},{9,10},{10,1... | collective-permute-start | bytes 98312 | tf_op jit(solution)/shard_map/ppermute | solution.py:615
  42.2 7.3 %collective-permute-start.12 = (f32[64,128]{1,0:T(8,128)S(1)}, f32[64,128]{1,0:T(8,128)S(1)}, u32[]{:S(2)}, u32[]{:S(2)}) collective-permute-start(f32[64,128]{1,0:T(8,128)S(1)} %get-tuple-element.133.dir_cell.refs_0_.refs_21_), channel_id=1, source_target_pairs={{0,248},{8,0},{16,8},{24,16},{32,24},{40,32},{48,40},{56,48},{64,5... | collective-permute-start | bytes 98312 | tf_op jit(solution)/shard_map/ppermute | solution.py:615
  48.5 6.1 %collective-permute-start.11 = (f32[64,128]{1,0:T(8,128)S(1)}, f32[64,128]{1,0:T(8,128)S(1)}, u32[]{:S(2)}, u32[]{:S(2)}) collective-permute-start(f32[64,128]{1,0:T(8,128)S(1)} %get-tuple-element.133.dir_cell.refs_0_.refs_21_), channel_id=1, source_target_pairs={{0,8},{8,16},{16,24},{24,32},{32,40},{40,48},{48,56},{56,64},{64,7... | collective-permute-start | bytes 98312 | tf_op jit(solution)/shard_map/ppermute | solution.py:615
  54.7 3.6 %collective-permute-start.18 = (f32[64,128]{1,0:T(8,128)S(1)}, f32[64,128]{1,0:T(8,128)S(1)}, u32[]{:S(2)}, u32[]{:S(2)}) collective-permute-start(f32[64,128]{1,0:T(8,128)S(1)} %get-tuple-element.146.dir_cell.refs_0_.refs_22_), channel_id=1, source_target_pairs={{0,7},{1,0},{2,1},{3,2},{4,3},{5,4},{6,5},{7,6},{8,15},{9,8},{10,9... | collective-permute-start | bytes 98312 | tf_op jit(solution)/shard_map/ppermute | solution.py:615
  56.5 2.8 %collective-permute-start.16 = (f32[64,128]{1,0:T(8,128)S(1)}, f32[64,128]{1,0:T(8,128)S(1)}, u32[]{:S(2)}, u32[]{:S(2)}) collective-permute-start(f32[64,128]{1,0:T(8,128)S(1)} %get-tuple-element.146.dir_cell.refs_0_.refs_22_), channel_id=1, source_target_pairs={{0,248},{8,0},{16,8},{24,16},{32,24},{40,32},{48,40},{56,48},{64,5... | collective-permute-start | bytes 98312 | tf_op jit(solution)/shard_map/ppermute | solution.py:615
  56.5 6.1 %collective-permute-start.15 = (f32[64,128]{1,0:T(8,128)S(1)}, f32[64,128]{1,0:T(8,128)S(1)}, u32[]{:S(2)}, u32[]{:S(2)}) collective-permute-start(f32[64,128]{1,0:T(8,128)S(1)} %get-tuple-element.146.dir_cell.refs_0_.refs_22_), channel_id=1, source_target_pairs={{0,8},{8,16},{16,24},{24,32},{32,40},{40,48},{48,56},{56,64},{64,7... | collective-permute-start | bytes 98312 | tf_op jit(solution)/shard_map/ppermute | solution.py:615
  62.7 4.1 %collective-permute-start.22 = (f32[64,128]{1,0:T(8,128)S(1)}, f32[64,128]{1,0:T(8,128)S(1)}, u32[]{:S(2)}, u32[]{:S(2)}) collective-permute-start(f32[64,128]{1,0:T(8,128)S(1)} %get-tuple-element.151.dir_cell.refs_0_.refs_23_), channel_id=1, source_target_pairs={{0,7},{1,0},{2,1},{3,2},{4,3},{5,4},{6,5},{7,6},{8,15},{9,8},{10,9... | collective-permute-start | bytes 98312 | tf_op jit(solution)/shard_map/ppermute | solution.py:615
  64.9 2.8 %collective-permute-start.20 = (f32[64,128]{1,0:T(8,128)S(1)}, f32[64,128]{1,0:T(8,128)S(1)}, u32[]{:S(2)}, u32[]{:S(2)}) collective-permute-start(f32[64,128]{1,0:T(8,128)S(1)} %get-tuple-element.151.dir_cell.refs_0_.refs_23_), channel_id=1, source_target_pairs={{0,248},{8,0},{16,8},{24,16},{32,24},{40,32},{48,40},{56,48},{64,5... | collective-permute-start | bytes 98312 | tf_op jit(solution)/shard_map/ppermute | solution.py:615
  64.9 6.1 %collective-permute-start.19 = (f32[64,128]{1,0:T(8,128)S(1)}, f32[64,128]{1,0:T(8,128)S(1)}, u32[]{:S(2)}, u32[]{:S(2)}) collective-permute-start(f32[64,128]{1,0:T(8,128)S(1)} %get-tuple-element.151.dir_cell.refs_0_.refs_23_), channel_id=1, source_target_pairs={{0,8},{8,16},{16,24},{24,32},{32,40},{40,48},{48,56},{56,64},{64,7... | collective-permute-start | bytes 98312 | tf_op jit(solution)/shard_map/ppermute | solution.py:615
  71.1 4.8 %collective-permute-start.26 = (f32[64,128]{1,0:T(8,128)S(1)}, f32[64,128]{1,0:T(8,128)S(1)}, u32[]{:S(2)}, u32[]{:S(2)}) collective-permute-start(f32[64,128]{1,0:T(8,128)S(1)} %get-tuple-element.156.dir_cell.refs_0_.refs_24_), channel_id=1, source_target_pairs={{0,7},{1,0},{2,1},{3,2},{4,3},{5,4},{6,5},{7,6},{8,15},{9,8},{10,9... | collective-permute-start | bytes 98312 | tf_op jit(solution)/shard_map/ppermute | solution.py:615
  74.1 2.8 %collective-permute-start.24 = (f32[64,128]{1,0:T(8,128)S(1)}, f32[64,128]{1,0:T(8,128)S(1)}, u32[]{:S(2)}, u32[]{:S(2)}) collective-permute-start(f32[64,128]{1,0:T(8,128)S(1)} %get-tuple-element.156.dir_cell.refs_0_.refs_24_), channel_id=1, source_target_pairs={{0,248},{8,0},{16,8},{24,16},{32,24},{40,32},{48,40},{56,48},{64,5... | collective-permute-start | bytes 98312 | tf_op jit(solution)/shard_map/ppermute | solution.py:615
  74.1 6.1 %collective-permute-start.23 = (f32[64,128]{1,0:T(8,128)S(1)}, f32[64,128]{1,0:T(8,128)S(1)}, u32[]{:S(2)}, u32[]{:S(2)}) collective-permute-start(f32[64,128]{1,0:T(8,128)S(1)} %get-tuple-element.156.dir_cell.refs_0_.refs_24_), channel_id=1, source_target_pairs={{0,8},{8,16},{16,24},{24,32},{32,40},{40,48},{48,56},{56,64},{64,7... | collective-permute-start | bytes 98312 | tf_op jit(solution)/shard_map/ppermute | solution.py:615
  80.3 4.8 %collective-permute-start.30 = (f32[64,128]{1,0:T(8,128)S(1)}, f32[64,128]{1,0:T(8,128)S(1)}, u32[]{:S(2)}, u32[]{:S(2)}) collective-permute-start(f32[64,128]{1,0:T(8,128)S(1)} %get-tuple-element.161.dir_cell.refs_0_.refs_25_), channel_id=1, source_target_pairs={{0,7},{1,0},{2,1},{3,2},{4,3},{5,4},{6,5},{7,6},{8,15},{9,8},{10,9... | collective-permute-start | bytes 98312 | tf_op jit(solution)/shard_map/ppermute | solution.py:615
  83.3 2.8 %collective-permute-start.28 = (f32[64,128]{1,0:T(8,128)S(1)}, f32[64,128]{1,0:T(8,128)S(1)}, u32[]{:S(2)}, u32[]{:S(2)}) collective-permute-start(f32[64,128]{1,0:T(8,128)S(1)} %get-tuple-element.161.dir_cell.refs_0_.refs_25_), channel_id=1, source_target_pairs={{0,248},{8,0},{16,8},{24,16},{32,24},{40,32},{48,40},{56,48},{64,5... | collective-permute-start | bytes 98312 | tf_op jit(solution)/shard_map/ppermute | solution.py:615
  83.3 6.1 %collective-permute-start.27 = (f32[64,128]{1,0:T(8,128)S(1)}, f32[64,128]{1,0:T(8,128)S(1)}, u32[]{:S(2)}, u32[]{:S(2)}) collective-permute-start(f32[64,128]{1,0:T(8,128)S(1)} %get-tuple-element.161.dir_cell.refs_0_.refs_25_), channel_id=1, source_target_pairs={{0,8},{8,16},{16,24},{24,32},{32,40},{40,48},{48,56},{56,64},{64,7... | collective-permute-start | bytes 98312 | tf_op jit(solution)/shard_map/ppermute | solution.py:615
  111.9 3.6 %collective-permute-start.34 = (f32[64,128]{1,0:T(8,128)S(1)}, f32[64,128]{1,0:T(8,128)S(1)}, u32[]{:S(2)}, u32[]{:S(2)}) collective-permute-start(f32[64,128]{1,0:T(8,128)S(1)} %get-tuple-element.173.dir_cell.refs_0_.refs_3_), channel_id=1, source_target_pairs={{0,7},{1,0},{2,1},{3,2},{4,3},{5,4},{6,5},{7,6},{8,15},{9,8},{10,9... | collective-permute-start | bytes 98312 | tf_op jit(solution)/shard_map/ppermute | solution.py:615
  112.9 2.6 %collective-permute-start.33 = (f32[64,128]{1,0:T(8,128)S(1)}, f32[64,128]{1,0:T(8,128)S(1)}, u32[]{:S(2)}, u32[]{:S(2)}) collective-permute-start(f32[64,128]{1,0:T(8,128)S(1)} %get-tuple-element.173.dir_cell.refs_0_.refs_3_), channel_id=1, source_target_pairs={{0,1},{1,2},{2,3},{3,4},{4,5},{5,6},{6,7},{7,0},{8,9},{9,10},{10,1... | collective-permute-start | bytes 98312 | tf_op jit(solution)/shard_map/ppermute | solution.py:615
  113.7 2.8 %collective-permute-start.32 = (f32[64,128]{1,0:T(8,128)S(1)}, f32[64,128]{1,0:T(8,128)S(1)}, u32[]{:S(2)}, u32[]{:S(2)}) collective-permute-start(f32[64,128]{1,0:T(8,128)S(1)} %get-tuple-element.173.dir_cell.refs_0_.refs_3_), channel_id=1, source_target_pairs={{0,248},{8,0},{16,8},{24,16},{32,24},{40,32},{48,40},{56,48},{64,5... | collective-permute-start | bytes 98312 | tf_op jit(solution)/shard_map/ppermute | solution.py:615
  115.0 6.1 %collective-permute-start.31 = (f32[64,128]{1,0:T(8,128)S(1)}, f32[64,128]{1,0:T(8,128)S(1)}, u32[]{:S(2)}, u32[]{:S(2)}) collective-permute-start(f32[64,128]{1,0:T(8,128)S(1)} %get-tuple-element.173.dir_cell.refs_0_.refs_3_), channel_id=1, source_target_pairs={{0,8},{8,16},{16,24},{24,32},{32,40},{40,48},{48,56},{56,64},{64,7... | collective-permute-start | bytes 98312 | tf_op jit(solution)/shard_map/ppermute | solution.py:615
  121.2 3.6 %collective-permute-start.38 = (f32[64,128]{1,0:T(8,128)S(1)}, f32[64,128]{1,0:T(8,128)S(1)}, u32[]{:S(2)}, u32[]{:S(2)}) collective-permute-start(f32[64,128]{1,0:T(8,128)S(1)} %get-tuple-element.186.dir_cell.refs_0_.refs_4_), channel_id=1, source_target_pairs={{0,7},{1,0},{2,1},{3,2},{4,3},{5,4},{6,5},{7,6},{8,15},{9,8},{10,9... | collective-permute-start | bytes 98312 | tf_op jit(solution)/shard_map/ppermute | solution.py:615
  122.3 2.5 %collective-permute-start.37 = (f32[64,128]{1,0:T(8,128)S(1)}, f32[64,128]{1,0:T(8,128)S(1)}, u32[]{:S(2)}, u32[]{:S(2)}) collective-permute-start(f32[64,128]{1,0:T(8,128)S(1)} %get-tuple-element.186.dir_cell.refs_0_.refs_4_), channel_id=1, source_target_pairs={{0,1},{1,2},{2,3},{3,4},{4,5},{5,6},{6,7},{7,0},{8,9},{9,10},{10,1... | collective-permute-start | bytes 98312 | tf_op jit(solution)/shard_map/ppermute | solution.py:615
  122.9 2.8 %collective-permute-start.36 = (f32[64,128]{1,0:T(8,128)S(1)}, f32[64,128]{1,0:T(8,128)S(1)}, u32[]{:S(2)}, u32[]{:S(2)}) collective-permute-start(f32[64,128]{1,0:T(8,128)S(1)} %get-tuple-element.186.dir_cell.refs_0_.refs_4_), channel_id=1, source_target_pairs={{0,248},{8,0},{16,8},{24,16},{32,24},{40,32},{48,40},{56,48},{64,5... | collective-permute-start | bytes 98312 | tf_op jit(solution)/shard_map/ppermute | solution.py:615
  123.4 6.1 %collective-permute-start.35 = (f32[64,128]{1,0:T(8,128)S(1)}, f32[64,128]{1,0:T(8,128)S(1)}, u32[]{:S(2)}, u32[]{:S(2)}) collective-permute-start(f32[64,128]{1,0:T(8,128)S(1)} %get-tuple-element.186.dir_cell.refs_0_.refs_4_), channel_id=1, source_target_pairs={{0,8},{8,16},{16,24},{24,32},{32,40},{40,48},{48,56},{56,64},{64,7... | collective-permute-start | bytes 98312 | tf_op jit(solution)/shard_map/ppermute | solution.py:615
  129.6 3.6 %collective-permute-start.42 = (f32[64,128]{1,0:T(8,128)S(1)}, f32[64,128]{1,0:T(8,128)S(1)}, u32[]{:S(2)}, u32[]{:S(2)}) collective-permute-start(f32[64,128]{1,0:T(8,128)S(1)} %get-tuple-element.191.dir_cell.refs_0_.refs_5_), channel_id=1, source_target_pairs={{0,7},{1,0},{2,1},{3,2},{4,3},{5,4},{6,5},{7,6},{8,15},{9,8},{10,9... | collective-permute-start | bytes 98312 | tf_op jit(solution)/shard_map/ppermute | solution.py:615
  131.0 2.2 %collective-permute-start.41 = (f32[64,128]{1,0:T(8,128)S(1)}, f32[64,128]{1,0:T(8,128)S(1)}, u32[]{:S(2)}, u32[]{:S(2)}) collective-permute-start(f32[64,128]{1,0:T(8,128)S(1)} %get-tuple-element.191.dir_cell.refs_0_.refs_5_), channel_id=1, source_target_pairs={{0,1},{1,2},{2,3},{3,4},{4,5},{5,6},{6,7},{7,0},{8,9},{9,10},{10,1... | collective-permute-start | bytes 98312 | tf_op jit(solution)/shard_map/ppermute | solution.py:615
  131.4 2.8 %collective-permute-start.40 = (f32[64,128]{1,0:T(8,128)S(1)}, f32[64,128]{1,0:T(8,128)S(1)}, u32[]{:S(2)}, u32[]{:S(2)}) collective-permute-start(f32[64,128]{1,0:T(8,128)S(1)} %get-tuple-element.191.dir_cell.refs_0_.refs_5_), channel_id=1, source_target_pairs={{0,248},{8,0},{16,8},{24,16},{32,24},{40,32},{48,40},{56,48},{64,5... | collective-permute-start | bytes 98312 | tf_op jit(solution)/shard_map/ppermute | solution.py:615
  131.4 6.1 %collective-permute-start.39 = (f32[64,128]{1,0:T(8,128)S(1)}, f32[64,128]{1,0:T(8,128)S(1)}, u32[]{:S(2)}, u32[]{:S(2)}) collective-permute-start(f32[64,128]{1,0:T(8,128)S(1)} %get-tuple-element.191.dir_cell.refs_0_.refs_5_), channel_id=1, source_target_pairs={{0,8},{8,16},{16,24},{24,32},{32,40},{40,48},{48,56},{56,64},{64,7... | collective-permute-start | bytes 98312 | tf_op jit(solution)/shard_map/ppermute | solution.py:615
  137.6 4.5 %collective-permute-start.46 = (f32[64,128]{1,0:T(8,128)S(1)}, f32[64,128]{1,0:T(8,128)S(1)}, u32[]{:S(2)}, u32[]{:S(2)}) collective-permute-start(f32[64,128]{1,0:T(8,128)S(1)} %get-tuple-element.196.dir_cell.refs_0_.refs_6_), channel_id=1, source_target_pairs={{0,7},{1,0},{2,1},{3,2},{4,3},{5,4},{6,5},{7,6},{8,15},{9,8},{10,9... | collective-permute-start | bytes 98312 | tf_op jit(solution)/shard_map/ppermute | solution.py:615
  140.2 2.8 %collective-permute-start.44 = (f32[64,128]{1,0:T(8,128)S(1)}, f32[64,128]{1,0:T(8,128)S(1)}, u32[]{:S(2)}, u32[]{:S(2)}) collective-permute-start(f32[64,128]{1,0:T(8,128)S(1)} %get-tuple-element.196.dir_cell.refs_0_.refs_6_), channel_id=1, source_target_pairs={{0,248},{8,0},{16,8},{24,16},{32,24},{40,32},{48,40},{56,48},{64,5... | collective-permute-start | bytes 98312 | tf_op jit(solution)/shard_map/ppermute | solution.py:615
  140.2 6.1 %collective-permute-start.43 = (f32[64,128]{1,0:T(8,128)S(1)}, f32[64,128]{1,0:T(8,128)S(1)}, u32[]{:S(2)}, u32[]{:S(2)}) collective-permute-start(f32[64,128]{1,0:T(8,128)S(1)} %get-tuple-element.196.dir_cell.refs_0_.refs_6_), channel_id=1, source_target_pairs={{0,8},{8,16},{16,24},{24,32},{32,40},{40,48},{48,56},{56,64},{64,7... | collective-permute-start | bytes 98312 | tf_op jit(solution)/shard_map/ppermute | solution.py:615
  147.9 14.8 %all-to-all-start.2 = ((f32[8,96,128]{2,1,0:T(8,128)}), f32[8,96,128]{2,1,0:T(8,128)S(1)}, u32[]{:S(2)}, u32[]{:S(2)}) async-start(f32[8,96,128]{2,1,0:T(8,128)} %address.1), calls=%async_computation.2 | async-start | bytes 786432 | tf_op jit(solution)/shard_map/all_to_all | solution.py:838
  154.6 7.4 %collective-permute-start.50 = (f32[64,128]{1,0:T(8,128)S(1)}, f32[64,128]{1,0:T(8,128)S(1)}, u32[]{:S(2)}, u32[]{:S(2)}) collective-permute-start(f32[64,128]{1,0:T(8,128)S(1)} %get-tuple-element.201.dir_cell.refs_0_.refs_7_), channel_id=1, source_target_pairs={{0,7},{1,0},{2,1},{3,2},{4,3},{5,4},{6,5},{7,6},{8,15},{9,8},{10,9... | collective-permute-start | bytes 98312 | tf_op jit(solution)/shard_map/ppermute | solution.py:615
  154.7 7.3 %collective-permute-start.49 = (f32[64,128]{1,0:T(8,128)S(1)}, f32[64,128]{1,0:T(8,128)S(1)}, u32[]{:S(2)}, u32[]{:S(2)}) collective-permute-start(f32[64,128]{1,0:T(8,128)S(1)} %get-tuple-element.201.dir_cell.refs_0_.refs_7_), channel_id=1, source_target_pairs={{0,1},{1,2},{2,3},{3,4},{4,5},{5,6},{6,7},{7,0},{8,9},{9,10},{10,1... | collective-permute-start | bytes 98312 | tf_op jit(solution)/shard_map/ppermute | solution.py:615
  156.3 5.7 %collective-permute-start.48 = (f32[64,128]{1,0:T(8,128)S(1)}, f32[64,128]{1,0:T(8,128)S(1)}, u32[]{:S(2)}, u32[]{:S(2)}) collective-permute-start(f32[64,128]{1,0:T(8,128)S(1)} %get-tuple-element.201.dir_cell.refs_0_.refs_7_), channel_id=1, source_target_pairs={{0,248},{8,0},{16,8},{24,16},{32,24},{40,32},{48,40},{56,48},{64,5... | collective-permute-start | bytes 98312 | tf_op jit(solution)/shard_map/ppermute | solution.py:615
  156.4 6.1 %collective-permute-start.47 = (f32[64,128]{1,0:T(8,128)S(1)}, f32[64,128]{1,0:T(8,128)S(1)}, u32[]{:S(2)}, u32[]{:S(2)}) collective-permute-start(f32[64,128]{1,0:T(8,128)S(1)} %get-tuple-element.201.dir_cell.refs_0_.refs_7_), channel_id=1, source_target_pairs={{0,8},{8,16},{16,24},{24,32},{32,40},{40,48},{48,56},{56,64},{64,7... | collective-permute-start | bytes 98312 | tf_op jit(solution)/shard_map/ppermute | solution.py:615
  (11 other events, 94.4 us)
